TPU v7x, 32 devices: a whole 2x2x4 slice. The times are simulated.
32 devices in a mesh: dp: 8 (over z, y), mp: 4 (over x, core).
Axes of the slice: x: 2, y: 2, z: 4, core: 2. Of those that a mesh axis runs over, the one named last changes fastest.
Arguments:
- images: bfloat16 [4, 24, 16, 16, 1024], P(None, 'dp'), may hold values from -6 to 6
- image_size: int32 [4, 24, 2], P(None, 'dp'), may hold values from 8 to 16, as said below
- entry_weight: bfloat16 [1024, 512], P('dp', 'mp'), may hold values from -0.1875 to 0.1875
- entry_gain: float32 [512], P('mp'), may hold values from 0.25 to 1.75
- entry_shift: float32 [512], P('mp'), may hold values from -3 to 3
- stride_weight: bfloat16 [3, 3, 512, 512], P(None, None, 'dp', 'mp'), may hold values from -0.09375 to 0.09375
- stride_gain: float32 [512], P('mp'), may hold values from 0.25 to 1.75
- stride_shift: float32 [512], P('mp'), may hold values from -3 to 3
- expand_weight: bfloat16 [512, 2048], P('mp', 'dp'), may hold values from -0.25 to 0.25
- expand_gain: float32 [2048], P('mp'), may hold values from 0.25 to 1.75
- expand_shift: float32 [2048], P('mp'), may hold values from -3 to 3
- project_weight: bfloat16 [1024, 2048], P('dp', 'mp'), may hold values from -0.1875 to 0.1875
- project_gain: float32 [2048], P('mp'), may hold values from 0.25 to 1.75
- project_shift: float32 [2048], P('mp'), may hold values from -3 to 3
- squeeze_weight: bfloat16 [2048, 128], P('mp', 'dp'), may hold values from -0.5 to 0.5
- squeeze_bias: float32 [128], replicated, may hold values from -3 to 3
- excite_weight: bfloat16 [128, 2048], P('dp', 'mp'), may hold values from -0.5 to 0.5
- excite_bias: float32 [2048], P('mp'), may hold values from -3 to 3
- reduce_weight: bfloat16 [2048, 512], P('dp', 'mp'), may hold values from -0.125 to 0.125
- reduce_gain: float32 [512], P('mp'), may hold values from 0.25 to 1.75
- reduce_shift: float32 [512], P('mp'), may hold values from -3 to 3
- spatial_weight: bfloat16 [3, 3, 512, 512], P(None, None, 'dp', 'mp'), may hold values from -0.09375 to 0.09375
- spatial_gain: float32 [512], P('mp'), may hold values from 0.25 to 1.75
- spatial_shift: float32 [512], P('mp'), may hold values from -3 to 3
- widen_weight: bfloat16 [512, 2048], P('mp', 'dp'), may hold values from -0.25 to 0.25
- widen_gain: float32 [2048], P('mp'), may hold values from 0.25 to 1.75
- widen_shift: float32 [2048], P('mp'), may hold values from -3 to 3
- shrink_weight: bfloat16 [2048, 128], P('mp', 'dp'), may hold values from -0.5 to 0.5
- shrink_bias: float32 [128], replicated, may hold values from -3 to 3
- gating_weight: bfloat16 [128, 2048], P('dp', 'mp'), may hold values from -0.5 to 0.5
- gating_bias: float32 [2048], P('mp'), may hold values from -3 to 3
- cotangent: bfloat16 [4, 24, 8, 8, 2048], P(None, 'dp', None, None, 'mp'), may hold values from -6 to 6
Outputs:
- result: bfloat16 [4, 24, 8, 8, 2048], P(None, 'dp', None, None, 'mp')
- images_grad: float32 [4, 24, 16, 16, 1024], P(None, 'dp', None, None, 'mp')
- entry_weight_grad: float32 [1024, 512], P('dp', 'mp')
- entry_gain_grad: float32 [512], P('mp')
- entry_shift_grad: float32 [512], P('mp')
- stride_weight_grad: float32 [3, 3, 512, 512], P(None, None, 'dp', 'mp')
- stride_gain_grad: float32 [512], P('mp')
- stride_shift_grad: float32 [512], P('mp')
- expand_weight_grad: float32 [512, 2048], P('mp', 'dp')
- expand_gain_grad: float32 [2048], P('mp')
- expand_shift_grad: float32 [2048], P('mp')
- project_weight_grad: float32 [1024, 2048], P('dp', 'mp')
- project_gain_grad: float32 [2048], P('mp')
- project_shift_grad: float32 [2048], P('mp')
- squeeze_weight_grad: float32 [2048, 128], P('mp', 'dp')
- squeeze_bias_grad: float32 [128], replicated
- excite_weight_grad: float32 [128, 2048], P('dp', 'mp')
- excite_bias_grad: float32 [2048], P('mp')
- reduce_weight_grad: float32 [2048, 512], P('dp', 'mp')
- reduce_gain_grad: float32 [512], P('mp')
- reduce_shift_grad: float32 [512], P('mp')
- spatial_weight_grad: float32 [3, 3, 512, 512], P(None, None, 'dp', 'mp')
- spatial_gain_grad: float32 [512], P('mp')
- spatial_shift_grad: float32 [512], P('mp')
- widen_weight_grad: float32 [512, 2048], P('mp', 'dp')
- widen_gain_grad: float32 [2048], P('mp')
- widen_shift_grad: float32 [2048], P('mp')
- shrink_weight_grad: float32 [2048, 128], P('mp', 'dp')
- shrink_bias_grad: float32 [128], replicated
- gating_weight_grad: float32 [128, 2048], P('dp', 'mp')
- gating_bias_grad: float32 [2048], P('mp')
Inputs may be any that keep to these rules, and one draw needn't show every extreme that they name: `image_size`: each image's content fills its top left corner of height by width pixels; the rest is padding. In every micro-batch one image is 16 by 16 and another is 8 by 8.
All inputs are finite; a program needn't handle non-finite values.
Results may differ from a plain program's by a relative error of at most 0.025.
Values may be sent and summed in bfloat16 or wider, within the bound.
A program may use at most 192 MiB of HBM per device.

v0:
```python
import jax
import jax.numpy as jnp
from jax import lax
from jax.sharding import PartitionSpec as P

eps_norm = 1e-05
highest = lax.Precision.HIGHEST


def matmul(left, right):
    return jnp.dot(left, right, preferred_element_type=jnp.float32)


def contract_rows(left, right):
    return lax.dot_general(
        left, right, (((0,), (0,)), ((), ())), preferred_element_type=jnp.float32
    )


def contract_cols(left, right):
    return lax.dot_general(
        left, right, (((1,), (1,)), ((), ())), preferred_element_type=jnp.float32
    )


def swish_slope(value):
    sigma = jax.nn.sigmoid(value)
    return sigma * (1.0 + value * (1.0 - sigma))


def pixel_masks(sizes, side):
    half = side // 2
    height = sizes[:, 0]
    breadth = sizes[:, 1]
    places = jnp.arange(side, dtype=jnp.int32)
    inside = (
        (places[None, :, None] < height[:, None, None])
        & (places[None, None, :] < breadth[:, None, None])
    ).astype(jnp.float32)
    halves = jnp.arange(half, dtype=jnp.int32)
    reduced = (
        (halves[None, :, None] < ((height + 1) // 2)[:, None, None])
        & (halves[None, None, :] < ((breadth + 1) // 2)[:, None, None])
    ).astype(jnp.float32)
    return (inside, reduced)


def spatial_taps(field, stride):
    count, side, channels = (field.shape[0], field.shape[1], field.shape[3])
    reach = stride * (side // stride - 1) + 1
    padded = jnp.pad(field, ((0, 0), (1, 1), (1, 1), (0, 0)))
    pieces = []
    for row in range(3):
        for column in range(3):
            pieces.append(
                lax.slice(
                    padded,
                    (0, row, column, 0),
                    (count, row + reach, column + reach, channels),
                    (1, stride, stride, 1),
                )
            )
    return jnp.concatenate(pieces, axis=3)


def untap(grads, stride, side):
    count, out_side = (grads.shape[0], grads.shape[1])
    channels = grads.shape[3] // 9
    reach = stride * (out_side - 1) + 1
    total = jnp.zeros((count, side + 2, side + 2, channels), jnp.float32)
    for row in range(3):
        for column in range(3):
            first = (row * 3 + column) * channels
            piece = grads[:, :, :, first : first + channels]
            total = total + lax.pad(
                piece,
                jnp.float32(0.0),
                (
                    (0, 0, 0),
                    (row, side + 2 - row - reach, stride - 1),
                    (column, side + 2 - column - reach, stride - 1),
                    (0, 0, 0),
                ),
            )
    return total[:, 1 : side + 1, 1 : side + 1, :]


def batch_statistics(fields, mask):
    weights = mask[..., None]
    terms = []
    for field in fields:
        terms.append(jnp.sum(field * weights, axis=(0, 1, 2)))
        terms.append(jnp.sum(field * field * weights, axis=(0, 1, 2)))
    packed, total_vector = lax.psum((jnp.concatenate(terms), jnp.sum(mask).reshape(1)), "dp")
    total = total_vector[0]
    result = []
    offset = 0
    for field in fields:
        breadth = field.shape[3]
        mean = packed[offset : offset + breadth] / total
        second = packed[offset + breadth : offset + 2 * breadth] / total
        result.append((mean, lax.rsqrt(second - mean * mean + eps_norm)))
        offset = offset + 2 * breadth
    return (result, total)


def standardize(raw, statistics, gain, shift):
    mean, scale = statistics
    normed = (raw - mean) * scale
    return (normed, normed * gain + shift)


def batch_backward(grads, normeds, scales, gains, mask, total, extras):
    terms = []
    for grad, normed in zip(grads, normeds):
        terms.append(jnp.sum(grad * normed, axis=(0, 1, 2)))
        terms.append(jnp.sum(grad, axis=(0, 1, 2)))
    for extra in extras:
        terms.append(extra)
    packed = lax.psum(jnp.concatenate(terms), "dp")
    results = []
    pairs = []
    offset = 0
    for grad, normed, scale, gain in zip(grads, normeds, scales, gains):
        breadth = grad.shape[3]
        gain_grad = packed[offset : offset + breadth]
        shift_grad = packed[offset + breadth : offset + 2 * breadth]
        offset = offset + 2 * breadth
        results.append(
            scale * gain * (grad - mask[..., None] * (shift_grad + normed * gain_grad) / total)
        )
        pairs.append((gain_grad, shift_grad))
    rest = []
    for extra in extras:
        rest.append(packed[offset : offset + extra.shape[0]])
        offset = offset + extra.shape[0]
    return (results, pairs, rest)


def channel_sum(value):
    return lax.psum(value, "mp")


def expand_sum(value):
    return lax.psum_scatter(
        value.astype(jnp.bfloat16), "mp", scatter_dimension=3, tiled=True
    ).astype(jnp.float32)


def expand_spread(value):
    return lax.all_gather(value, "mp", axis=3, tiled=True)


def excite_forward(field, mask, pixels, squeeze_full, squeeze_bias, excite_full, excite_bias):
    pooled = jnp.sum(field * mask[..., None], axis=(1, 2)) / pixels[:, None]
    inner_pre = (
        channel_sum(jnp.dot(pooled, squeeze_full.astype(jnp.float32), precision=highest))
        + squeeze_bias
    )
    hidden = jax.nn.silu(inner_pre)
    scale = jax.nn.sigmoid(
        jnp.dot(hidden, excite_full.astype(jnp.float32), precision=highest) + excite_bias
    )
    return (pooled, inner_pre, hidden, scale)


def excite_backward(grad_branch, field, mask, pixels, saved, squeeze_full, excite_full):
    pooled, inner_pre, hidden, scale = saved
    grad_scale = jnp.sum(grad_branch * field, axis=(1, 2))
    grad_gate = grad_scale * scale * (1.0 - scale)
    excite_grad = jnp.dot(hidden.T, grad_gate, precision=highest)
    grad_hidden = channel_sum(
        jnp.dot(grad_gate, excite_full.astype(jnp.float32).T, precision=highest)
    )
    grad_inner = grad_hidden * swish_slope(inner_pre)
    squeeze_grad = jnp.dot(pooled.T, grad_inner, precision=highest)
    grad_pooled = jnp.dot(grad_inner, squeeze_full.astype(jnp.float32).T, precision=highest)
    grad_field = (
        grad_branch * scale[:, None, None, :]
        + grad_pooled[:, None, None, :] * mask[..., None] / pixels[:, None, None, None]
    )
    return (
        grad_field,
        squeeze_grad,
        excite_grad,
        jnp.sum(grad_inner, axis=0),
        jnp.sum(grad_gate, axis=0),
    )


def shards(
    images,
    image_size,
    entry_weight,
    entry_gain,
    entry_shift,
    stride_weight,
    stride_gain,
    stride_shift,
    expand_weight,
    expand_gain,
    expand_shift,
    project_weight,
    project_gain,
    project_shift,
    squeeze_weight,
    squeeze_bias,
    excite_weight,
    excite_bias,
    reduce_weight,
    reduce_gain,
    reduce_shift,
    spatial_weight,
    spatial_gain,
    spatial_shift,
    widen_weight,
    widen_gain,
    widen_shift,
    shrink_weight,
    shrink_bias,
    gating_weight,
    gating_bias,
    cotangent,
):
    micro_count, count, side = (images.shape[0], images.shape[1], images.shape[2])
    half = side // 2
    channels_in = images.shape[4]
    full_sums = None
    shard_sums = None
    gain_sums = None
    shift_sums = None
    bias_sums = None
    outputs = []
    picture_grads = []
    for micro in range(micro_count):
        gathered = (
            lax.all_gather(entry_weight, "dp", axis=0, tiled=True),
            lax.all_gather(stride_weight, "dp", axis=2, tiled=True),
            lax.all_gather(expand_weight, "dp", axis=1, tiled=True),
            lax.all_gather(project_weight, "dp", axis=0, tiled=True),
            lax.all_gather(squeeze_weight, "dp", axis=1, tiled=True),
            lax.all_gather(excite_weight, "dp", axis=0, tiled=True),
            lax.all_gather(reduce_weight, "dp", axis=0, tiled=True),
            lax.all_gather(spatial_weight, "dp", axis=2, tiled=True),
            lax.all_gather(widen_weight, "dp", axis=1, tiled=True),
            lax.all_gather(shrink_weight, "dp", axis=1, tiled=True),
            lax.all_gather(gating_weight, "dp", axis=0, tiled=True),
        )
        (
            entry_full,
            stride_full,
            expand_full,
            project_full,
            squeeze_full,
            excite_full,
            reduce_full,
            spatial_full,
            widen_full,
            shrink_full,
            gating_full,
        ) = gathered
        picture = images[micro]
        inside, reduced = pixel_masks(image_size[micro], side)
        pixels = jnp.sum(reduced, axis=(1, 2))
        reduced_mask = reduced[..., None]
        entry_raw = matmul(picture.reshape(-1, channels_in), entry_full).reshape(
            count, side, side, -1
        )
        stats, inside_total = batch_statistics([entry_raw], inside)
        entry_stats = stats[0]
        entry_normed, entry_pre = standardize(entry_raw, entry_stats, entry_gain, entry_shift)
        entry_act = (jax.nn.silu(entry_pre) * inside[..., None]).astype(jnp.bfloat16)
        entry_wide = lax.all_gather(entry_act, "mp", axis=3, tiled=True)
        bottleneck = entry_wide.shape[3]
        stride_taps = spatial_taps(entry_wide, 2).reshape(-1, 9 * bottleneck)
        stride_raw = matmul(stride_taps, stride_full.reshape(9 * bottleneck, -1)).reshape(
            count, half, half, -1
        )
        stats, reduced_total = batch_statistics([stride_raw], reduced)
        stride_stats = stats[0]
        stride_normed, stride_pre = standardize(stride_raw, stride_stats, stride_gain, stride_shift)
        stride_act = (jax.nn.silu(stride_pre) * reduced_mask).astype(jnp.bfloat16)
        local_bottleneck = stride_act.shape[3]
        stride_flat = stride_act.reshape(-1, local_bottleneck)
        expand_raw = expand_sum(matmul(stride_flat, expand_full).reshape(count, half, half, -1))
        strided_flat = picture[:, ::2, ::2, :].reshape(-1, channels_in)
        project_raw = matmul(strided_flat, project_full).reshape(count, half, half, -1)
        stats, reduced_total = batch_statistics([expand_raw, project_raw], reduced)
        expand_stats, project_stats = (stats[0], stats[1])
        expand_normed, expand_pre = standardize(expand_raw, expand_stats, expand_gain, expand_shift)
        project_normed, project_pre = standardize(
            project_raw, project_stats, project_gain, project_shift
        )
        first_saved = excite_forward(
            expand_pre, reduced, pixels, squeeze_full, squeeze_bias, excite_full, excite_bias
        )
        first_sum = expand_pre * first_saved[3][:, None, None, :] + project_pre
        first_out = (jax.nn.silu(first_sum) * reduced_mask).astype(jnp.bfloat16)
        block_wide = lax.all_gather(first_out, "mp", axis=3, tiled=True)
        block_flat = block_wide.reshape(-1, block_wide.shape[3])
        reduce_raw = matmul(block_flat, reduce_full).reshape(count, half, half, -1)
        stats, reduced_total = batch_statistics([reduce_raw], reduced)
        reduce_stats = stats[0]
        reduce_normed, reduce_pre = standardize(reduce_raw, reduce_stats, reduce_gain, reduce_shift)
        reduce_act = (jax.nn.silu(reduce_pre) * reduced_mask).astype(jnp.bfloat16)
        reduce_wide = lax.all_gather(reduce_act, "mp", axis=3, tiled=True)
        second_taps = spatial_taps(reduce_wide, 1).reshape(-1, 9 * bottleneck)
        spatial_raw = matmul(second_taps, spatial_full.reshape(9 * bottleneck, -1)).reshape(
            count, half, half, -1
        )
        stats, reduced_total = batch_statistics([spatial_raw], reduced)
        spatial_stats = stats[0]
        spatial_normed, spatial_pre = standardize(
            spatial_raw, spatial_stats, spatial_gain, spatial_shift
        )
        spatial_act = (jax.nn.silu(spatial_pre) * reduced_mask).astype(jnp.bfloat16)
        spatial_flat = spatial_act.reshape(-1, local_bottleneck)
        widen_raw = expand_sum(matmul(spatial_flat, widen_full).reshape(count, half, half, -1))
        stats, reduced_total = batch_statistics([widen_raw], reduced)
        widen_stats = stats[0]
        widen_normed, widen_pre = standardize(widen_raw, widen_stats, widen_gain, widen_shift)
        second_saved = excite_forward(
            widen_pre, reduced, pixels, shrink_full, shrink_bias, gating_full, gating_bias
        )
        second_sum = widen_pre * second_saved[3][:, None, None, :] + first_out.astype(jnp.float32)
        outputs.append((jax.nn.silu(second_sum) * reduced_mask).astype(jnp.bfloat16))
        second_grad = cotangent[micro].astype(jnp.float32) * reduced_mask * swish_slope(second_sum)
        widen_grad, shrink_grad, gating_grad, shrink_bias_grad, gating_bias_grad = excite_backward(
            second_grad, widen_pre, reduced, pixels, second_saved, shrink_full, gating_full
        )
        grads, widen_pair, extras = batch_backward(
            [widen_grad],
            [widen_normed],
            [widen_stats[1]],
            [widen_gain],
            reduced,
            reduced_total,
            (shrink_bias_grad, gating_bias_grad),
        )
        widen_pair = widen_pair[0]
        shrink_bias_total, gating_bias_total = (extras[0], extras[1])
        widen_local = grads[0].astype(jnp.bfloat16)
        widen_low = expand_spread(widen_local)
        widen_flat = widen_low.reshape(-1, widen_low.shape[3])
        widen_weight_grad = contract_rows(spatial_flat, widen_flat)
        spatial_act_grad = contract_cols(widen_flat, widen_full).reshape(count, half, half, -1)
        spatial_grad = spatial_act_grad * reduced_mask * swish_slope(spatial_pre)
        grads, spatial_pair, extras = batch_backward(
            [spatial_grad],
            [spatial_normed],
            [spatial_stats[1]],
            [spatial_gain],
            reduced,
            reduced_total,
            (),
        )
        spatial_pair = spatial_pair[0]
        spatial_low = grads[0].astype(jnp.bfloat16).reshape(-1, local_bottleneck)
        spatial_weight_grad = contract_rows(second_taps, spatial_low).reshape(
            3, 3, bottleneck, local_bottleneck
        )
        second_tap_grad = contract_cols(spatial_low, spatial_full.reshape(9 * bottleneck, -1))
        reduce_act_grad = lax.psum_scatter(
            untap(second_tap_grad.reshape(count, half, half, -1), 1, half).astype(jnp.bfloat16),
            "mp",
            scatter_dimension=3,
            tiled=True,
        ).astype(jnp.float32)
        reduce_grad = reduce_act_grad * reduced_mask * swish_slope(reduce_pre)
        grads, reduce_pair, extras = batch_backward(
            [reduce_grad],
            [reduce_normed],
            [reduce_stats[1]],
            [reduce_gain],
            reduced,
            reduced_total,
            (),
        )
        reduce_pair = reduce_pair[0]
        reduce_low = grads[0].astype(jnp.bfloat16).reshape(-1, local_bottleneck)
        reduce_weight_grad = contract_rows(block_flat, reduce_low)
        first_partial = contract_cols(reduce_low, reduce_full).reshape(count, half, half, -1)
        first_out_grad = (
            lax.psum_scatter(
                first_partial.astype(jnp.bfloat16), "mp", scatter_dimension=3, tiled=True
            ).astype(jnp.float32)
            + second_grad
        )
        first_grad = first_out_grad * reduced_mask * swish_slope(first_sum)
        expand_grad, squeeze_grad, excite_grad, squeeze_bias_grad, excite_bias_grad = (
            excite_backward(
                first_grad, expand_pre, reduced, pixels, first_saved, squeeze_full, excite_full
            )
        )
        grads, pairs, extras = batch_backward(
            [expand_grad, first_grad],
            [expand_normed, project_normed],
            [expand_stats[1], project_stats[1]],
            [expand_gain, project_gain],
            reduced,
            reduced_total,
            (squeeze_bias_grad, excite_bias_grad),
        )
        expand_pair, project_pair = (pairs[0], pairs[1])
        squeeze_bias_total, excite_bias_total = (extras[0], extras[1])
        expand_local = grads[0].astype(jnp.bfloat16)
        expand_low = expand_spread(expand_local)
        expand_flat = expand_low.reshape(-1, expand_low.shape[3])
        expand_weight_grad = contract_rows(stride_flat, expand_flat)
        stride_act_grad = contract_cols(expand_flat, expand_full).reshape(count, half, half, -1)
        project_low = grads[1].astype(jnp.bfloat16).reshape(-1, grads[1].shape[3])
        project_weight_grad = contract_rows(strided_flat, project_low)
        strided_grad = contract_cols(project_low, project_full).reshape(
            count, half, half, channels_in
        )
        stride_grad = stride_act_grad * reduced_mask * swish_slope(stride_pre)
        grads, stride_pair, extras = batch_backward(
            [stride_grad],
            [stride_normed],
            [stride_stats[1]],
            [stride_gain],
            reduced,
            reduced_total,
            (),
        )
        stride_pair = stride_pair[0]
        stride_low = grads[0].astype(jnp.bfloat16).reshape(-1, local_bottleneck)
        stride_weight_grad = contract_rows(stride_taps, stride_low).reshape(
            3, 3, bottleneck, local_bottleneck
        )
        first_tap_grad = contract_cols(stride_low, stride_full.reshape(9 * bottleneck, -1))
        entry_act_grad = lax.psum_scatter(
            untap(first_tap_grad.reshape(count, half, half, -1), 2, side).astype(jnp.bfloat16),
            "mp",
            scatter_dimension=3,
            tiled=True,
        ).astype(jnp.float32)
        entry_grad = entry_act_grad * inside[..., None] * swish_slope(entry_pre)
        grads, entry_pair, extras = batch_backward(
            [entry_grad], [entry_normed], [entry_stats[1]], [entry_gain], inside, inside_total, ()
        )
        entry_pair = entry_pair[0]
        entry_low = grads[0].astype(jnp.bfloat16).reshape(-1, local_bottleneck)
        entry_weight_grad = contract_rows(picture.reshape(-1, channels_in), entry_low)
        picture_partial = contract_cols(entry_low, entry_full).reshape(
            count, side, side, channels_in
        )
        picture_partial = picture_partial + lax.pad(
            strided_grad, jnp.float32(0.0), ((0, 0, 0), (0, 1, 1), (0, 1, 1), (0, 0, 0))
        )
        picture_grads.append(
            lax.psum_scatter(
                picture_partial.astype(jnp.bfloat16), "mp", scatter_dimension=3, tiled=True
            ).astype(jnp.float32)
        )
        micro_grads = [
            entry_weight_grad,
            stride_weight_grad,
            expand_weight_grad,
            project_weight_grad,
            squeeze_grad,
            excite_grad,
            reduce_weight_grad,
            spatial_weight_grad,
            widen_weight_grad,
            shrink_grad,
            gating_grad,
        ]
        full_sums = (
            micro_grads
            if full_sums is None
            else [total + part for total, part in zip(full_sums, micro_grads)]
        )
        micro_pairs = [
            entry_pair,
            stride_pair,
            expand_pair,
            project_pair,
            reduce_pair,
            spatial_pair,
            widen_pair,
        ]
        micro_gains = [pair[0] for pair in micro_pairs]
        micro_shifts = [pair[1] for pair in micro_pairs]
        micro_biases = [squeeze_bias_total, excite_bias_total, shrink_bias_total, gating_bias_total]
        gain_sums = (
            micro_gains
            if gain_sums is None
            else [total + part for total, part in zip(gain_sums, micro_gains)]
        )
        shift_sums = (
            micro_shifts
            if shift_sums is None
            else [total + part for total, part in zip(shift_sums, micro_shifts)]
        )
        bias_sums = (
            micro_biases
            if bias_sums is None
            else [total + part for total, part in zip(bias_sums, micro_biases)]
        )
    shard_sums = list(
        (
            lax.psum_scatter(full_sums[0], "dp", scatter_dimension=0, tiled=True),
            lax.psum_scatter(full_sums[1], "dp", scatter_dimension=2, tiled=True),
            lax.psum_scatter(full_sums[2], "dp", scatter_dimension=1, tiled=True),
            lax.psum_scatter(full_sums[3], "dp", scatter_dimension=0, tiled=True),
            lax.psum_scatter(full_sums[4], "dp", scatter_dimension=1, tiled=True),
            lax.psum_scatter(full_sums[5], "dp", scatter_dimension=0, tiled=True),
            lax.psum_scatter(full_sums[6], "dp", scatter_dimension=0, tiled=True),
            lax.psum_scatter(full_sums[7], "dp", scatter_dimension=2, tiled=True),
            lax.psum_scatter(full_sums[8], "dp", scatter_dimension=1, tiled=True),
            lax.psum_scatter(full_sums[9], "dp", scatter_dimension=1, tiled=True),
            lax.psum_scatter(full_sums[10], "dp", scatter_dimension=0, tiled=True),
        )
    )
    return (
        jnp.stack(outputs),
        jnp.stack(picture_grads),
        shard_sums[0],
        gain_sums[0],
        shift_sums[0],
        shard_sums[1],
        gain_sums[1],
        shift_sums[1],
        shard_sums[2],
        gain_sums[2],
        shift_sums[2],
        shard_sums[3],
        gain_sums[3],
        shift_sums[3],
        shard_sums[4],
        bias_sums[0],
        shard_sums[5],
        bias_sums[1],
        shard_sums[6],
        gain_sums[4],
        shift_sums[4],
        shard_sums[7],
        gain_sums[5],
        shift_sums[5],
        shard_sums[8],
        gain_sums[6],
        shift_sums[6],
        shard_sums[9],
        bias_sums[2],
        shard_sums[10],
        bias_sums[3],
    )


def solution(mesh):
    in_specs = (
        P(None, "dp", None, None, None),
        P(None, "dp", None),
        P("dp", "mp"),
        P("mp"),
        P("mp"),
        P(None, None, "dp", "mp"),
        P("mp"),
        P("mp"),
        P("mp", "dp"),
        P("mp"),
        P("mp"),
        P("dp", "mp"),
        P("mp"),
        P("mp"),
        P("mp", "dp"),
        P(),
        P("dp", "mp"),
        P("mp"),
        P("dp", "mp"),
        P("mp"),
        P("mp"),
        P(None, None, "dp", "mp"),
        P("mp"),
        P("mp"),
        P("mp", "dp"),
        P("mp"),
        P("mp"),
        P("mp", "dp"),
        P(),
        P("dp", "mp"),
        P("mp"),
        P(None, "dp", None, None, "mp"),
    )
    out_specs = (
        P(None, "dp", None, None, "mp"),
        P(None, "dp", None, None, "mp"),
        P("dp", "mp"),
        P("mp"),
        P("mp"),
        P(None, None, "dp", "mp"),
        P("mp"),
        P("mp"),
        P("mp", "dp"),
        P("mp"),
        P("mp"),
        P("dp", "mp"),
        P("mp"),
        P("mp"),
        P("mp", "dp"),
        P(),
        P("dp", "mp"),
        P("mp"),
        P("dp", "mp"),
        P("mp"),
        P("mp"),
        P(None, None, "dp", "mp"),
        P("mp"),
        P("mp"),
        P("mp", "dp"),
        P("mp"),
        P("mp"),
        P("mp", "dp"),
        P(),
        P("dp", "mp"),
        P("mp"),
    )
    return jax.shard_map(shards, mesh=mesh, in_specs=in_specs, out_specs=out_specs, check_vma=False)
```

profile of v0, /device:TPU:0, one launch (start us, length us, event | category | flops | bytes accessed | tf_op | source)
XLA Modules:
  0.0 3219.9 jit_solution(6439799067558908478)
XLA Ops:
  10.6 33.0 %all_gather.62 = bf16[1024,128]{1,0:T(8,128)(2,1)S(1)} all-gather(bf16[128,128]{1,0:T(8,128)(2,1)} %param.34), channel_id=1, replica_groups=mesh['dp'=8,'mp'=4] {'dp'}, dimensions={0}, use_global_device_ids=true | all-gather | bytes 294912 | tf_op jit(solution)/shard_map/all_gather | solution.py:237
  123.0 31.4 all_gather.129
  201.3 30.6 all_gather.131
  232.0 30.8 all_gather.132
  262.8 31.6 all_gather.134
  294.4 31.2 all_gather.137
  325.6 32.5 %all_gather.138 = bf16[512,128]{0,1:T(8,128)(2,1)} all-gather(bf16[512,16]{0,1:T(8,128)(2,1)S(1)} %copy-done.425), channel_id=1, replica_groups=mesh['dp'=8,'mp'=4] {'dp'}, dimensions={1}, use_global_device_ids=true | all-gather | bytes 147456 | tf_op jit(solution)/shard_map/all_gather | solution.py:246
  358.1 32.6 %all_gather.139 = bf16[128,512]{1,0:T(8,128)(2,1)} all-gather(bf16[16,512]{1,0:T(8,128)(2,1)S(1)} %copy-done.426), channel_id=1, replica_groups=mesh['dp'=8,'mp'=4] {'dp'}, dimensions={0}, use_global_device_ids=true | all-gather | bytes 147456 | tf_op jit(solution)/shard_map/all_gather | solution.py:247
  555.2 33.8 %all-reduce.95 = (f32[256]{0:T(256)S(1)}, f32[]{:T(128)}, f32[1664]{0:T(1024)S(1)}, f32[256]{0:T(256)S(1)}, f32[]{:T(128)}, /*index=5*/f32[256]{0:T(256)S(1)}, f32[]{:T(128)}) all-reduce(f32[256]{0:T(256)} %pad_maximum_fusion.25, f32[]{:T(128)} %fusion.370, f32[1664]{0:T(1024)S(1)} %pad_maximum_fusion.5, ...), channel_id=1, replica_groups=mesh['dp'=8,'mp'=4] {'dp'}, use_global_device_ids=true, to_apply=%region_95.96 | all-reduce | flops 2435 | bytes 19480 | tf_op jit(solution)/shard_map/psum | solution.py:94
  1075.2 37.8 %all-reduce.93 = (f32[2048]{0:T(1024)}, f32[256]{0:T(256)S(1)}, f32[2048]{0:T(1024)}, f32[2048]{0:T(1024)}) all-reduce(f32[2048]{0:T(1024)S(1)} %pad_maximum_fusion.4, f32[256]{0:T(256)S(1)} %pad_maximum_fusion.30, f32[2048]{0:T(1024)S(1)} %pad_maximum_fusion.2, f32[2048]{0:T(1024)S(1)} %pad_maximum_fusion.3), channel_id=1, replica_groups=mesh['dp'=8,'mp'=4] {'dp'}, use_global_device_ids=true, to_apply=%region_108.109 | all-reduce | flops 6400 | bytes 51200 | tf_op jit(solution)/shard_map/psum | solution.py:94
  1333.1 37.1 %all-reduce.90 = (f32[1024]{0:T(1024)}, f32[1024]{0:T(1024)}, f32[1024]{0:T(1024)}) all-reduce(f32[1024]{0:T(1024)} %pad_maximum_fusion.10, f32[1024]{0:T(1024)} %pad_maximum_fusion.11, f32[1024]{0:T(1024)} %pad_maximum_fusion.12), channel_id=1, replica_groups=mesh['dp'=8,'mp'=4] {'dp'}, use_global_device_ids=true, to_apply=%region_59.60 | all-reduce | flops 3072 | bytes 24576 | tf_op jit(solution)/shard_map/psum | solution.py:94
  1423.9 34.5 %all-reduce.89 = (f32[1664]{0:T(1024)}, f32[1664]{0:T(1024)}, f32[1664]{0:T(1024)}) all-reduce(f32[1664]{0:T(1024)} %pad_maximum_fusion.6, f32[1664]{0:T(1024)} %pad_maximum_fusion.7, f32[1664]{0:T(1024)} %pad_maximum_fusion.8), channel_id=1, replica_groups=mesh['dp'=8,'mp'=4] {'dp'}, use_global_device_ids=true, to_apply=%region_162.163 | all-reduce | flops 4992 | bytes 39936 | tf_op jit(solution)/shard_map/psum | solution.py:120
  1721.9 37.8 %all-reduce.86 = (f32[2688]{0:T(1024)S(1)}, f32[2688]{0:T(1024)S(1)}, f32[2688]{0:T(1024)S(1)}, f32[2688]{0:T(1024)S(1)}) all-reduce(f32[2688]{0:T(1024)S(1)} %constant_dynamic-update-slice_fusion.63, f32[2688]{0:T(1024)S(1)} %constant_dynamic-update-slice_fusion.62, ...), channel_id=1, replica_groups=mesh['dp'=8,'mp'=4] {'dp'}, use_global_device_ids=true, to_apply=%region_243.244 | all-reduce | flops 10752 | bytes 86016 | tf_op jit(solution)/shard_map/psum | solution.py:120
  2546.4 30.9 reduce-scatter.78.cloned.1.call-done
  2577.3 30.8 reduce-scatter.82.cloned.1.call-done
  2611.3 62.1 %reduce-scatter.104.cloned.1.call-done = f32[16,512]{1,0:T(8,128)} async-done(((f32[128,512]{1,0:T(8,128)}), f32[16,512]{1,0:T(8,128)}) %reduce-scatter.104.cloned.1.call-update) | async-done | bytes 32784 | tf_op jit(solution)/shard_map/reduce_scatter | solution.py:513
  2673.4 64.5 %reduce-scatter.102.cloned.1.call-done = f32[512,16]{0,1:T(8,128)} async-done(((f32[512,128]{0,1:T(8,128)}), f32[512,16]{0,1:T(8,128)}) %reduce-scatter.102.cloned.1.call-update) | async-done | bytes 32784 | tf_op jit(solution)/shard_map/reduce_scatter | solution.py:512
  2738.0 67.3 %reduce-scatter.100.cloned.1.call-done = f32[128,256]{1,0:T(8,128)} async-done(((f32[128,2048]{1,0:T(8,128)}), f32[128,256]{1,0:T(8,128)}) %reduce-scatter.100.cloned.1.call-update) | async-done | bytes 131088 | tf_op jit(solution)/shard_map/reduce_scatter | solution.py:511
  2805.3 66.3 %reduce-scatter.96.cloned.1.call-done = f32[256,128]{1,0:T(8,128)} async-done(((f32[2048,128]{1,0:T(8,128)}), f32[256,128]{1,0:T(8,128)}) %reduce-scatter.96.cloned.1.call-update) | async-done | bytes 131088 | tf_op jit(solution)/shard_map/reduce_scatter | solution.py:509
  2871.6 64.5 %reduce-scatter.94.cloned.1.call-done = f32[16,512]{1,0:T(8,128)} async-done(((f32[128,512]{1,0:T(8,128)}), f32[16,512]{1,0:T(8,128)}) %reduce-scatter.94.cloned.1.call-update) | async-done | bytes 32784 | tf_op jit(solution)/shard_map/reduce_scatter | solution.py:508
  2936.1 64.6 %reduce-scatter.92.cloned.1.call-done = f32[512,16]{0,1:T(8,128)} async-done(((f32[512,128]{0,1:T(8,128)}), f32[512,16]{0,1:T(8,128)}) %reduce-scatter.92.cloned.1.call-update) | async-done | bytes 32784 | tf_op jit(solution)/shard_map/reduce_scatter | solution.py:507
  3000.7 67.3 %reduce-scatter.88.cloned.1.call-done = f32[128,256]{1,0:T(8,128)} async-done(((f32[128,2048]{1,0:T(8,128)}), f32[128,256]{1,0:T(8,128)}) %reduce-scatter.88.cloned.1.call-update) | async-done | bytes 131088 | tf_op jit(solution)/shard_map/reduce_scatter | solution.py:505
  3067.9 72.5 %reduce-scatter.98.cloned.1.call-done = f32[3,3,64,128]{3,2,1,0:T(8,128)} async-done(((f32[3,3,512,128]{3,2,1,0:T(8,128)}), f32[3,3,64,128]{3,2,1,0:T(8,128)}) %reduce-scatter.98.cloned.1.call-update) | async-done | bytes 294928 | tf_op jit(solution)/shard_map/reduce_scatter | solution.py:510
  3140.4 72.7 %reduce-scatter.86.cloned.1.call-done = f32[3,3,64,128]{3,2,1,0:T(8,128)} async-done(((f32[3,3,512,128]{3,2,1,0:T(8,128)}), f32[3,3,64,128]{3,2,1,0:T(8,128)}) %reduce-scatter.86.cloned.1.call-update) | async-done | bytes 294928 | tf_op jit(solution)/shard_map/reduce_scatter | solution.py:504
  (1888 shorter events, 2099.3 us)
Async XLA Ops:
  7.9 392.2 %all-gather.6.cloned.1.call-start = ((), (), s32[]{:S(2)}) async-start(), calls=%async_computation.37 | async-start | bytes 1179648 | tf_op jit(solution)/shard_map/all_gather | solution.py:240
  8.7 391.4 %reduce-scatter.52.cloned.1.call-start = ((), (), s32[]{:S(2)}) async-start(), calls=%async_computation.36 | async-start | bytes 983040 | tf_op jit(solution)/shard_map/reduce_scatter | solution.py:145
  177.3 292.3 %all-gather.8.cloned.1.call-start = ((), (), s32[]{:S(2)}) async-start(), calls=%async_computation.38 | async-start | bytes 1327104 | tf_op jit(solution)/shard_map/all_gather | solution.py:244
  177.9 336.1 %reduce-scatter.54.cloned.1.call-start = ((), (), s32[]{:S(2)}) async-start(), calls=%async_computation.39 | async-start | bytes 983040 | tf_op jit(solution)/shard_map/reduce_scatter | solution.py:145
  493.8 527.1 %reduce-scatter.106.cloned.1.call-start = ((), (), s32[]{:S(2)}) async-start(), calls=%async_computation.65 | async-start | bytes 327680
  1116.0 162.6 %reduce-scatter.66.cloned.1.call-start = ((), (), s32[]{:S(2)}) async-start(), calls=%async_computation.45 | async-start | bytes 983040 | tf_op jit(solution)/shard_map/reduce_scatter | solution.py:145
  1262.0 291.5 %reduce-scatter.118.cloned.1.call-start = ((), (), s32[]{:S(2)}) async-start(), calls=%async_computation.71 | async-start | bytes 327680
  1621.6 676.7 %reduce-scatter.116.cloned.1.call-start = ((), (), s32[]{:S(2)}) async-start(), calls=%async_computation.70 | async-start | bytes 983040
  1949.6 352.0 %reduce-scatter.112.cloned.1.call-start = ((), (), s32[]{:S(2)}) async-start(), calls=%async_computation.68 | async-start | bytes 983040
  2073.1 232.4 %reduce-scatter.108.cloned.1.call-start = ((), (), s32[]{:S(2)}) async-start(), calls=%async_computation.66 | async-start | bytes 983040
  2294.3 209.3 %reduce-scatter.84.cloned.1.call-start = ((), (), s32[]{:S(2)}) async-start(), calls=%async_computation.54 | async-start | bytes 589824 | tf_op jit(solution)/shard_map/reduce_scatter | solution.py:503
  2360.9 154.9 %reduce-scatter.70.cloned.1.call-start = ((), (), s32[]{:S(2)}) async-start(), calls=%async_computation.47 | async-start | bytes 1966080 | tf_op jit(solution)/shard_map/reduce_scatter | solution.py:452
  2375.7 170.7 %reduce-scatter.74.cloned.1.call-start = ((), (), s32[]{:S(2)}) async-start(), calls=%async_computation.49 | async-start | bytes 1966080 | tf_op jit(solution)/shard_map/reduce_scatter | solution.py:452
  2389.2 188.1 %reduce-scatter.78.cloned.1.call-start = ((), (), s32[]{:S(2)}) async-start(), calls=%async_computation.51 | async-start | bytes 1966080 | tf_op jit(solution)/shard_map/reduce_scatter | solution.py:452
  2402.8 205.3 %reduce-scatter.82.cloned.1.call-start = ((), (), s32[]{:S(2)}) async-start(), calls=%async_computation.53 | async-start | bytes 1966080 | tf_op jit(solution)/shard_map/reduce_scatter | solution.py:452
  2416.5 256.9 %reduce-scatter.104.cloned.1.call-start = ((), (), s32[]{:S(2)}) async-start(), calls=%async_computation.64 | async-start | bytes 294912 | tf_op jit(solution)/shard_map/reduce_scatter | solution.py:513
  2420.2 317.8 %reduce-scatter.102.cloned.1.call-start = ((), (), s32[]{:S(2)}) async-start(), calls=%async_computation.63 | async-start | bytes 294912 | tf_op jit(solution)/shard_map/reduce_scatter | solution.py:512
  2422.5 382.8 %reduce-scatter.100.cloned.1.call-start = ((), (), s32[]{:S(2)}) async-start(), calls=%async_computation.62 | async-start | bytes 1179648 | tf_op jit(solution)/shard_map/reduce_scatter | solution.py:511
  2427.0 444.6 %reduce-scatter.96.cloned.1.call-start = ((), (), s32[]{:S(2)}) async-start(), calls=%async_computation.60 | async-start | bytes 1179648 | tf_op jit(solution)/shard_map/reduce_scatter | solution.py:509
  2433.9 502.2 %reduce-scatter.94.cloned.1.call-start = ((), (), s32[]{:S(2)}) async-start(), calls=%async_computation.59 | async-start | bytes 294912 | tf_op jit(solution)/shard_map/reduce_scatter | solution.py:508
  2437.8 562.9 %reduce-scatter.92.cloned.1.call-start = ((), (), s32[]{:S(2)}) async-start(), calls=%async_computation.58 | async-start | bytes 294912 | tf_op jit(solution)/shard_map/reduce_scatter | solution.py:507
  2440.0 627.9 %reduce-scatter.88.cloned.1.call-start = ((), (), s32[]{:S(2)}) async-start(), calls=%async_computation.56 | async-start | bytes 1179648 | tf_op jit(solution)/shard_map/reduce_scatter | solution.py:505
  2444.4 696.1 %reduce-scatter.98.cloned.1.call-start = ((), (), s32[]{:S(2)}) async-start(), calls=%async_computation.61 | async-start | bytes 2654208 | tf_op jit(solution)/shard_map/reduce_scatter | solution.py:510
  2471.5 741.6 %reduce-scatter.86.cloned.1.call-start = ((), (), s32[]{:S(2)}) async-start(), calls=%async_computation.55 | async-start | bytes 2654208 | tf_op jit(solution)/shard_map/reduce_scatter | solution.py:504
  (609 other events, 18759.9 us)
Sparse Core Ops, SparseCore 0:
  10.2 44.2 all-gather.3
  56.7 38.9 all-gather.5
  200.8 41.4 all-gather.7
  1023.2 23.2 reduce-scatter.55
  1049.7 23.2 reduce-scatter.63
  1281.6 23.2 reduce-scatter.61
  1308.1 23.2 reduce-scatter.57
  1639.3 23.2 reduce-scatter.71
  1665.9 23.2 reduce-scatter.75
  2356.2 58.6 reduce-scatter.83
  2418.9 67.1 reduce-scatter.89
  2488.6 27.1 reduce-scatter.69
  2518.2 28.1 reduce-scatter.73
  2549.1 28.1 reduce-scatter.77
  2579.8 28.1 reduce-scatter.81
  2612.2 61.2 reduce-scatter.103
  2677.7 60.2 reduce-scatter.101
  2742.3 62.8 reduce-scatter.99
  2809.1 62.4 reduce-scatter.95
  2875.9 60.2 reduce-scatter.93
  2940.4 60.2 reduce-scatter.91
  3004.9 63.0 reduce-scatter.87
  3071.9 68.4 reduce-scatter.97
  3144.5 68.5 reduce-scatter.85
  (14 shorter events, 284.0 us)
where the time goes:
time: 3290 us; the launch traced here: 3220 us
  local copies, waits for them, and re-layouts  1030 us (31%)
  waiting for transfers between devices  951 us (29%)
  blocking collectives  898 us (27%)
  other arithmetic  162 us (5%)
  matrix products  151 us (5%)
    slice x36, local copies, waits for them, and re-layouts, spatial_taps(): lax.slice(padded, (0, row, column, 0), (count, row + reach, column + reac...  347 us
    psum x12, blocking collectives, batch_statistics(): lax.psum((jnp.concatenate(terms), jnp.sum(mask).reshape(1)), 'dp')  283 us
    unnamed x1312, local copies, waits for them, and re-layouts  202 us
    slice x16, local copies, waits for them, and re-layouts, untap(): return total[:, 1:side + 1, 1:side + 1, :]  184 us
    psum x6, blocking collectives, batch_backward(): packed = lax.psum(jnp.concatenate(terms), 'dp')  150 us
    pad x16, local copies, waits for them, and re-layouts, untap(): lax.pad(piece, jnp.float32(0.0), ((0, 0, 0), (row, side + 2 - row - reach...  144 us
    reduce_scatter x8, waiting for transfers between devices, expand_sum(): lax.psum_scatter(value.astype(jnp.bfloat16), 'mp', scatter_dimension=3, t...  127 us
    reduce_scatter x4, waiting for transfers between devices, shards(): lax.psum_scatter(picture_partial.astype(jnp.bfloat16), 'mp', scatter_dime...  101 us
  transfers between devices with their start and end apart: 38, of which 26 were waited for; matrix products, arithmetic and copies ran while one was open for 22% of the time, Pallas kernels for 0%

commit v1 on v0

v1 whole, which is shorter than its diff:
```python
import jax
import jax.numpy as jnp
from jax import lax
from jax.sharding import PartitionSpec as P

eps_norm = 1e-05
highest = lax.Precision.HIGHEST


def matmul(left, right):
    return jnp.dot(left, right, preferred_element_type=jnp.float32)


def contract_rows(left, right):
    return lax.dot_general(
        left, right, (((0,), (0,)), ((), ())), preferred_element_type=jnp.float32
    )


def contract_cols(left, right):
    return lax.dot_general(
        left, right, (((1,), (1,)), ((), ())), preferred_element_type=jnp.float32
    )


def swish_slope(value):
    sigma = jax.nn.sigmoid(value)
    return sigma * (1.0 + value * (1.0 - sigma))


def pixel_masks(sizes, side):
    half = side // 2
    height = sizes[:, 0]
    breadth = sizes[:, 1]
    places = jnp.arange(side, dtype=jnp.int32)
    inside = (
        (places[None, :, None] < height[:, None, None])
        & (places[None, None, :] < breadth[:, None, None])
    ).astype(jnp.float32)
    halves = jnp.arange(half, dtype=jnp.int32)
    reduced = (
        (halves[None, :, None] < ((height + 1) // 2)[:, None, None])
        & (halves[None, None, :] < ((breadth + 1) // 2)[:, None, None])
    ).astype(jnp.float32)
    return (inside, reduced)


def spatial_taps(field, stride):
    count, side, channels = (field.shape[0], field.shape[1], field.shape[3])
    reach = stride * (side // stride - 1) + 1
    padded = jnp.pad(field, ((0, 0), (1, 1), (1, 1), (0, 0)))
    pieces = []
    for row in range(3):
        for column in range(3):
            pieces.append(
                lax.slice(
                    padded,
                    (0, row, column, 0),
                    (count, row + reach, column + reach, channels),
                    (1, stride, stride, 1),
                )
            )
    return jnp.concatenate(pieces, axis=3)


def untap(grads, stride, side):
    count, out_side = (grads.shape[0], grads.shape[1])
    channels = grads.shape[3] // 9
    reach = stride * (out_side - 1) + 1
    total = jnp.zeros((count, side + 2, side + 2, channels), jnp.float32)
    for row in range(3):
        for column in range(3):
            first = (row * 3 + column) * channels
            piece = grads[:, :, :, first : first + channels]
            total = total + lax.pad(
                piece,
                jnp.float32(0.0),
                (
                    (0, 0, 0),
                    (row, side + 2 - row - reach, stride - 1),
                    (column, side + 2 - column - reach, stride - 1),
                    (0, 0, 0),
                ),
            )
    return total[:, 1 : side + 1, 1 : side + 1, :]


def batch_statistics(fields, mask):
    weights = mask[..., None]
    terms = []
    for field in fields:
        terms.append(jnp.sum(field * weights, axis=(0, 1, 2)))
        terms.append(jnp.sum(field * field * weights, axis=(0, 1, 2)))
    packed, total_vector = lax.psum((jnp.concatenate(terms), jnp.sum(mask).reshape(1)), "dp")
    total = total_vector[0]
    result = []
    offset = 0
    for field in fields:
        breadth = field.shape[3]
        mean = packed[offset : offset + breadth] / total
        second = packed[offset + breadth : offset + 2 * breadth] / total
        result.append((mean, lax.rsqrt(second - mean * mean + eps_norm)))
        offset = offset + 2 * breadth
    return (result, total)


def standardize(raw, statistics, gain, shift):
    mean, scale = statistics
    normed = (raw - mean) * scale
    return (normed, normed * gain + shift)


def batch_backward(grads, normeds, scales, gains, mask, total, extras):
    terms = []
    for grad, normed in zip(grads, normeds):
        terms.append(jnp.sum(grad * normed, axis=(0, 1, 2)))
        terms.append(jnp.sum(grad, axis=(0, 1, 2)))
    for extra in extras:
        terms.append(extra)
    packed = lax.psum(jnp.concatenate(terms), "dp")
    results = []
    pairs = []
    offset = 0
    for grad, normed, scale, gain in zip(grads, normeds, scales, gains):
        breadth = grad.shape[3]
        gain_grad = packed[offset : offset + breadth]
        shift_grad = packed[offset + breadth : offset + 2 * breadth]
        offset = offset + 2 * breadth
        results.append(
            scale * gain * (grad - mask[..., None] * (shift_grad + normed * gain_grad) / total)
        )
        pairs.append((gain_grad, shift_grad))
    rest = []
    for extra in extras:
        rest.append(packed[offset : offset + extra.shape[0]])
        offset = offset + extra.shape[0]
    return (results, pairs, rest)


def excite_forward(field, mask, pixels, squeeze_full, squeeze_bias, excite_full, excite_bias):
    pooled = jnp.sum(field * mask[..., None], axis=(1, 2)) / pixels[:, None]
    inner_pre = (
        jnp.dot(pooled, squeeze_full.astype(jnp.float32), precision=highest) + squeeze_bias
    )
    hidden = jax.nn.silu(inner_pre)
    scale = jax.nn.sigmoid(
        jnp.dot(hidden, excite_full.astype(jnp.float32), precision=highest) + excite_bias
    )
    return (pooled, inner_pre, hidden, scale)


def excite_backward(grad_branch, field, mask, pixels, saved, squeeze_full, excite_full):
    pooled, inner_pre, hidden, scale = saved
    grad_scale = jnp.sum(grad_branch * field, axis=(1, 2))
    grad_gate = grad_scale * scale * (1.0 - scale)
    excite_grad = jnp.dot(hidden.T, grad_gate, precision=highest)
    grad_hidden = jnp.dot(grad_gate, excite_full.astype(jnp.float32).T, precision=highest)
    grad_inner = grad_hidden * swish_slope(inner_pre)
    squeeze_grad = jnp.dot(pooled.T, grad_inner, precision=highest)
    grad_pooled = jnp.dot(grad_inner, squeeze_full.astype(jnp.float32).T, precision=highest)
    grad_field = (
        grad_branch * scale[:, None, None, :]
        + grad_pooled[:, None, None, :] * mask[..., None] / pixels[:, None, None, None]
    )
    return (
        grad_field,
        squeeze_grad,
        excite_grad,
        jnp.sum(grad_inner, axis=0),
        jnp.sum(grad_gate, axis=0),
    )


def whole_vector(value):
    return lax.all_gather(value, "mp", axis=0, tiled=True)


def whole_matrix(value, dp_axis, mp_axis):
    value = lax.all_gather(value, "dp", axis=dp_axis, tiled=True)
    return lax.all_gather(value, "mp", axis=mp_axis, tiled=True)


def own_part(value, dp_axis, mp_axis):
    value = lax.psum_scatter(
        value.astype(jnp.bfloat16), "mp", scatter_dimension=mp_axis, tiled=True
    )
    return lax.psum_scatter(value, "dp", scatter_dimension=dp_axis, tiled=True).astype(
        jnp.float32
    )


def shards(
    images,
    image_size,
    entry_weight,
    entry_gain,
    entry_shift,
    stride_weight,
    stride_gain,
    stride_shift,
    expand_weight,
    expand_gain,
    expand_shift,
    project_weight,
    project_gain,
    project_shift,
    squeeze_weight,
    squeeze_bias,
    excite_weight,
    excite_bias,
    reduce_weight,
    reduce_gain,
    reduce_shift,
    spatial_weight,
    spatial_gain,
    spatial_shift,
    widen_weight,
    widen_gain,
    widen_shift,
    shrink_weight,
    shrink_bias,
    gating_weight,
    gating_bias,
    cotangent,
):
    place = lax.axis_index("mp")
    count, side = (images.shape[1], images.shape[2])
    half = side // 2
    channels_in = images.shape[4]
    entry_full = whole_matrix(entry_weight, 0, 1)
    stride_full = whole_matrix(stride_weight, 2, 3)
    expand_full = whole_matrix(expand_weight, 1, 0)
    project_full = whole_matrix(project_weight, 0, 1)
    squeeze_full = whole_matrix(squeeze_weight, 1, 0)
    excite_full = whole_matrix(excite_weight, 0, 1)
    reduce_full = whole_matrix(reduce_weight, 0, 1)
    spatial_full = whole_matrix(spatial_weight, 2, 3)
    widen_full = whole_matrix(widen_weight, 1, 0)
    shrink_full = whole_matrix(shrink_weight, 1, 0)
    gating_full = whole_matrix(gating_weight, 0, 1)
    entry_gain, entry_shift = whole_vector(entry_gain), whole_vector(entry_shift)
    stride_gain, stride_shift = whole_vector(stride_gain), whole_vector(stride_shift)
    expand_gain, expand_shift = whole_vector(expand_gain), whole_vector(expand_shift)
    project_gain, project_shift = whole_vector(project_gain), whole_vector(project_shift)
    reduce_gain, reduce_shift = whole_vector(reduce_gain), whole_vector(reduce_shift)
    spatial_gain, spatial_shift = whole_vector(spatial_gain), whole_vector(spatial_shift)
    widen_gain, widen_shift = whole_vector(widen_gain), whole_vector(widen_shift)
    excite_bias, gating_bias = whole_vector(excite_bias), whole_vector(gating_bias)
    seed_grad = lax.all_to_all(cotangent, "mp", split_axis=0, concat_axis=4, tiled=True)[0]
    picture = lax.dynamic_index_in_dim(images, place, 0, keepdims=False)
    sizes = lax.dynamic_index_in_dim(image_size, place, 0, keepdims=False)
    inside, reduced = pixel_masks(sizes, side)
    pixels = jnp.sum(reduced, axis=(1, 2))
    reduced_mask = reduced[..., None]
    entry_raw = matmul(picture.reshape(-1, channels_in), entry_full).reshape(
        count, side, side, -1
    )
    stats, inside_total = batch_statistics([entry_raw], inside)
    entry_stats = stats[0]
    entry_normed, entry_pre = standardize(entry_raw, entry_stats, entry_gain, entry_shift)
    entry_act = (jax.nn.silu(entry_pre) * inside[..., None]).astype(jnp.bfloat16)
    entry_wide = entry_act
    bottleneck = entry_wide.shape[3]
    stride_taps = spatial_taps(entry_wide, 2).reshape(-1, 9 * bottleneck)
    stride_raw = matmul(stride_taps, stride_full.reshape(9 * bottleneck, -1)).reshape(
        count, half, half, -1
    )
    stats, reduced_total = batch_statistics([stride_raw], reduced)
    stride_stats = stats[0]
    stride_normed, stride_pre = standardize(stride_raw, stride_stats, stride_gain, stride_shift)
    stride_act = (jax.nn.silu(stride_pre) * reduced_mask).astype(jnp.bfloat16)
    local_bottleneck = stride_act.shape[3]
    stride_flat = stride_act.reshape(-1, local_bottleneck)
    expand_raw = matmul(stride_flat, expand_full).reshape(count, half, half, -1)
    strided_flat = picture[:, ::2, ::2, :].reshape(-1, channels_in)
    project_raw = matmul(strided_flat, project_full).reshape(count, half, half, -1)
    stats, reduced_total = batch_statistics([expand_raw, project_raw], reduced)
    expand_stats, project_stats = (stats[0], stats[1])
    expand_normed, expand_pre = standardize(expand_raw, expand_stats, expand_gain, expand_shift)
    project_normed, project_pre = standardize(
        project_raw, project_stats, project_gain, project_shift
    )
    first_saved = excite_forward(
        expand_pre, reduced, pixels, squeeze_full, squeeze_bias, excite_full, excite_bias
    )
    first_sum = expand_pre * first_saved[3][:, None, None, :] + project_pre
    first_out = (jax.nn.silu(first_sum) * reduced_mask).astype(jnp.bfloat16)
    block_wide = first_out
    block_flat = block_wide.reshape(-1, block_wide.shape[3])
    reduce_raw = matmul(block_flat, reduce_full).reshape(count, half, half, -1)
    stats, reduced_total = batch_statistics([reduce_raw], reduced)
    reduce_stats = stats[0]
    reduce_normed, reduce_pre = standardize(reduce_raw, reduce_stats, reduce_gain, reduce_shift)
    reduce_act = (jax.nn.silu(reduce_pre) * reduced_mask).astype(jnp.bfloat16)
    reduce_wide = reduce_act
    second_taps = spatial_taps(reduce_wide, 1).reshape(-1, 9 * bottleneck)
    spatial_raw = matmul(second_taps, spatial_full.reshape(9 * bottleneck, -1)).reshape(
        count, half, half, -1
    )
    stats, reduced_total = batch_statistics([spatial_raw], reduced)
    spatial_stats = stats[0]
    spatial_normed, spatial_pre = standardize(
        spatial_raw, spatial_stats, spatial_gain, spatial_shift
    )
    spatial_act = (jax.nn.silu(spatial_pre) * reduced_mask).astype(jnp.bfloat16)
    spatial_flat = spatial_act.reshape(-1, local_bottleneck)
    widen_raw = matmul(spatial_flat, widen_full).reshape(count, half, half, -1)
    stats, reduced_total = batch_statistics([widen_raw], reduced)
    widen_stats = stats[0]
    widen_normed, widen_pre = standardize(widen_raw, widen_stats, widen_gain, widen_shift)
    second_saved = excite_forward(
        widen_pre, reduced, pixels, shrink_full, shrink_bias, gating_full, gating_bias
    )
    second_sum = widen_pre * second_saved[3][:, None, None, :] + first_out.astype(jnp.float32)
    output = (jax.nn.silu(second_sum) * reduced_mask).astype(jnp.bfloat16)
    second_grad = seed_grad.astype(jnp.float32) * reduced_mask * swish_slope(second_sum)
    widen_grad, shrink_grad, gating_grad, shrink_bias_grad, gating_bias_grad = excite_backward(
        second_grad, widen_pre, reduced, pixels, second_saved, shrink_full, gating_full
    )
    grads, widen_pair, extras = batch_backward(
        [widen_grad],
        [widen_normed],
        [widen_stats[1]],
        [widen_gain],
        reduced,
        reduced_total,
        (shrink_bias_grad, gating_bias_grad),
    )
    widen_pair = widen_pair[0]
    shrink_bias_total, gating_bias_total = (extras[0], extras[1])
    widen_local = grads[0].astype(jnp.bfloat16)
    widen_low = widen_local
    widen_flat = widen_low.reshape(-1, widen_low.shape[3])
    widen_weight_grad = contract_rows(spatial_flat, widen_flat)
    spatial_act_grad = contract_cols(widen_flat, widen_full).reshape(count, half, half, -1)
    spatial_grad = spatial_act_grad * reduced_mask * swish_slope(spatial_pre)
    grads, spatial_pair, extras = batch_backward(
        [spatial_grad],
        [spatial_normed],
        [spatial_stats[1]],
        [spatial_gain],
        reduced,
        reduced_total,
        (),
    )
    spatial_pair = spatial_pair[0]
    spatial_low = grads[0].astype(jnp.bfloat16).reshape(-1, local_bottleneck)
    spatial_weight_grad = contract_rows(second_taps, spatial_low).reshape(
        3, 3, bottleneck, local_bottleneck
    )
    second_tap_grad = contract_cols(spatial_low, spatial_full.reshape(9 * bottleneck, -1))
    reduce_act_grad = untap(second_tap_grad.reshape(count, half, half, -1), 1, half)
    reduce_grad = reduce_act_grad * reduced_mask * swish_slope(reduce_pre)
    grads, reduce_pair, extras = batch_backward(
        [reduce_grad],
        [reduce_normed],
        [reduce_stats[1]],
        [reduce_gain],
        reduced,
        reduced_total,
        (),
    )
    reduce_pair = reduce_pair[0]
    reduce_low = grads[0].astype(jnp.bfloat16).reshape(-1, local_bottleneck)
    reduce_weight_grad = contract_rows(block_flat, reduce_low)
    first_partial = contract_cols(reduce_low, reduce_full).reshape(count, half, half, -1)
    first_out_grad = first_partial + second_grad
    first_grad = first_out_grad * reduced_mask * swish_slope(first_sum)
    expand_grad, squeeze_grad, excite_grad, squeeze_bias_grad, excite_bias_grad = (
        excite_backward(
            first_grad, expand_pre, reduced, pixels, first_saved, squeeze_full, excite_full
        )
    )
    grads, pairs, extras = batch_backward(
        [expand_grad, first_grad],
        [expand_normed, project_normed],
        [expand_stats[1], project_stats[1]],
        [expand_gain, project_gain],
        reduced,
        reduced_total,
        (squeeze_bias_grad, excite_bias_grad),
    )
    expand_pair, project_pair = (pairs[0], pairs[1])
    squeeze_bias_total, excite_bias_total = (extras[0], extras[1])
    expand_local = grads[0].astype(jnp.bfloat16)
    expand_low = expand_local
    expand_flat = expand_low.reshape(-1, expand_low.shape[3])
    expand_weight_grad = contract_rows(stride_flat, expand_flat)
    stride_act_grad = contract_cols(expand_flat, expand_full).reshape(count, half, half, -1)
    project_low = grads[1].astype(jnp.bfloat16).reshape(-1, grads[1].shape[3])
    project_weight_grad = contract_rows(strided_flat, project_low)
    strided_grad = contract_cols(project_low, project_full).reshape(
        count, half, half, channels_in
    )
    stride_grad = stride_act_grad * reduced_mask * swish_slope(stride_pre)
    grads, stride_pair, extras = batch_backward(
        [stride_grad],
        [stride_normed],
        [stride_stats[1]],
        [stride_gain],
        reduced,
        reduced_total,
        (),
    )
    stride_pair = stride_pair[0]
    stride_low = grads[0].astype(jnp.bfloat16).reshape(-1, local_bottleneck)
    stride_weight_grad = contract_rows(stride_taps, stride_low).reshape(
        3, 3, bottleneck, local_bottleneck
    )
    first_tap_grad = contract_cols(stride_low, stride_full.reshape(9 * bottleneck, -1))
    entry_act_grad = untap(first_tap_grad.reshape(count, half, half, -1), 2, side)
    entry_grad = entry_act_grad * inside[..., None] * swish_slope(entry_pre)
    grads, entry_pair, extras = batch_backward(
        [entry_grad], [entry_normed], [entry_stats[1]], [entry_gain], inside, inside_total, ()
    )
    entry_pair = entry_pair[0]
    entry_low = grads[0].astype(jnp.bfloat16).reshape(-1, local_bottleneck)
    entry_weight_grad = contract_rows(picture.reshape(-1, channels_in), entry_low)
    picture_partial = contract_cols(entry_low, entry_full).reshape(
        count, side, side, channels_in
    )
    picture_partial = picture_partial + lax.pad(
        strided_grad, jnp.float32(0.0), ((0, 0, 0), (0, 1, 1), (0, 1, 1), (0, 0, 0))
    )

    def own_vector(value):
        return lax.psum_scatter(value, "mp", scatter_dimension=0, tiled=True)

    picture_grad = lax.all_to_all(
        picture_partial.astype(jnp.bfloat16)[None], "mp", split_axis=4, concat_axis=0, tiled=True
    ).astype(jnp.float32)
    result = lax.all_to_all(output[None], "mp", split_axis=4, concat_axis=0, tiled=True)
    return (
        result,
        picture_grad,
        own_part(entry_weight_grad, 0, 1),
        own_vector(entry_pair[0]),
        own_vector(entry_pair[1]),
        own_part(stride_weight_grad, 2, 3),
        own_vector(stride_pair[0]),
        own_vector(stride_pair[1]),
        own_part(expand_weight_grad, 1, 0),
        own_vector(expand_pair[0]),
        own_vector(expand_pair[1]),
        own_part(project_weight_grad, 0, 1),
        own_vector(project_pair[0]),
        own_vector(project_pair[1]),
        own_part(squeeze_grad, 1, 0),
        lax.psum(squeeze_bias_total, "mp"),
        own_part(excite_grad, 0, 1),
        own_vector(excite_bias_total),
        own_part(reduce_weight_grad, 0, 1),
        own_vector(reduce_pair[0]),
        own_vector(reduce_pair[1]),
        own_part(spatial_weight_grad, 2, 3),
        own_vector(spatial_pair[0]),
        own_vector(spatial_pair[1]),
        own_part(widen_weight_grad, 1, 0),
        own_vector(widen_pair[0]),
        own_vector(widen_pair[1]),
        own_part(shrink_grad, 1, 0),
        lax.psum(shrink_bias_total, "mp"),
        own_part(gating_grad, 0, 1),
        own_vector(gating_bias_total),
    )


def solution(mesh):
    in_specs = (
        P(None, "dp", None, None, None),
        P(None, "dp", None),
        P("dp", "mp"),
        P("mp"),
        P("mp"),
        P(None, None, "dp", "mp"),
        P("mp"),
        P("mp"),
        P("mp", "dp"),
        P("mp"),
        P("mp"),
        P("dp", "mp"),
        P("mp"),
        P("mp"),
        P("mp", "dp"),
        P(),
        P("dp", "mp"),
        P("mp"),
        P("dp", "mp"),
        P("mp"),
        P("mp"),
        P(None, None, "dp", "mp"),
        P("mp"),
        P("mp"),
        P("mp", "dp"),
        P("mp"),
        P("mp"),
        P("mp", "dp"),
        P(),
        P("dp", "mp"),
        P("mp"),
        P(None, "dp", None, None, "mp"),
    )
    out_specs = (
        P(None, "dp", None, None, "mp"),
        P(None, "dp", None, None, "mp"),
        P("dp", "mp"),
        P("mp"),
        P("mp"),
        P(None, None, "dp", "mp"),
        P("mp"),
        P("mp"),
        P("mp", "dp"),
        P("mp"),
        P("mp"),
        P("dp", "mp"),
        P("mp"),
        P("mp"),
        P("mp", "dp"),
        P(),
        P("dp", "mp"),
        P("mp"),
        P("dp", "mp"),
        P("mp"),
        P("mp"),
        P(None, None, "dp", "mp"),
        P("mp"),
        P("mp"),
        P("mp", "dp"),
        P("mp"),
        P("mp"),
        P("mp", "dp"),
        P(),
        P("dp", "mp"),
        P("mp"),
    )
    return jax.shard_map(shards, mesh=mesh, in_specs=in_specs, out_specs=out_specs, check_vma=False)
```

time: 3290 us -> 2010 us (0.61); the launches traced: 3220 us -> 2000 us
  local copies, waits for them, and re-layouts: 1030 us -> 346 us
  blocking collectives: 898 us -> 668 us
  waiting for transfers between devices: 951 us -> 804 us
  other arithmetic: 162 us -> 68.5 us
  matrix products: 151 us -> 79.5 us
    slice x36 -> x9, local copies, waits for them, and re-layouts: 347 us -> 13.2 us  [spatial_taps(): lax.slice(padded, (0, row, column, 0), (count, row + reach, column + reac...]
    reduce_scatter x27 -> x16, waiting for transfers between devices: 909 us -> 618 us  [the longest x9 570 us: own_part(): lax.psum_scatter(value, 'dp', scatter_dimension=dp_axis, tiled=True)]
    slice x16 -> x4, local copies, waits for them, and re-layouts: 184 us -> 25.7 us  [untap(): return total[:, 1:side + 1, 1:side + 1, :]]
    psum x12 -> x6, blocking collectives: 283 us -> 145 us  [batch_statistics(): lax.psum((jnp.concatenate(terms), jnp.sum(mask).reshape(1)), 'dp')]
    pad x16 -> x3, local copies, waits for them, and re-layouts: 144 us -> 26.9 us  [untap(): lax.pad(piece, jnp.float32(0.0), ((0, 0, 0), (row, side + 2 - row - reach...]
    unnamed x46 -> x40, waiting for transfers between devices: 41.6 us -> 135 us
    all_gather x3 -> x10, waiting for transfers between devices: 0.01 us -> 51.2 us  [the longest x3 51.1 us: whole_matrix(): value = lax.all_gather(value, 'dp', axis=dp_axis, tiled=True)]
    psum x8 -> x0, blocking collectives: 49.1 us -> none  [channel_sum(): return lax.psum(value, 'mp')]
  transfers between devices with their start and end apart: 38 -> 36, of which waited for: 26 -> 16; matrix products, arithmetic and copies ran while one was open for 22% -> 22% of each run, Pallas kernels for 0% -> 0%
where the time goes in v1:
time: 2010 us; the launch traced here: 2000 us
  waiting for transfers between devices  804 us (40%)
  blocking collectives  668 us (33%)
  local copies, waits for them, and re-layouts  346 us (17%)
  matrix products  79.5 us (4%)
  other arithmetic  68.5 us (3%)
    reduce_scatter x9, waiting for transfers between devices, own_part(): lax.psum_scatter(value, 'dp', scatter_dimension=dp_axis, tiled=True)  570 us
    all_gather x8, blocking collectives, whole_matrix(): value = lax.all_gather(value, 'dp', axis=dp_axis, tiled=True)  258 us
    unnamed x383, local copies, waits for them, and re-layouts  188 us
    psum x6, blocking collectives, batch_statistics(): lax.psum((jnp.concatenate(terms), jnp.sum(mask).reshape(1)), 'dp')  145 us
    psum x6, blocking collectives, batch_backward(): packed = lax.psum(jnp.concatenate(terms), 'dp')  142 us
    unnamed x40, waiting for transfers between devices  135 us
    all_gather x16, blocking collectives, whole_vector(): return lax.all_gather(value, 'mp', axis=0, tiled=True)  87.6 us
    all_gather x3, waiting for transfers between devices, whole_matrix(): value = lax.all_gather(value, 'dp', axis=dp_axis, tiled=True)  51.1 us
  transfers between devices with their start and end apart: 36, of which 16 were waited for; matrix products, arithmetic and copies ran while one was open for 22% of the time, Pallas kernels for 0%

profile of v1, /device:TPU:0, one launch (start us, length us, event | category | flops | bytes accessed | tf_op | source)
XLA Modules:
  0.0 1998.4 jit_solution(7788473287682646370)
XLA Ops:
  9.5 34.9 %all_gather.114 = bf16[1024,128]{1,0:T(8,128)(2,1)} all-gather(bf16[128,128]{1,0:T(8,128)(2,1)} %param.34), channel_id=1, replica_groups=mesh['dp'=8,'mp'=4] {'dp'}, dimensions={0}, use_global_device_ids=true | all-gather | bytes 294912 | tf_op jit(solution)/shard_map/all_gather | solution.py:179
  53.7 42.0 %all-gather.29.cloned.1.call-done = bf16[3,3,512,128]{3,2,1,0:T(8,128)(2,1)} async-done(((bf16[3,3,64,128]{3,2,1,0:T(8,128)(2,1)}), bf16[3,3,512,128]{3,2,1,0:T(8,128)(2,1)}) %all-gather.29.cloned.1.call-update) | async-done | bytes 1179664 | tf_op jit(solution)/shard_map/all_gather | solution.py:179
  95.7 33.7 %all_gather.122 = bf16[128,2048]{1,0:T(8,128)(2,1)} all-gather(bf16[128,256]{1,0:T(8,128)(2,1)S(1)} %copy-done.74), channel_id=1, replica_groups=mesh['dp'=8,'mp'=4] {'dp'}, dimensions={1}, use_global_device_ids=true | all-gather | bytes 589824 | tf_op jit(solution)/shard_map/all_gather | solution.py:179
  129.5 33.6 %all_gather.135 = bf16[2048,128]{1,0:T(8,128)(2,1)} all-gather(bf16[256,128]{1,0:T(8,128)(2,1)S(1)} %copy-done.75), channel_id=1, replica_groups=mesh['dp'=8,'mp'=4] {'dp'}, dimensions={0}, use_global_device_ids=true | all-gather | bytes 589824 | tf_op jit(solution)/shard_map/all_gather | solution.py:179
  167.6 33.3 %all_gather.143 = bf16[128,2048]{1,0:T(8,128)(2,1)} all-gather(bf16[128,256]{1,0:T(8,128)(2,1)S(1)} %copy-done.76), channel_id=1, replica_groups=mesh['dp'=8,'mp'=4] {'dp'}, dimensions={1}, use_global_device_ids=true | all-gather | bytes 589824 | tf_op jit(solution)/shard_map/all_gather | solution.py:179
  248.7 30.6 %all_gather.128 = bf16[512,128]{0,1:T(8,128)(2,1)S(1)} all-gather(bf16[512,16]{0,1:T(8,128)(2,1)S(1)} %copy-done.109), channel_id=1, replica_groups=mesh['dp'=8,'mp'=4] {'dp'}, dimensions={1}, use_global_device_ids=true | all-gather | bytes 147456 | tf_op jit(solution)/shard_map/all_gather | solution.py:179
  290.4 30.5 %all_gather.130 = bf16[128,512]{1,0:T(8,128)(2,1)S(1)} all-gather(bf16[16,512]{1,0:T(8,128)(2,1)S(1)} %copy-done.110), channel_id=1, replica_groups=mesh['dp'=8,'mp'=4] {'dp'}, dimensions={0}, use_global_device_ids=true | all-gather | bytes 147456 | tf_op jit(solution)/shard_map/all_gather | solution.py:179
  531.3 34.9 %psum.128 = f32[8192]{0:T(1024)S(1)} all-reduce(f32[8192]{0:T(1024)S(1)} %pad_maximum_fusion), channel_id=1, replica_groups=mesh['dp'=8,'mp'=4] {'dp'}, use_global_device_ids=true, to_apply=%region_14.15 | all-reduce | flops 8192 | bytes 65536 | tf_op jit(solution)/shard_map/psum | solution.py:94
  632.7 33.9 %psum.131 = f32[4096]{0:T(1024)} all-reduce(f32[4096]{0:T(1024)} %pad_maximum_fusion.2), channel_id=1, replica_groups=mesh['dp'=8,'mp'=4] {'dp'}, use_global_device_ids=true, to_apply=%region_25.26 | all-reduce | flops 4096 | bytes 32768 | tf_op jit(solution)/shard_map/psum | solution.py:94
  686.2 34.4 %psum.132 = f32[6272]{0:T(1024)} all-reduce(f32[6272]{0:T(1024)} %pad_maximum_fusion.1), channel_id=1, replica_groups=mesh['dp'=8,'mp'=4] {'dp'}, use_global_device_ids=true, to_apply=%region_32.33 | all-reduce | flops 6272 | bytes 50176 | tf_op jit(solution)/shard_map/psum | solution.py:120
  784.9 33.4 %psum.135 = f32[10368]{0:T(1024)S(1)} all-reduce(f32[10368]{0:T(1024)S(1)} %constant_dynamic-update-slice_fusion.13), channel_id=1, replica_groups=mesh['dp'=8,'mp'=4] {'dp'}, use_global_device_ids=true, to_apply=%region_46.47 | all-reduce | flops 10368 | bytes 82944 | tf_op jit(solution)/shard_map/psum | solution.py:120
  1053.8 34.0 %reduce-scatter.73.cloned.1.call-done = bf16[128,2048]{1,0:T(8,128)(2,1)} async-done(((bf16[512,2048]{1,0:T(8,128)(2,1)}), bf16[128,2048]{1,0:T(8,128)(2,1)}) %reduce-scatter.73.cloned.1.call-update) | async-done | bytes 524304
  1089.9 45.0 %reduce-scatter.43.cloned.1.call-done = bf16[1024,512]{1,0:T(8,128)(2,1)} async-done(((bf16[1024,2048]{1,0:T(8,128)(2,1)}), bf16[1024,512]{1,0:T(8,128)(2,1)}) %reduce-scatter.43.cloned.1.call-update) | async-done | bytes 1048592 | tf_op jit(solution)/shard_map/reduce_scatter | solution.py:184
  1135.0 50.3 %reduce-scatter.75.cloned.1.call-done = bf16[128,4608]{1,0:T(8,128)(2,1)} async-done(((bf16[512,4608]{1,0:T(8,128)(2,1)}), bf16[128,4608]{1,0:T(8,128)(2,1)}) %reduce-scatter.75.cloned.1.call-update) | async-done | bytes 1179664
  1190.4 45.3 %reduce-scatter.69.cloned.1.call-done = bf16[128,4608]{1,0:T(8,128)(2,1)} async-done(((bf16[512,4608]{1,0:T(8,128)(2,1)}), bf16[128,4608]{1,0:T(8,128)(2,1)}) %reduce-scatter.69.cloned.1.call-update) | async-done | bytes 1179664
  1407.0 59.9 %reduce-scatter.65.cloned.1.call-done = bf16[16,512]{1,0:T(8,128)(2,1)} async-done(((bf16[128,512]{1,0:T(8,128)(2,1)}), bf16[16,512]{1,0:T(8,128)(2,1)}) %reduce-scatter.65.cloned.1.call-update) | async-done | bytes 16400 | tf_op jit(solution)/shard_map/reduce_scatter | solution.py:187
  1468.2 61.7 %reduce-scatter.51.cloned.1.call-done = bf16[16,512]{1,0:T(8,128)(2,1)} async-done(((bf16[128,512]{1,0:T(8,128)(2,1)}), bf16[16,512]{1,0:T(8,128)(2,1)}) %reduce-scatter.51.cloned.1.call-update) | async-done | bytes 16400 | tf_op jit(solution)/shard_map/reduce_scatter | solution.py:187
  1531.3 62.7 %reduce-scatter.35.cloned.1.call-done = bf16[128,128]{1,0:T(8,128)(2,1)} async-done(((bf16[1024,128]{1,0:T(8,128)(2,1)}), bf16[128,128]{1,0:T(8,128)(2,1)}) %reduce-scatter.35.cloned.1.call-update) | async-done | bytes 32784 | tf_op jit(solution)/shard_map/reduce_scatter | solution.py:187
  1595.4 63.4 %reduce-scatter.59.cloned.1.call-done = bf16[128,256]{1,0:T(8,128)(2,1)} async-done(((bf16[128,2048]{1,0:T(8,128)(2,1)}), bf16[128,256]{1,0:T(8,128)(2,1)}) %reduce-scatter.59.cloned.1.call-update) | async-done | bytes 65552 | tf_op jit(solution)/shard_map/reduce_scatter | solution.py:187
  1660.4 63.6 %reduce-scatter.41.cloned.1.call-done = bf16[128,256]{1,0:T(8,128)(2,1)} async-done(((bf16[128,2048]{1,0:T(8,128)(2,1)}), bf16[128,256]{1,0:T(8,128)(2,1)}) %reduce-scatter.41.cloned.1.call-update) | async-done | bytes 65552 | tf_op jit(solution)/shard_map/reduce_scatter | solution.py:187
  1725.5 62.7 %reduce-scatter.53.cloned.1.call-done = bf16[256,128]{1,0:T(8,128)(2,1)} async-done(((bf16[2048,128]{1,0:T(8,128)(2,1)}), bf16[256,128]{1,0:T(8,128)(2,1)}) %reduce-scatter.53.cloned.1.call-update) | async-done | bytes 65552 | tf_op jit(solution)/shard_map/reduce_scatter | solution.py:187
  1789.7 64.8 %reduce-scatter.45.cloned.1.call-done = bf16[128,512]{1,0:T(8,128)(2,1)} async-done(((bf16[1024,512]{1,0:T(8,128)(2,1)}), bf16[128,512]{1,0:T(8,128)(2,1)}) %reduce-scatter.45.cloned.1.call-update) | async-done | bytes 131088 | tf_op jit(solution)/shard_map/reduce_scatter | solution.py:187
  1856.1 65.4 %reduce-scatter.55.cloned.1.call-done = bf16[3,3,64,128]{3,2,1,0:T(8,128)(2,1)} async-done(((bf16[3,3,512,128]{3,2,1,0:T(8,128)(2,1)}), bf16[3,3,64,128]{3,2,1,0:T(8,128)(2,1)}) %reduce-scatter.55.cloned.1.call-update) | async-done | bytes 147472 | tf_op jit(solution)/shard_map/reduce_scatter | solution.py:187
  1923.2 65.2 %reduce-scatter.37.cloned.1.call-done = bf16[3,3,64,128]{3,2,1,0:T(8,128)(2,1)} async-done(((bf16[3,3,512,128]{3,2,1,0:T(8,128)(2,1)}), bf16[3,3,64,128]{3,2,1,0:T(8,128)(2,1)}) %reduce-scatter.37.cloned.1.call-update) | async-done | bytes 147472 | tf_op jit(solution)/shard_map/reduce_scatter | solution.py:187
  (636 shorter events, 860.6 us)
Async XLA Ops:
  9.4 452.0 %all-gather.27.cloned.1.call-start = ((), (), s32[]{:S(2)}) async-start(), calls=%async_computation.25 | async-start | bytes 1310720 | tf_op jit(solution)/shard_map/all_gather | solution.py:180
  44.5 455.7 %all-gather.37.cloned.1.call-start = ((), (), s32[]{:S(2)}) async-start(), calls=%async_computation.30 | async-start | bytes 5242880 | tf_op jit(solution)/shard_map/all_gather | solution.py:180
  53.6 450.5 %all-gather.31.cloned.1.call-start = ((), (), s32[]{:S(2)}) async-start(), calls=%async_computation.27 | async-start | bytes 5898240 | tf_op jit(solution)/shard_map/all_gather | solution.py:180
  95.7 432.1 %all-gather.33.cloned.1.call-start = ((), (), s32[]{:S(2)}) async-start(), calls=%async_computation.28 | async-start | bytes 2621440 | tf_op jit(solution)/shard_map/all_gather | solution.py:180
  129.4 441.3 %all-gather.39.cloned.1.call-start = ((), (), s32[]{:S(2)}) async-start(), calls=%async_computation.31 | async-start | bytes 2621440 | tf_op jit(solution)/shard_map/all_gather | solution.py:180
  163.1 438.1 %all-gather.43.cloned.1.call-start = ((), (), s32[]{:S(2)}) async-start(), calls=%async_computation.33 | async-start | bytes 5898240 | tf_op jit(solution)/shard_map/all_gather | solution.py:180
  163.9 295.9 %all-to-all-start.1 = ((bf16[4,3,8,8,512]{4,3,2,1,0:T(8,128)(2,1)}), bf16[4,3,8,8,512]{4,3,2,1,0:T(8,128)(2,1)S(1)}, u32[]{:S(2)}, u32[]{:S(2)}) async-start(bf16[4,3,8,8,512]{4,3,2,1,0:T(8,128)(2,1)} %param.63), calls=%async_computation.1 | async-start | bytes 1572864 | tf_op jit(solution)/shard_map/all_to_all | solution.py:249
  167.6 460.8 %all-gather.45.cloned.1.call-start = ((), (), s32[]{:S(2)}) async-start(), calls=%async_computation.34 | async-start | bytes 2621440 | tf_op jit(solution)/shard_map/all_gather | solution.py:180
  201.0 841.9 %reduce-scatter.61.cloned.1.call-start = ((), (), s32[]{:S(2)}) async-start(), calls=%async_computation.48 | async-start | bytes 655360 | tf_op jit(solution)/shard_map/reduce_scatter | solution.py:184
  784.7 259.9 %reduce-scatter.47.cloned.1.call-start = ((), (), s32[]{:S(2)}) async-start(), calls=%async_computation.41 | async-start | bytes 655360 | tf_op jit(solution)/shard_map/reduce_scatter | solution.py:184
  821.6 224.8 %reduce-scatter.63.cloned.1.call-start = ((), (), s32[]{:S(2)}) async-start(), calls=%async_computation.49 | async-start | bytes 655360 | tf_op jit(solution)/shard_map/reduce_scatter | solution.py:184
  1009.0 226.7 %reduce-scatter.69.cloned.1.call-start = ((), (), s32[]{:S(2)}) async-start(), calls=%async_computation.52 | async-start | bytes 5898240
  1041.1 284.4 %all-reduce.42.cloned.1.call-start = ((), (), s32[]{:S(2)}) async-start(), calls=%async_computation.57 | async-start | bytes 165888
  1042.8 361.1 %reduce-scatter.77.cloned.1.call-start = ((), (), s32[]{:S(2)}) async-start(), calls=%async_computation.56 | async-start | bytes 147456
  1044.6 360.9 %reduce-scatter.71.cloned.1.call-start = ((), (), s32[]{:S(2)}) async-start(), calls=%async_computation.53 | async-start | bytes 147456
  1046.4 420.5 %reduce-scatter.65.cloned.1.call-start = ((), (), s32[]{:S(2)}) async-start(), calls=%async_computation.50 | async-start | bytes 147456 | tf_op jit(solution)/shard_map/reduce_scatter | solution.py:187
  1047.1 482.8 %reduce-scatter.51.cloned.1.call-start = ((), (), s32[]{:S(2)}) async-start(), calls=%async_computation.43 | async-start | bytes 147456 | tf_op jit(solution)/shard_map/reduce_scatter | solution.py:187
  1047.7 546.3 %reduce-scatter.35.cloned.1.call-start = ((), (), s32[]{:S(2)}) async-start(), calls=%async_computation.35 | async-start | bytes 294912 | tf_op jit(solution)/shard_map/reduce_scatter | solution.py:187
  1049.6 609.3 %reduce-scatter.59.cloned.1.call-start = ((), (), s32[]{:S(2)}) async-start(), calls=%async_computation.47 | async-start | bytes 589824 | tf_op jit(solution)/shard_map/reduce_scatter | solution.py:187
  1050.4 673.6 %reduce-scatter.41.cloned.1.call-start = ((), (), s32[]{:S(2)}) async-start(), calls=%async_computation.38 | async-start | bytes 589824 | tf_op jit(solution)/shard_map/reduce_scatter | solution.py:187
  1053.8 734.4 %reduce-scatter.53.cloned.1.call-start = ((), (), s32[]{:S(2)}) async-start(), calls=%async_computation.44 | async-start | bytes 589824 | tf_op jit(solution)/shard_map/reduce_scatter | solution.py:187
  1089.9 764.6 %reduce-scatter.45.cloned.1.call-start = ((), (), s32[]{:S(2)}) async-start(), calls=%async_computation.40 | async-start | bytes 1179648 | tf_op jit(solution)/shard_map/reduce_scatter | solution.py:187
  1134.9 786.6 %reduce-scatter.55.cloned.1.call-start = ((), (), s32[]{:S(2)}) async-start(), calls=%async_computation.45 | async-start | bytes 1327104 | tf_op jit(solution)/shard_map/reduce_scatter | solution.py:187
  1190.2 798.2 %reduce-scatter.37.cloned.1.call-start = ((), (), s32[]{:S(2)}) async-start(), calls=%async_computation.36 | async-start | bytes 1327104 | tf_op jit(solution)/shard_map/reduce_scatter | solution.py:187
  (172 other events, 7013.1 us)
Sparse Core Ops, SparseCore 0:
  10.2 43.3 all-gather.34
  55.8 39.8 all-gather.28
  97.8 43.5 all-gather.40
  159.8 42.8 all-gather.36
  204.2 36.9 all-gather.30
  294.2 40.8 all-gather.42
  987.9 31.4 reduce-scatter.56
  1022.3 31.4 reduce-scatter.38
  1056.3 31.4 reduce-scatter.72
  1090.3 44.5 reduce-scatter.42
  1137.4 47.8 reduce-scatter.74
  1187.9 47.8 reduce-scatter.68
  1241.6 32.1 all-reduce.41
  1277.7 62.2 reduce-scatter.76
  1343.8 59.8 reduce-scatter.70
  1407.0 59.8 reduce-scatter.64
  1470.1 59.8 reduce-scatter.50
  1533.7 60.2 reduce-scatter.34
  1597.4 61.4 reduce-scatter.58
  1662.6 61.3 reduce-scatter.40
  1727.2 60.9 reduce-scatter.52
  1792.0 62.4 reduce-scatter.44
  1857.9 63.6 reduce-scatter.54
  1924.8 63.5 reduce-scatter.36
  (9 shorter events, 184.7 us)

commit v2 on v1

--- a/solution.py
+++ b/solution.py
@@ -1,10 +1,1053 @@
+import functools
+
 import jax
 import jax.numpy as jnp
 from jax import lax
+from jax.experimental import pallas as pl
+from jax.experimental.pallas import tpu as pltpu
 from jax.sharding import PartitionSpec as P
 
 eps_norm = 1e-05
 highest = lax.Precision.HIGHEST
+BF = jnp.bfloat16
+F32 = jnp.float32
+MESH = pl.DeviceIdType.MESH
+
+TENSORS = {
+    "E": (128, 512, 1, "E"),
+    "P": (128, 2048, 1, "P"),
+    "S": (576, 512, 1, "S"),
+    "X": (512, 256, 0, "X"),
+    "A": (32, 2048, 1, "A"),
+    "R": (256, 512, 1, "R"),
+    "T": (576, 512, 1, "S"),
+    "V": (512, 256, 0, "X"),
+    "B": (32, 2048, 1, "A"),
+}
+NAMES = list(TENSORS)
+INDEX = {n: i for i, n in enumerate(NAMES)}
+CLASSES = {"E": (128, 128), "P": (128, 512), "S": (576, 128), "X": (128, 256), "A": (32, 512), "R": (256, 128)}
+Q = 192
+VMEM_LIMIT = 64 * 2**20
+WIDE = 2048
+EXCHANGES = {
+    "entry": (4, 512), "stride": (2, 512), "xp": (4, 2048), "reduce": (2, 512), "spatial": (2, 512), "widen": (2, 2048),
+    "widen_b": (4, 2048), "spatial_b": (2, 512), "reduce_b": (2, 512), "xp_b": (4, 2048), "bias_b": (2, 2048),
+    "stride_b": (2, 512), "entry_b": (2, 512),
+}
+EX = {n: i for i, n in enumerate(EXCHANGES)}
+ROW = {"entry": 0, "stride": 2, "reduce": 4, "spatial": 6, "expand": 8, "project": 16, "widen": 24, "excite": 32, "gating": 36,
+       "squeeze": 40, "shrink": 41}
+SMALL = 48
+NORM512 = {"entry": 0, "stride": 1, "reduce": 2, "spatial": 3}
+NORM2048 = {"expand": 0, "project": 1, "widen": 2}
+
+
+def sigmoid(v):
+    return 0.5 + 0.5 * jnp.tanh(0.5 * v)
+
+
+def dot(a, b):
+    return jnp.dot(a, b, preferred_element_type=F32)
+
+
+def dot_cols(a, b):
+    return lax.dot_general(a, b, (((1,), (1,)), ((), ())), preferred_element_type=F32)
+
+
+def dot_rows(a, b):
+    return lax.dot_general(a, b, (((0,), (0,)), ((), ())), preferred_element_type=F32)
+
+
+def halves(v):
+    high = v.astype(BF)
+    return high, (v - high.astype(F32)).astype(BF)
+
+
+def exact(fn, v, w):
+    high, low = halves(v)
+    return fn(high, w) + fn(low, w)
+
+
+def outer(a, b):
+    ah, al = halves(a)
+    bh, bl = halves(b)
+    af, alf, bf, blf = ah.astype(F32), al.astype(F32), bh.astype(F32), bl.astype(F32)
+    left = jnp.concatenate([af, af, alf, jnp.zeros_like(af)], axis=0).astype(BF)
+    right = jnp.concatenate([bf, blf, bf, jnp.zeros_like(bf)], axis=0).astype(BF)
+    return dot_rows(left, right)
+
+
+def lanes(v, times):
+    return jnp.concatenate([v] * times, axis=1) if times > 1 else v
+
+
+def scratch_list():
+    s = {}
+    for n, (r, c, _, _) in TENSORS.items():
+        s["W" + n] = pltpu.VMEM((4, 2, r, c), BF)
+    for k, (r, c) in CLASSES.items():
+        s["RC" + k] = pltpu.VMEM((2, 4, 2, r, c), BF)
+        s["R1" + k] = pltpu.VMEM((2, 2, r, c), BF)
+        s["R2" + k] = pltpu.VMEM((2, 4, r, c), BF)
+        s["RZ" + k] = pltpu.VMEM((3, r, c), BF)
+    for n, (r, c) in EXCHANGES.items():
+        s["X_" + n] = pltpu.VMEM((8, r, c), F32)
+    s["picT"] = pltpu.VMEM((768, 1024), BF)
+    s["stage"] = pltpu.VMEM((768, 1024), BF)
+    s["taps1"] = pltpu.VMEM((Q, 4608), BF)
+    s["taps2"] = pltpu.VMEM((Q, 4608), BF)
+    s["act_e"] = pltpu.VMEM((Q, WIDE), BF)
+    s["act_s"] = pltpu.VMEM((Q, 512), BF)
+    s["act_p"] = pltpu.VMEM((Q, 512), BF)
+    s["first"] = pltpu.VMEM((Q, WIDE), BF)
+    s["cotb"] = pltpu.VMEM((Q, WIDE), BF)
+    s["g1"] = pltpu.VMEM((Q, WIDE), BF)
+    s["g2"] = pltpu.VMEM((Q, WIDE), BF)
+    s["gs"] = pltpu.VMEM((Q, 512), BF)
+    s["shift"] = pltpu.VMEM((9, Q, Q), BF)
+    s["perm"] = pltpu.VMEM((256, 256), BF)
+    for n in ("e_raw", "x_raw", "j_raw", "w_raw", "sg"):
+        s[n] = pltpu.VMEM((Q, WIDE), F32)
+    for n in ("s_raw", "r_raw", "p_raw", "gq", "acc"):
+        s[n] = pltpu.VMEM((Q, 512), F32)
+    s["sgrad"] = pltpu.VMEM((Q, 1024), F32)
+    s["insm"] = pltpu.VMEM((768, 128), F32)
+    s["redm"] = pltpu.VMEM((Q, 128), F32)
+    s["pix"] = pltpu.VMEM((8, 128), F32)
+    s["cnt"] = pltpu.VMEM((8, 512), F32)
+    s["gv5"] = pltpu.VMEM((8, 512), F32)
+    s["gv20"] = pltpu.VMEM((8, WIDE), F32)
+    s["nv5"] = pltpu.VMEM((4, 8, 512), F32)
+    s["nv20"] = pltpu.VMEM((3, 8, WIDE), F32)
+    for n in ("isum1", "isum2", "pool1", "pool2", "scale1", "scale2", "pg", "G0", "G1", "gate"):
+        s[n] = pltpu.VMEM((8, WIDE), F32)
+    for n in ("inner1", "inner2", "ing"):
+        s[n] = pltpu.VMEM((8, 128), F32)
+    s["PR"] = pltpu.VMEM((4, SMALL, 128), F32)
+    s["FS"] = pltpu.VMEM((4, SMALL, 128), F32)
+    s["FR"] = pltpu.VMEM((4, SMALL, 128), F32)
+    dma = pltpu.SemaphoreType.DMA
+    s["ag_s"] = dma((9, 9))
+    s["ag_r"] = dma((9, 9))
+    s["loc"] = dma((16,))
+    s["rs_s"] = dma((9, 9))
+    s["rs_r"] = dma((9, 9))
+    s["st_s"] = dma((13, 7))
+    s["st_r"] = dma((13, 8))
+    s["mp_s"] = dma((5, 4))
+    s["mp_r"] = dma((5, 4))
+    s["free"] = pltpu.SemaphoreType.REGULAR((3,))
+    return s
+
+
+IN_NAMES = ["images", "sizes", "cot_in", "params"] + ["in" + n for n in NAMES]
+OUT_NAMES = ["result", "igrad"] + ["out" + n for n in NAMES] + ["small"]
+
+
+def body(*refs):
+    names = IN_NAMES + OUT_NAMES + list(scratch_list())
+    g = dict(zip(names, refs))
+
+    class NS:
+        def __getattr__(self, k):
+            return g[k]
+
+    s = NS()
+    d = lax.axis_index("dp")
+    m = lax.axis_index("mp")
+    z, y = d // 2, lax.rem(d, 2)
+    x, c = m // 2, lax.rem(m, 2)
+    mx = (1 - x) * 2 + c
+    mc = x * 2 + (1 - c)
+    whole = slice(None)
+    xdev, ydev, cdev = (d, mx), (z * 2 + (1 - y), m), (d, mc)
+
+    def zdev(k):
+        return (lax.rem(z + k, 4) * 2 + y, m)
+
+    def mdev(k):
+        return (d, lax.rem(m + k, 4))
+
+    def col(j, w):
+        return pl.ds(pl.multiple_of(j * w, w), w)
+
+    def rcopy(src, dst, ss, rs, dev):
+        return pltpu.make_async_remote_copy(
+            src_ref=src, dst_ref=dst, send_sem=ss, recv_sem=rs, device_id=dev, device_id_type=MESH
+        )
+
+    partners = [(lax.rem(z + k // 2, 4) * 2 + lax.rem(y + k % 2, 2), m) for k in range(1, 8)]
+    partners += [mdev(k) for k in range(1, 4)]
+    barrier = pltpu.get_barrier_semaphore()
+    for dev in partners:
+        pl.semaphore_signal(barrier, inc=1, device_id=dev, device_id_type=MESH)
+    pl.semaphore_wait(barrier, len(partners))
+
+    def part(n, zs, ys, mi):
+        rows, columns, dim, _ = TENSORS[n]
+        if dim == 1:
+            return g["W" + n].at[zs, ys, :, col(mi, columns // 4)]
+        return g["W" + n].at[zs, ys, col(mi, rows // 4), :]
+
+    def ag(n, slot, region, dev, src=None):
+        i = INDEX[n]
+        return rcopy(region if src is None else src, region, s.ag_s.at[i, slot], s.ag_r.at[i, slot], dev)
+
+    def ag_z(n):
+        own = part(n, z, y, m)
+        pltpu.make_async_copy(g["in" + n], own, s.loc.at[INDEX[n]]).start()
+        for k in range(1, 4):
+            ag(n, k - 1, own, zdev(k), g["in" + n]).start()
+
+    def ag_1(n):
+        pltpu.make_async_copy(g["in" + n], part(n, z, y, m), s.loc.at[INDEX[n]]).wait()
+        for k in range(1, 4):
+            ag(n, k - 1, part(n, lax.rem(z + 4 - k, 4), y, m), zdev(k)).wait_recv()
+        ag(n, 3, part(n, whole, y, m), xdev).start()
+        ag(n, 4, part(n, whole, y, m), ydev).start()
+
+    def ag_2(n):
+        ag(n, 3, part(n, whole, y, mx), xdev).wait_recv()
+        ag(n, 4, part(n, whole, 1 - y, m), ydev).wait_recv()
+        ag(n, 5, part(n, pl.ds(0, 2), y, mx), ydev).start()
+        ag(n, 6, part(n, pl.ds(2, 2), 1 - y, m), xdev).start()
+
+    def ag_c(n):
+        ag(n, 5, part(n, pl.ds(0, 2), 1 - y, mx), ydev).wait_recv()
+        ag(n, 6, part(n, pl.ds(2, 2), 1 - y, mx), xdev).wait_recv()
+        for xx in range(2):
+            ag(n, 7 + xx, part(n, whole, whole, xx * 2 + c), cdev).start()
+
+    def ag_done(n):
+        for xx in range(2):
+            ag(n, 7 + xx, part(n, whole, whole, xx * 2 + (1 - c)), cdev).wait_recv()
+
+    def ag_drain(n):
+        own = part(n, z, y, m)
+        for k in range(1, 4):
+            ag(n, k - 1, own, zdev(k), g["in" + n]).wait_send()
+        ag(n, 3, part(n, whole, y, m), xdev).wait_send()
+        ag(n, 4, part(n, whole, y, m), ydev).wait_send()
+        ag(n, 5, part(n, pl.ds(0, 2), y, mx), ydev).wait_send()
+        ag(n, 6, part(n, pl.ds(2, 2), 1 - y, m), xdev).wait_send()
+        for xx in range(2):
+            ag(n, 7 + xx, part(n, whole, whole, xx * 2 + c), cdev).wait_send()
+
+    ticks = {"k": 0}
+
+    def tick():
+        k = ticks["k"]
+        ticks["k"] = k + 1
+        if 0 <= k - 2 < 9:
+            ag_c(NAMES[k - 2])
+        if 0 <= k - 1 < 9:
+            ag_2(NAMES[k - 1])
+        if k < 9:
+            ag_1(NAMES[k])
+        if k + 2 < 9:
+            ag_z(NAMES[k + 2])
+
+    def loop(count, fn, unroll=1):
+        def step(j, carry):
+            fn(j)
+            return carry
+
+        lax.fori_loop(0, count, step, 0, unroll=unroll)
+
+    def rs(n, slot, region, landing, dev):
+        i = INDEX[n]
+        return rcopy(region, landing, s.rs_s.at[i, slot], s.rs_r.at[i, slot], dev)
+
+    credits = {"T": 0, "V": 1, "B": 2}
+    takes = {"S": 0, "X": 1, "A": 2}
+
+    def rs_partners():
+        return [xdev, ydev, cdev] + [zdev(k) for k in range(1, 4)]
+
+    def rs_copies(n):
+        k = TENSORS[n][3]
+        rc, r1, r2, rz = g["RC" + k], g["R1" + k], g["R2" + k], g["RZ" + k]
+        out = {"c": [rs(n, xx, part(n, whole, whole, xx * 2 + (1 - c)), rc.at[xx], cdev) for xx in range(2)]}
+        out["1"] = [
+            rs(n, 2, part(n, pl.ds(0, 2), 1 - y, mx), r1.at[0], xdev),
+            rs(n, 3, part(n, pl.ds(2, 2), 1 - y, mx), r1.at[1], ydev),
+        ]
+        out["2"] = [
+            rs(n, 4, part(n, whole, y, mx), r2.at[0], xdev),
+            rs(n, 5, part(n, whole, 1 - y, m), r2.at[1], ydev),
+        ]
+        out["z"] = [rs(n, 5 + k, part(n, lax.rem(z + k, 4), y, m), rz.at[k - 1], zdev(k)) for k in range(1, 4)]
+        return out, rc, r1, r2, rz
+
+    def bump(region, extra):
+        region[...] = region[...] + extra
+
+    def reduce_scatter(n):
+        cp, rc, r1, r2, rz = rs_copies(n)
+        if n in takes:
+            pl.semaphore_wait(s.free.at[takes[n]], 6)
+        for t in cp["c"]:
+            t.start()
+        yield
+        for t in cp["c"]:
+            t.wait_recv()
+
+        def add_c(j):
+            zz, yy = j // 2, lax.rem(j, 2)
+            for xx in range(2):
+                bump(part(n, zz, yy, xx * 2 + c), rc[xx, zz, yy])
+
+        loop(8, add_c)
+        for t in cp["1"]:
+            t.start()
+        yield
+        for t in cp["1"]:
+            t.wait_recv()
+        for h in range(2):
+            bump(part(n, h, 1 - y, m), r1[0, h])
+            bump(part(n, 2 + h, y, mx), r1[1, h])
+        for t in cp["2"]:
+            t.start()
+        yield
+        for t in cp["2"]:
+            t.wait_recv()
+
+        def add_2(zz):
+            bump(part(n, zz, y, m), (r2[0, zz].astype(F32) + r2[1, zz].astype(F32)).astype(BF))
+
+        loop(4, add_2)
+        for t in cp["z"]:
+            t.start()
+        yield
+        for t in cp["z"]:
+            t.wait_recv()
+        total = part(n, z, y, m)[...].astype(F32)
+        for k in range(3):
+            total = total + rz[k].astype(F32)
+        g["out" + n][...] = total
+        if n in credits:
+            for dev in rs_partners():
+                pl.semaphore_signal(s.free.at[credits[n]], inc=1, device_id=dev, device_id_type=MESH)
+        for stage in cp.values():
+            for t in stage:
+                t.wait_send()
+
+    active = []
+
+    def pump():
+        for gen in list(active):
+            try:
+                next(gen)
+            except StopIteration:
+                active.remove(gen)
+
+    def begin(n):
+        gen = reduce_scatter(n)
+        active.append(gen)
+        next(gen)
+
+    def st_peers():
+        return [lax.rem(z + k // 2, 4) * 2 + lax.rem(y + k % 2, 2) for k in range(1, 8)]
+
+    def send_stats(e):
+        buf, i = g["X_" + e], EX[e]
+        for k, dd in enumerate(st_peers()):
+            rcopy(buf.at[d], buf.at[d], s.st_s.at[i, k], s.st_r.at[i, d], (dd, m)).start()
+
+    def get_stats(e):
+        buf, i = g["X_" + e], EX[e]
+        for k, dd in enumerate(st_peers()):
+            rcopy(buf.at[dd], buf.at[dd], s.st_s.at[i, k], s.st_r.at[i, dd], (dd, m)).wait_recv()
+        for k, dd in enumerate(st_peers()):
+            rcopy(buf.at[d], buf.at[d], s.st_s.at[i, k], s.st_r.at[i, d], (dd, m)).wait_send()
+        total = buf[0]
+        for k in range(1, 8):
+            total = total + buf[k]
+        return total
+
+    def mp_copies(i, src, dst):
+        return [rcopy(src(lax.rem(m + k, 4)), dst(m), s.mp_s.at[i, k], s.mp_r.at[i, k], mdev(k)) for k in range(1, 4)]
+
+    def mp_wait(i, src, dst, recv=True, send=True):
+        for k in range(1, 4):
+            if recv:
+                rcopy(src(m), dst(lax.rem(m + 4 - k, 4)), s.mp_s.at[i, k], s.mp_r.at[i, k], mdev(k)).wait_recv()
+            if send:
+                rcopy(src(lax.rem(m + k, 4)), dst(m), s.mp_s.at[i, k], s.mp_r.at[i, k], mdev(k)).wait_send()
+
+    cot_src, cot_dst = (lambda j: s.cot_in.at[j]), (lambda j: s.cotb.at[:, col(j, 512)])
+    par_src, par_dst = (lambda j: s.params), (lambda j: s.PR.at[j])
+    res_src, res_dst = (lambda j: s.g2.at[:, col(j, 512)]), (lambda j: s.result.at[j])
+    img_src, img_dst = (lambda j: s.stage.at[:, col(j, 256)]), (lambda j: s.igrad.at[j])
+    fin_src, fin_dst = (lambda j: s.FS.at[j]), (lambda j: s.FR.at[j])
+
+    ag_z("E")
+    for t in mp_copies(1, par_src, par_dst):
+        t.start()
+    own_pic = pltpu.make_async_copy(s.images.at[m], s.stage, s.loc.at[9])
+    own_pic.start()
+    ag_z("P")
+    s.PR[m] = s.params[...]
+
+    r64 = lax.broadcasted_iota(jnp.int32, (64, 128), 0)
+    p64, q64 = r64 >> 3, r64 & 7
+    s.pix[...] = jnp.ones((8, 128), F32)
+    for i in range(3):
+        high, wide = s.sizes[m, i, 0], s.sizes[m, i, 1]
+        for pa in range(2):
+            for pb in range(2):
+                ok = (2 * p64 + pa < high) & (2 * q64 + pb < wide)
+                s.insm[(pa * 2 + pb) * Q + i * 64 : (pa * 2 + pb) * Q + i * 64 + 64, :] = jnp.where(ok, 1.0, 0.0).astype(F32)
+        ok = (2 * p64 < high) & (2 * q64 < wide)
+        mask = jnp.where(ok, 1.0, 0.0).astype(F32)
+        s.redm[i * 64 : i * 64 + 64, :] = mask
+        s.pix[i : i + 1, :] = jnp.sum(mask, axis=0, keepdims=True)
+    r8 = lax.broadcasted_iota(jnp.int32, (8, 128), 0)
+    real = jnp.where(r8 < 3, 1.0, 0.0).astype(F32)
+
+    rr = lax.broadcasted_iota(jnp.int32, (Q, Q), 0)
+    cc = lax.broadcasted_iota(jnp.int32, (Q, Q), 1)
+    pp, qq = (rr >> 3) & 7, rr & 7
+    for t in range(9):
+        da, db = t // 3 - 1, t % 3 - 1
+        ok = (cc == rr + (da * 8 + db)) & (qq + db >= 0) & (qq + db < 8) & (pp + da >= 0) & (pp + da < 8)
+        s.shift[t] = jnp.where(ok, 1.0, 0.0).astype(BF)
+    rp = lax.broadcasted_iota(jnp.int32, (256, 256), 0)
+    cp_ = lax.broadcasted_iota(jnp.int32, (256, 256), 1)
+    source = ((rp >> 3) & 7) * 32 + (rp >> 7) * 16 + (rp & 7) * 2 + ((rp >> 6) & 1)
+    s.perm[...] = jnp.where(cp_ == source, 1.0, 0.0).astype(BF)
+
+    own_pic.wait()
+    for i in range(3):
+        def permute(j, i=i):
+            v = dot(s.perm[...], s.stage[i * 256 : (i + 1) * 256, col(j, 256)]).astype(BF)
+            for pl_ in range(4):
+                s.picT[pl_ * Q + i * 64 : pl_ * Q + i * 64 + 64, col(j, 256)] = v[pl_ * 64 : pl_ * 64 + 64]
+
+        loop(4, permute)
+
+    tick()
+    tick()
+    mp_wait(1, par_src, par_dst)
+    for n, r in ROW.items():
+        if n in NORM512:
+            for k in range(2):
+                row = NORM512[n] * 2 + k
+                for j in range(4):
+                    s.gv5[row : row + 1, j * 128 : j * 128 + 128] = s.PR[j, r + k : r + k + 1, :]
+        elif n in NORM2048 or n in ("excite", "gating"):
+            first_row = NORM2048[n] * 2 if n in NORM2048 else (6 if n == "excite" else 7)
+            for k in range(2 if n in NORM2048 else 1):
+                for j in range(4):
+                    for h in range(4):
+                        b = (j * 4 + h) * 128
+                        s.gv20[first_row + k : first_row + k + 1, b : b + 128] = s.PR[j, r + k * 4 + h : r + k * 4 + h + 1, :]
+    tick()
+
+    def put(e, row, columns, value):
+        g["X_" + e][d, row : row + 1, columns] = value
+
+    def colsum(v):
+        return jnp.sum(v, axis=0, keepdims=True)
+
+    def norm_vectors(nv, index, total, square, count, gv, grow):
+        mean = total / count
+        rstd = lax.rsqrt(square / count - mean * mean + eps_norm)
+        a = gv[grow : grow + 1, :] * rstd
+        nv[index, 0:1, :] = a
+        nv[index, 1:2, :] = gv[grow + 1 : grow + 2, :] - mean * a
+        nv[index, 2:3, :] = mean
+        nv[index, 3:4, :] = rstd
+
+    def norm_back_vectors(nv, index, gain_grad, shift_grad, count):
+        a, mean, rstd = nv[index, 0:1, :], nv[index, 2:3, :], nv[index, 3:4, :]
+        w = a * rstd * gain_grad / count
+        nv[index, 4:5, :] = a * shift_grad / count - mean * w
+        nv[index, 5:6, :] = w
+
+    def activate(raw, index, out):
+        for j in range(4):
+            b = slice(j * 128, j * 128 + 128)
+            pre = raw[:, b] * s.nv5[index, 0:1, b] + s.nv5[index, 1:2, b]
+            out[:, b] = (pre * sigmoid(pre) * s.redm[...]).astype(BF)
+
+    def sums_512(e, columns, value, mask, row=0):
+        vm = value * mask
+        put(e, row, columns, colsum(vm))
+        put(e, row + 1, columns, colsum(vm * value))
+
+    def sums_wide(e, columns, value, isum, row):
+        total = 0.0
+        square = 0.0
+        for i in range(3):
+            v = value[i * 64 : i * 64 + 64]
+            vm = v * lanes(s.redm[i * 64 : i * 64 + 64, :], v.shape[1] // 128)
+            si = colsum(vm)
+            if isum is not None:
+                isum[i : i + 1, columns] = si
+            total = total + si
+            square = square + colsum(vm * v)
+        put(e, row, columns, total)
+        put(e, row + 1, columns, square)
+
+    tick()
+    ag_done("E")
+
+    def entry_step(n):
+        b = col(n, 256)
+        v = dot(s.picT[...], s.WE[:, :, :, b].reshape(1024, 256))
+        total = 0.0
+        square = 0.0
+        for k in range(4):
+            vk = v[k * Q : k * Q + Q]
+            s.e_raw[:, pl.ds(pl.multiple_of(k * 512 + n * 256, 256), 256)] = vk
+            vm = vk * lanes(s.insm[k * Q : k * Q + Q, :], 2)
+            total = total + colsum(vm)
+            square = square + colsum(vm * vk)
+        put("entry", 0, b, total)
+        put("entry", 1, b, square)
+
+    loop(2, entry_step)
+    put("entry", 2, slice(0, 512), lanes(colsum(s.insm[...]), 4))
+    put("entry", 3, slice(0, 512), lanes(colsum(s.redm[...]), 4))
+    send_stats("entry")
+
+    tick()
+    ag_done("P")
+
+    def project_step(n):
+        b = col(n, 256)
+        v = dot(s.picT[0:Q, :], s.WP[:, :, :, b].reshape(1024, 256))
+        s.j_raw[:, b] = v
+        sums_wide("xp", b, v, None, 2)
+
+    loop(8, project_step)
+    tot = get_stats("entry")
+    s.cnt[0:2, :] = tot[2:4]
+    norm_vectors(s.nv5, 0, tot[0:1], tot[1:2], tot[2:3], s.gv5, 0)
+
+    def entry_act_step(j):
+        pcol = col(lax.rem(j, 4), 128)
+        mask = s.insm[pl.ds(pl.multiple_of((j // 4) * Q, Q), Q), :]
+        pre = s.e_raw[:, col(j, 128)] * s.nv5[0, 0:1, pcol] + s.nv5[0, 1:2, pcol]
+        s.act_e[:, col(j, 128)] = (pre * sigmoid(pre) * mask).astype(BF)
+
+    loop(16, entry_act_step, 2)
+    for a in range(3):
+        for b in range(3):
+            t = a * 3 + b
+            plane = (2 if a != 1 else 0) + (1 if b != 1 else 0)
+            which = (0 if a == 0 else 1) * 3 + (0 if b == 0 else 1)
+            v = s.act_e[:, plane * 512 : plane * 512 + 512]
+            if which != 4:
+                v = dot(s.shift[which], v).astype(BF)
+            s.taps1[:, t * 512 : t * 512 + 512] = v
+
+    def conv3(taps, w, raw, e):
+        def step(n):
+            b = col(n, 256)
+            v = dot(taps[:, 0:512], w[:, :, 0:64, b].reshape(512, 256))
+            for t in range(1, 9):
+                v = v + dot(taps[:, t * 512 : t * 512 + 512], w[:, :, t * 64 : t * 64 + 64, b].reshape(512, 256))
+            raw[:, b] = v
+            sums_512(e, b, v, lanes(s.redm[...], 2))
+
+        loop(2, step)
+
+    tick()
+    ag_done("S")
+    conv3(s.taps1, s.WS, s.s_raw, "stride")
+    send_stats("stride")
+    for t in mp_copies(0, cot_src, cot_dst):
+        t.start()
+    own_cot = pltpu.make_async_copy(cot_src(m), cot_dst(m), s.loc.at[10])
+    own_cot.start()
+    tick()
+    ag_done("X")
+    tot = get_stats("stride")
+    count5 = s.cnt[1:2, :]
+    norm_vectors(s.nv5, 1, tot[0:1], tot[1:2], count5, s.gv5, 2)
+    activate(s.s_raw, 1, s.act_s)
+
+    for n in ("isum1", "isum2", "G0", "G1"):
+        g[n][...] = jnp.zeros((8, WIDE), F32)
+
+    def widening(act, w, raw, e, isum):
+        def step(k):
+            b = col(k, 256)
+            v = dot(act[...], w[k // 2, lax.rem(k, 2)])
+            raw[:, b] = v
+            sums_wide(e, b, v, isum, 0)
+
+        loop(8, step)
+
+    widening(s.act_s, s.WX, s.x_raw, "xp", s.isum1)
+    send_stats("xp")
+    tick()
+    ag_done("A")
+    count20 = lanes(s.cnt[1:2, :], 4)
+    tot = get_stats("xp")
+    norm_vectors(s.nv20, 0, tot[0:1], tot[1:2], count20, s.gv20, 0)
+    norm_vectors(s.nv20, 1, tot[2:3], tot[3:4], count20, s.gv20, 2)
+
+    def squeeze_excite(index, isum, w, bias, gate_row, pool, inner, scale):
+        pooled = (s.nv20[index, 0:1, :] * isum[...] / lanes(s.pix[...], 16) + s.nv20[index, 1:2, :]) * lanes(real, 16)
+        pool[...] = pooled
+        pre = exact(dot_cols, pooled, w[:, :, 0:16, :].reshape(128, WIDE)) + bias
+        inner[...] = pre
+        gate = exact(dot, pre * sigmoid(pre), w[:, :, 16:32, :].reshape(128, WIDE)) + s.gv20[gate_row : gate_row + 1, :]
+        scale[...] = sigmoid(gate)
+
+    squeeze_excite(0, s.isum1, s.WA, s.PR[0, 40:41, :], 6, s.pool1, s.inner1, s.scale1)
+
+    def first_sum(j, i):
+        b, rows = col(j, 128), slice(i * 64, i * 64 + 64)
+        pre = s.x_raw[rows, b] * s.nv20[0, 0:1, b] + s.nv20[0, 1:2, b]
+        return pre * s.scale1[i : i + 1, b] + (s.j_raw[rows, b] * s.nv20[1, 0:1, b] + s.nv20[1, 1:2, b])
+
+    def first_step(j):
+        for i in range(3):
+            rows = slice(i * 64, i * 64 + 64)
+            v = first_sum(j, i)
+            s.first[rows, col(j, 128)] = (v * sigmoid(v) * s.redm[rows, :]).astype(BF)
+
+    loop(16, first_step, 2)
+
+    tick()
+    ag_done("R")
+
+    def reduce_step(n):
+        b = col(n, 256)
+        v = dot(s.first[...], s.WR[:, :, :, b].reshape(WIDE, 256))
+        s.r_raw[:, b] = v
+        sums_512("reduce", b, v, lanes(s.redm[...], 2))
+
+    loop(2, reduce_step)
+    send_stats("reduce")
+    tick()
+    tot = get_stats("reduce")
+    norm_vectors(s.nv5, 2, tot[0:1], tot[1:2], count5, s.gv5, 4)
+    activate(s.r_raw, 2, s.act_p)
+    for t in range(9):
+        v = s.act_p[...]
+        if t != 4:
+            v = dot(s.shift[t], v).astype(BF)
+        s.taps2[:, t * 512 : t * 512 + 512] = v
+    ag_done("T")
+    conv3(s.taps2, s.WT, s.p_raw, "spatial")
+    send_stats("spatial")
+    tick()
+    ag_done("V")
+    tot = get_stats("spatial")
+    norm_vectors(s.nv5, 3, tot[0:1], tot[1:2], count5, s.gv5, 6)
+    activate(s.p_raw, 3, s.act_p)
+    widening(s.act_p, s.WV, s.w_raw, "widen", s.isum2)
+    send_stats("widen")
+    ag_done("B")
+    own_cot.wait()
+    mp_wait(0, cot_src, cot_dst)
+    tot = get_stats("widen")
+    norm_vectors(s.nv20, 2, tot[0:1], tot[1:2], count20, s.gv20, 4)
+    squeeze_excite(2, s.isum2, s.WB, s.PR[0, 41:42, :], 7, s.pool2, s.inner2, s.scale2)
+
+    def result_step(j):
+        b = col(j, 128)
+        for i in range(3):
+            rows = slice(i * 64, i * 64 + 64)
+            raw = s.w_raw[rows, b]
+            pre = raw * s.nv20[2, 0:1, b] + s.nv20[2, 1:2, b]
+            v = pre * s.scale2[i : i + 1, b] + s.first[rows, b].astype(F32)
+            sg = sigmoid(v)
+            mask = s.redm[rows, :]
+            s.g2[rows, b] = (v * sg * mask).astype(BF)
+            grad = s.cotb[rows, b].astype(F32) * mask * (sg * (1.0 + v * (1.0 - sg)))
+            s.sg[rows, b] = grad
+            s.G0[i : i + 1, b] = colsum(grad)
+            s.G1[i : i + 1, b] = colsum(grad * ((raw - s.nv20[2, 2:3, b]) * s.nv20[2, 3:4, b]))
+
+    loop(16, result_step, 2)
+    for t in mp_copies(2, res_src, res_dst):
+        t.start()
+    own_res = pltpu.make_async_copy(res_src(m), res_dst(m), s.loc.at[11])
+    own_res.start()
+
+    def keep512(n, k, v):
+        for j in range(4):
+            s.FS[j, ROW[n] + k : ROW[n] + k + 1, :] = v[:, j * 128 : j * 128 + 128]
+
+    def keep2048(row, v):
+        for j in range(4):
+            for h in range(4):
+                b = (j * 4 + h) * 128
+                s.FS[j, row + h : row + h + 1, :] = v[:, b : b + 128]
+
+    def excite_back(index, isum, w, inner, scale):
+        scl = scale[...]
+        gate_grad = (s.gv20[index * 2 : index * 2 + 1, :] * s.G1[...] + s.gv20[index * 2 + 1 : index * 2 + 2, :] * s.G0[...]) * (
+            scl * (1.0 - scl)
+        )
+        s.gate[...] = gate_grad
+        pre = inner[...]
+        sg = sigmoid(pre)
+        ing = exact(dot_cols, gate_grad, w[:, :, 16:32, :].reshape(128, WIDE)) * (sg * (1.0 + pre * (1.0 - sg)))
+        s.ing[...] = ing
+        pix = lanes(s.pix[...], 16)
+        pg = exact(dot, ing, w[:, :, 0:16, :].reshape(128, WIDE)) / pix
+        s.pg[...] = pg
+        spread = (isum[...] - s.nv20[index, 2:3, :] * pix) * s.nv20[index, 3:4, :]
+        return (colsum(scl * s.G1[...] + pg * spread), colsum(scl * s.G0[...] + pg * pix), colsum(gate_grad), colsum(ing))
+
+    def excite_weights(n, pool, inner):
+        pre = inner[...]
+        hidden = pre * sigmoid(pre)
+        w = g["W" + n]
+
+        def step(j):
+            b = col(j, 512)
+            w[:, :, 0:16, b] = outer(s.ing[...], pool[:, b]).astype(BF).reshape(4, 2, 16, 512)
+            w[:, :, 16:32, b] = outer(hidden, s.gate[:, b]).astype(BF).reshape(4, 2, 16, 512)
+
+        loop(4, step)
+
+    def wide_grad(index, raw, out, scale):
+        def step(j):
+            b = col(j, 128)
+            for i in range(3):
+                rows = slice(i * 64, i * 64 + 64)
+                grad, mask = s.sg[rows, b], s.redm[rows, :]
+                if scale is not None:
+                    grad = grad * scale[i : i + 1, b] + mask * s.pg[i : i + 1, b]
+                v = s.nv20[index, 0:1, b] * grad - mask * (s.nv20[index, 4:5, b] + s.nv20[index, 5:6, b] * raw[rows, b])
+                out[rows, b] = v.astype(BF)
+
+        loop(16, step, 2)
+
+    def back_sums(e, index, b, grad, raw, mask):
+        out = []
+        pre = raw * s.nv5[index, 0:1, b] + s.nv5[index, 1:2, b]
+        sg = sigmoid(pre)
+        grad = grad * mask * (sg * (1.0 + pre * (1.0 - sg)))
+        put(e, 0, b, colsum(grad * ((raw - s.nv5[index, 2:3, b]) * s.nv5[index, 3:4, b])))
+        put(e, 1, b, colsum(grad))
+        return grad
+
+    def narrow_back(e, index, acc, raw):
+        for j in range(4):
+            b = slice(j * 128, j * 128 + 128)
+            s.gq[:, b] = back_sums(e, index, b, acc[:, b], raw[:, b], s.redm[...])
+
+    def narrow_grad(index, raw):
+        for j in range(4):
+            b = slice(j * 128, j * 128 + 128)
+            v = s.nv5[index, 0:1, b] * s.gq[:, b] - s.redm[...] * (s.nv5[index, 4:5, b] + s.nv5[index, 5:6, b] * raw[:, b])
+            s.gs[:, b] = v.astype(BF)
+
+    def narrow_stats(e, n):
+        tot = get_stats(e)
+        keep512(n, 0, tot[0:1])
+        keep512(n, 1, tot[1:2])
+        norm_back_vectors(s.nv5, NORM512[n], tot[0:1], tot[1:2], s.cnt[0:1, :] if n == "entry" else count5)
+
+    def widening_back(grads, w):
+        def step(n):
+            rows = col(n, 256)
+            v = dot_cols(grads[:, 0:256], w[0, 0, rows, :])
+            for k in range(1, 8):
+                v = v + dot_cols(grads[:, k * 256 : k * 256 + 256], w[k // 2, k % 2, rows, :])
+            s.acc[:, rows] = v
+
+        loop(2, step)
+
+    def widening_weights(n, act, grads):
+        ag_drain(n)
+        w = g["W" + n]
+
+        def step(k):
+            w[k // 2, lax.rem(k, 2)] = dot_rows(act[...], grads[:, col(k, 256)]).astype(BF)
+
+        loop(8, step)
+        begin(n)
+
+    def conv3_weights(n, taps):
+        ag_drain(n)
+        w = g["W" + n]
+
+        def step(t):
+            for h in range(2):
+                b = slice(h * 256, h * 256 + 256)
+                v = dot_rows(taps[:, col(t, 512)], s.gs[:, b]).astype(BF)
+                w[:, :, col(t, 64), b] = v.reshape(4, 2, 64, 256)
+
+        loop(9, step)
+        begin(n)
+
+    sums = excite_back(2, s.isum2, s.WB, s.inner2, s.scale2)
+    for k in range(3):
+        put("widen_b", k, slice(0, WIDE), sums[k])
+    put("widen_b", 3, slice(0, WIDE), lanes(sums[3], 16))
+    send_stats("widen_b")
+    ag_drain("B")
+    excite_weights("B", s.pool2, s.inner2)
+    begin("B")
+    tot = get_stats("widen_b")
+    keep2048(ROW["widen"], tot[0:1])
+    keep2048(ROW["widen"] + 4, tot[1:2])
+    keep2048(ROW["gating"], tot[2:3])
+    for j in range(4):
+        s.FS[j, ROW["shrink"] : ROW["shrink"] + 1, :] = tot[3:4, 0:128]
+    norm_back_vectors(s.nv20, 2, tot[0:1], tot[1:2], count20)
+    wide_grad(2, s.w_raw, s.g1, s.scale2)
+    widening_back(s.g1, s.WV)
+    narrow_back("spatial_b", 3, s.acc, s.p_raw)
+    send_stats("spatial_b")
+    pump()
+    widening_weights("V", s.act_p, s.g1)
+    narrow_stats("spatial_b", "spatial")
+    narrow_grad(3, s.p_raw)
+    pump()
+    s.acc[...] = jnp.zeros((Q, 512), F32)
+
+    def spatial_back(t):
+        v = dot(s.shift[8 - t], s.gs[...]).astype(BF)
+        s.acc[...] += dot_cols(v, s.WT[:, :, col(t, 64), :].reshape(512, 512))
+
+    loop(9, spatial_back)
+    narrow_back("reduce_b", 2, s.acc, s.r_raw)
+    send_stats("reduce_b")
+    pump()
+    conv3_weights("T", s.taps2)
+    narrow_stats("reduce_b", "reduce")
+    narrow_grad(2, s.r_raw)
+    pump()
+
+    def reduce_back(k):
+        v = dot_cols(s.gs[...], s.WR[k // 2, lax.rem(k, 2)])
+        for h in range(2):
+            j = k * 2 + h
+            b = col(j, 128)
+            project_sum = 0.0
+            shift_sum = 0.0
+            for i in range(3):
+                rows = slice(i * 64, i * 64 + 64)
+                fs = first_sum(j, i)
+                sg = sigmoid(fs)
+                grad = (v[rows, h * 128 : h * 128 + 128] + s.sg[rows, b]) * s.redm[rows, :] * (sg * (1.0 + fs * (1.0 - sg)))
+                s.sg[rows, b] = grad
+                total = colsum(grad)
+                s.G0[i : i + 1, b] = total
+                s.G1[i : i + 1, b] = colsum(grad * ((s.x_raw[rows, b] - s.nv20[0, 2:3, b]) * s.nv20[0, 3:4, b]))
+                shift_sum = shift_sum + total
+                project_sum = project_sum + colsum(grad * ((s.j_raw[rows, b] - s.nv20[1, 2:3, b]) * s.nv20[1, 3:4, b]))
+            put("xp_b", 2, b, project_sum)
+            put("xp_b", 3, b, shift_sum)
+
+    loop(8, reduce_back)
+    sums = excite_back(0, s.isum1, s.WA, s.inner1, s.scale1)
+    put("xp_b", 0, slice(0, WIDE), sums[0])
+    put("xp_b", 1, slice(0, WIDE), sums[1])
+    send_stats("xp_b")
+    put("bias_b", 0, slice(0, WIDE), sums[2])
+    put("bias_b", 1, slice(0, WIDE), lanes(sums[3], 16))
+    send_stats("bias_b")
+    pump()
+    ag_drain("R")
+
+    def reduce_weights(k):
+        s.WR[k // 2, lax.rem(k, 2)] = dot_rows(s.first[:, col(k, 256)], s.gs[...]).astype(BF)
+
+    loop(8, reduce_weights)
+    begin("R")
+    ag_drain("A")
+    excite_weights("A", s.pool1, s.inner1)
+    begin("A")
+    tot = get_stats("xp_b")
+    for k, n in enumerate(("expand", "project")):
+        keep2048(ROW[n], tot[2 * k : 2 * k + 1])
+        keep2048(ROW[n] + 4, tot[2 * k + 1 : 2 * k + 2])
+        norm_back_vectors(s.nv20, k, tot[2 * k : 2 * k + 1], tot[2 * k + 1 : 2 * k + 2], count20)
+    wide_grad(0, s.x_raw, s.g1, s.scale1)
+    widening_back(s.g1, s.WX)
+    narrow_back("stride_b", 1, s.acc, s.s_raw)
+    send_stats("stride_b")
+    pump()
+    own_res.wait()
+    mp_wait(2, res_src, res_dst)
+    wide_grad(1, s.j_raw, s.g2, None)
+
+    def project_back(zz):
+        w = s.WP[zz].reshape(256, WIDE)
+        s.sgrad[:, col(zz, 256)] = dot_cols(s.g2[...], w)
+
+    loop(4, project_back)
+    widening_weights("X", s.act_s, s.g1)
+    ag_drain("P")
+
+    def project_weights(n):
+        b = col(n, 256)
+        for h in range(2):
+            v = dot_rows(s.picT[0:Q, h * 512 : h * 512 + 512], s.g2[:, b]).astype(BF)
+            s.WP[2 * h : 2 * h + 2, :, :, b] = v.reshape(2, 2, 128, 256)
+
+    loop(8, project_weights)
+    begin("P")
+    narrow_stats("stride_b", "stride")
+    narrow_grad(1, s.s_raw)
+    pump()
+
+    for k in range(4):
+        pa, pb = k // 2, k % 2
+        columns = slice(k * 512, k * 512 + 512)
+        first_tap = True
+        for a in (0, 2) if pa else (1,):
+            for b in (0, 2) if pb else (1,):
+                t = a * 3 + b
+                which = (0 if a == 0 else 1) * 3 + (0 if b == 0 else 1)
+                v = s.gs[...]
+                if which != 4:
+                    v = dot(s.shift[8 - which], v).astype(BF)
+                v = dot_cols(v, s.WS[:, :, t * 64 : t * 64 + 64, :].reshape(512, 512))
+                if first_tap:
+                    s.w_raw[:, columns] = v
+                else:
+                    s.w_raw[:, columns] += v
+                first_tap = False
+
+    def entry_back(n):
+        b = col(n, 128)
+        gain_sum = 0.0
+        shift_sum = 0.0
+        for k in range(4):
+            kb = pl.ds(pl.multiple_of(k * 512 + n * 128, 128), 128)
+            raw = s.e_raw[:, kb]
+            pre = raw * s.nv5[0, 0:1, b] + s.nv5[0, 1:2, b]
+            sg = sigmoid(pre)
+            grad = s.w_raw[:, kb] * s.insm[k * Q : k * Q + Q, :] * (sg * (1.0 + pre * (1.0 - sg)))
+            s.w_raw[:, kb] = grad
+            gain_sum = gain_sum + colsum(grad * ((raw - s.nv5[0, 2:3, b]) * s.nv5[0, 3:4, b]))
+            shift_sum = shift_sum + colsum(grad)
+        put("entry_b", 0, b, gain_sum)
+        put("entry_b", 1, b, shift_sum)
+
+    loop(4, entry_back)
+    send_stats("entry_b")
+    pump()
+    conv3_weights("S", s.taps1)
+    narrow_stats("entry_b", "entry")
+
+    def entry_grad(j):
+        pcol = col(lax.rem(j, 4), 128)
+        mask = s.insm[pl.ds(pl.multiple_of((j // 4) * Q, Q), Q), :]
+        b = col(j, 128)
+        v = s.nv5[0, 0:1, pcol] * s.w_raw[:, b] - mask * (s.nv5[0, 4:5, pcol] + s.nv5[0, 5:6, pcol] * s.e_raw[:, b])
+        s.act_e[:, b] = v.astype(BF)
+
+    loop(16, entry_grad, 2)
+    tot = get_stats("bias_b")
+    keep2048(ROW["excite"], tot[0:1])
+    for j in range(4):
+        s.FS[j, ROW["squeeze"] : ROW["squeeze"] + 1, :] = tot[1:2, 0:128]
+        for r in range(42, SMALL, 2):
+            s.FS[j, r : r + 2, :] = jnp.zeros((2, 128), F32)
+    s.FR[m] = s.FS[m]
+    for t in mp_copies(4, fin_src, fin_dst):
+        t.start()
+
+    def image_grad(zz):
+        w = s.WE[zz].reshape(256, 512)
+        for k in range(4):
+            v = dot_cols(s.act_e[:, k * 512 : k * 512 + 512], w)
+            if k == 0:
+                v = v + s.sgrad[:, col(zz, 256)]
+            s.taps1[:, pl.ds(pl.multiple_of(k * 1024 + zz * 256, 256), 256)] = v.astype(BF)
+
+    loop(4, image_grad)
+    for i in range(3):
+        def unpermute(j, i=i):
+            v = jnp.concatenate(
+                [s.taps1[i * 64 : i * 64 + 64, pl.ds(pl.multiple_of(k * 1024 + j * 256, 256), 256)] for k in range(4)], axis=0
+            )
+            s.stage[i * 256 : i * 256 + 256, col(j, 256)] = dot_rows(s.perm[...], v).astype(BF)
+
+        loop(4, unpermute)
+    for t in mp_copies(3, img_src, img_dst):
+        t.start()
+    own_img = pltpu.make_async_copy(img_src(m), img_dst(m), s.loc.at[12])
+    own_img.start()
+    ag_drain("E")
+
+    def entry_weights(zz):
+        v = dot_rows(s.picT[0:Q, col(zz, 256)], s.act_e[:, 0:512])
+        for k in range(1, 4):
+            v = v + dot_rows(s.picT[k * Q : k * Q + Q, col(zz, 256)], s.act_e[:, k * 512 : k * 512 + 512])
+        s.WE[zz] = v.astype(BF).reshape(2, 128, 512)
+
+    loop(4, entry_weights)
+    begin("E")
+    while active:
+        pump()
+    mp_wait(4, fin_src, fin_dst)
+    s.small[...] = ((s.FR[0] + s.FR[1]) + s.FR[2]) + s.FR[3]
+    own_img.wait()
+    mp_wait(3, img_src, img_dst)
+
+def fused_shards(*arrays):
+    (images, image_size, entry_weight, entry_gain, entry_shift, stride_weight, stride_gain, stride_shift, expand_weight,
+     expand_gain, expand_shift, project_weight, project_gain, project_shift, squeeze_weight, squeeze_bias, excite_weight,
+     excite_bias, reduce_weight, reduce_gain, reduce_shift, spatial_weight, spatial_gain, spatial_shift, widen_weight,
+     widen_gain, widen_shift, shrink_weight, shrink_bias, gating_weight, gating_bias, cotangent) = arrays
+    small = [entry_gain, entry_shift, stride_gain, stride_shift, reduce_gain, reduce_shift, spatial_gain, spatial_shift,
+             expand_gain, expand_shift, project_gain, project_shift, widen_gain, widen_shift, excite_bias, gating_bias,
+             squeeze_bias, shrink_bias]
+    params = jnp.concatenate([v.reshape(-1, 128) for v in small] + [jnp.zeros((SMALL - 42, 128), F32)], axis=0)
+    shards = {
+        "E": entry_weight,
+        "P": project_weight,
+        "S": stride_weight.reshape(576, 128),
+        "X": expand_weight,
+        "A": jnp.concatenate([squeeze_weight.T, excite_weight], axis=0),
+        "R": reduce_weight,
+        "T": spatial_weight.reshape(576, 128),
+        "V": widen_weight,
+        "B": jnp.concatenate([shrink_weight.T, gating_weight], axis=0),
+    }
+    outs = [jax.ShapeDtypeStruct((4, Q, 512), BF), jax.ShapeDtypeStruct((4, 768, 256), BF)]
+    outs += [jax.ShapeDtypeStruct(CLASSES[TENSORS[n][3]], F32) for n in NAMES]
+    outs += [jax.ShapeDtypeStruct((SMALL, 128), F32)]
+    hbm, vmem = pl.BlockSpec(memory_space=pl.ANY), pl.BlockSpec(memory_space=pltpu.VMEM)
+    got = pl.pallas_call(
+        body,
+        out_shape=outs,
+        in_specs=[hbm, pl.BlockSpec(memory_space=pltpu.SMEM), hbm, vmem] + [hbm] * len(NAMES),
+        out_specs=[hbm, hbm] + [vmem] * (len(NAMES) + 1),
+        scratch_shapes=list(scratch_list().values()),
+        compiler_params=pltpu.CompilerParams(
+            collective_id=0, has_side_effects=True, vmem_limit_bytes=VMEM_LIMIT
+        ),
+        cost_estimate=pl.CostEstimate(flops=14_000_000_000, bytes_accessed=30_000_000, transcendentals=10_000_000),
+    )(images.reshape(4, 768, 1024), image_size, cotangent.reshape(4, Q, 512), params, *[shards[n] for n in NAMES])
+    result, igrad, weights, rows = got[0], got[1], dict(zip(NAMES, got[2:-1])), got[-1]
+
+    def vector(first, count):
+        return rows[first : first + count].reshape(-1)
+
+    def pair(n):
+        k = 1 if n in NORM512 else 4
+        return vector(ROW[n], k), vector(ROW[n] + k, k)
+
+    return (
+        result.reshape(cotangent.shape),
+        igrad.reshape(4, 3, 16, 16, 256).astype(F32),
+        weights["E"], *pair("entry"),
+        weights["S"].reshape(stride_weight.shape), *pair("stride"),
+        weights["X"], *pair("expand"),
+        weights["P"], *pair("project"),
+        weights["A"][:16].T, vector(ROW["squeeze"], 1), weights["A"][16:], vector(ROW["excite"], 4),
+        weights["R"], *pair("reduce"),
+        weights["T"].reshape(spatial_weight.shape), *pair("spatial"),
+        weights["V"], *pair("widen"),
+        weights["B"][:16].T, vector(ROW["shrink"], 1), weights["B"][16:], vector(ROW["gating"], 4),
+    )
 
 
 def matmul(left, right):
@@ -189,7 +1232,7 @@
     )
 
 
-def shards(
+def plain_shards(
     images,
     image_size,
     entry_weight,
@@ -533,4 +1576,5 @@
         P("dp", "mp"),
         P("mp"),
     )
+    shards = fused_shards if dict(mesh.shape) == {"dp": 8, "mp": 4} else plain_shards
     return jax.shard_map(shards, mesh=mesh, in_specs=in_specs, out_specs=out_specs, check_vma=False)

time: 2010 us -> 338 us (0.17)
  waiting for transfers between devices: 804 us -> 0 us
  blocking collectives: 668 us -> 0 us
  local copies, waits for them, and re-layouts: 346 us -> 19.2 us
  Pallas kernels: 0 us -> 311 us
  matrix products: 79.5 us -> 0 us
  other arithmetic: 68.5 us -> 6.31 us
    reduce_scatter x16 -> x0, waiting for transfers between devices: 618 us -> none  [the longest x9 570 us: own_part(): lax.psum_scatter(value, 'dp', scatter_dimension=dp_axis, tiled=True)]
    all_gather x28 -> x0, blocking collectives: 381 us -> none  [the longest x8 258 us: whole_matrix(): value = lax.all_gather(value, 'dp', axis=dp_axis, tiled=True)]
    pallas_call x0 -> x1, Pallas kernels: none -> 311 us  [fused_shards(): pl.pallas_call(body, out_shape=outs, in_specs=[hbm, pl.BlockSpec(memory_s...]
    psum x12 -> x0, blocking collectives: 287 us -> none  [the longest x6 145 us: batch_statistics(): lax.psum((jnp.concatenate(terms), jnp.sum(mask).reshape(1)), 'dp')]
    unnamed x383 -> x25, local copies, waits for them, and re-layouts: 188 us -> 7.02 us
    unnamed x40 -> x0, waiting for transfers between devices: 135 us -> none
    dot_general x33 -> x0, matrix products: 79.5 us -> none  [the longest x7 24.1 us: matmul(): return jnp.dot(left, right, preferred_element_type=jnp.float32)]
    slice x25 -> x1, local copies, waits for them, and re-layouts: 53.4 us -> 1.46 us  [fused_shards(): weights['B'][16:]]
  transfers between devices with their start and end apart: 36 -> 0, of which waited for: 16 -> 0; matrix products, arithmetic and copies ran while one was open for 22% -> 0% of each run, Pallas kernels for 0% -> 0%
where the time goes in v2:
time: 338 us; the launch traced here: 337 us
  Pallas kernels  311 us (92%)
  local copies, waits for them, and re-layouts  19.2 us (6%)
  other arithmetic  6.31 us (2%)
    pallas_call x1, Pallas kernels, fused_shards(): pl.pallas_call(body, out_shape=outs, in_specs=[hbm, pl.BlockSpec(memory_s...  311 us
    concatenate x1, local copies, waits for them, and re-layouts, fused_shards(): jnp.concatenate([v.reshape(-1, 128) for v in small] + [jnp.zeros((SMALL -...  7.83 us
    unnamed x25, local copies, waits for them, and re-layouts  7.02 us

profile of v2, /device:TPU:0, one launch (start us, length us, event | category | flops | bytes accessed | tf_op | source)
XLA Modules:
  0.0 337.0 jit_solution(13538205513836906552)
XLA Ops:
  0.7 1.4 copy.63.refs_1_
  2.1 7.8 %concatenate.9.refs_3_ = f32[48,128]{1,0:T(8,128)} concatenate(f32[1,128]{1,0:T(1,128)} %bitcast.83, f32[1,128]{1,0:T(1,128)} %bitcast.84, f32[1,128]{1,0:T(1,128)} %bitcast.85, f32[1,128]{1,0:T(1,128)} %bitcast.86, f32[1,128]{1,0:T(1,128)} %bitcast.87, f32[1,128]{1,0:T(1,128)} %bitcast.88, f32[1,128]{1,0:T(1,128)} %bitcast.89, f32[1,128]{1,0:T(1,128)} %bitcast.90, ...), dimensions={0} | concatenate | bytes 49152 | tf_op jit(solution)/shard_map/concatenate | solution.py:1002
  9.9 1.4 pad_maximum_fusion.refs_8_
  11.2 1.4 pad_maximum_fusion.1.refs_12_
  12.6 310.8 %shard_map.543 = (bf16[4,192,512]{2,1,0:T(8,128)(2,1)}, bf16[4,768,256]{2,1,0:T(8,128)(2,1)}, f32[128,128]{1,0:T(8,128)}, f32[128,512]{1,0:T(8,128)}, f32[576,12...) custom-call(bf16[4,768,1024]{2,1,0:T(8,128)(2,1)} %bitcast.93, ...), custom_call_target="tpu_custom_call" | custom-call | flops 14000000000 | bytes 30000000 | tf_op jit(solution)/shard_map/pallas_call | solution.py:1018
  323.4 0.0 copy-start
  323.4 1.5 slice_bitcast_fusion.10
  324.9 1.4 slice_bitcast_fusion.2
  326.3 1.5 fusion
  327.7 0.0 copy-start.3
  327.7 0.0 copy-start.5
  327.8 0.0 copy-start.1
  327.8 0.0 copy-start.4
  327.8 3.6 %convert.1 = f32[4,3,16,16,256]{4,3,2,1,0:T(8,128)} convert(bf16[4,3,16,16,256]{4,3,2,1,0:T(8,128)(2,1)} %bitcast.69) | non-fusion elementwise | flops 786432 | bytes 4718592 | tf_op jit(solution)/shard_map/convert_element_type | solution.py:1040
  331.4 0.0 copy-done
  331.4 0.9 copy.72
  332.3 0.0 copy-done.7
  332.3 0.6 copy.73
  332.9 0.7 copy.74
  333.6 0.7 copy.75
  334.3 0.7 copy.76
  335.0 0.7 copy.77
  335.6 0.7 copy.78
  336.4 0.7 copy.79
  (10 shorter events, 0.0 us)
Async XLA Ops:
  323.4 8.0 %copy-start = (bf16[4,192,512]{2,1,0:T(8,128)(2,1)S(1)}, bf16[4,192,512]{2,1,0:T(8,128)(2,1)}, u32[]{:S(2)}) copy-start(bf16[4,192,512]{2,1,0:T(8,128)(2,1)} %get-tuple-element.43) | copy-start | bytes 2359300
  327.7 4.5 %copy-start.7 = (f32[128,128]{1,0:T(8,128)S(1)}, f32[128,128]{1,0:T(8,128)}, u32[]{:S(2)}) copy-start(f32[128,128]{1,0:T(8,128)} %get-tuple-element.112) | copy-start | bytes 196612
  327.7 5.2 %copy-start.2 = (f32[576,128]{1,0:T(8,128)S(1)}, f32[576,128]{1,0:T(8,128)}, u32[]{:S(2)}) copy-start(f32[576,128]{1,0:T(8,128)} %get-tuple-element.47) | copy-start | bytes 884740
  327.7 5.9 %copy-start.6 = (f32[128,256]{1,0:T(8,128)S(1)}, f32[128,256]{1,0:T(8,128)}, u32[]{:S(2)}) copy-start(f32[128,256]{1,0:T(8,128)} %get-tuple-element.118) | copy-start | bytes 393220
  327.7 6.5 %copy-start.3 = (f32[128,512]{1,0:T(8,128)S(1)}, f32[128,512]{1,0:T(8,128)}, u32[]{:S(2)}) copy-start(f32[128,512]{1,0:T(8,128)} %get-tuple-element.121) | copy-start | bytes 786436
  327.7 7.2 %copy-start.5 = (f32[256,128]{1,0:T(8,128)S(1)}, f32[256,128]{1,0:T(8,128)}, u32[]{:S(2)}) copy-start(f32[256,128]{1,0:T(8,128)} %get-tuple-element.128) | copy-start | bytes 393220
  327.8 7.9 %copy-start.1 = (f32[576,128]{1,0:T(8,128)S(1)}, f32[576,128]{1,0:T(8,128)}, u32[]{:S(2)}) copy-start(f32[576,128]{1,0:T(8,128)} %get-tuple-element.52) | copy-start | bytes 884740
  327.8 8.6 %copy-start.4 = (f32[128,256]{1,0:T(8,128)S(1)}, f32[128,256]{1,0:T(8,128)}, u32[]{:S(2)}) copy-start(f32[128,256]{1,0:T(8,128)} %get-tuple-element.134) | copy-start | bytes 393220

commit v3 on v2

--- a/solution.py
+++ b/solution.py
@@ -25,7 +25,32 @@
     "B": (32, 2048, 1, "A"),
 }
 NAMES = list(TENSORS)
-INDEX = {n: i for i, n in enumerate(NAMES)}
+PIECES = {
+    "E": [(0, 128)],
+    "P": [(0, 32), (32, 32), (64, 32), (96, 32)],
+    "S": [(0, 128), (128, 128), (256, 128), (384, 192)],
+    "X": [(0, 128), (128, 128)],
+    "A": [(0, 32)],
+    "R": [(0, 128), (128, 128)],
+    "T": [(0, 128), (128, 128), (256, 128), (384, 192)],
+    "V": [(0, 128), (128, 128)],
+    "B": [(0, 32)],
+}
+ORDER = [(n, i) for n in NAMES for i in range(len(PIECES[n]))]
+INDEX = {piece: i for i, piece in enumerate(ORDER)}
+AG_Z_LAST = ()
+RS_Z_LAST = ()
+AG_MORE = {3: (), 4: ()}
+RS_MORE = {3: (), 4: ()}
+ZLAG = 5
+SLOTS = (0, 1, 2, 6, 9, 10)
+LAST = {n: INDEX[n, len(PIECES[n]) - 1] for n in NAMES}
+COUNT = len(ORDER)
+LEAD, LAG, RLAG = 3, 2, 3
+OPT = ()
+TICKS = "bch"
+STARTS = 1
+PUMPS = "ABCDEFGHIJKLMNOPQRSUVWXY"
 CLASSES = {"E": (128, 128), "P": (128, 512), "S": (576, 128), "X": (128, 256), "A": (32, 512), "R": (256, 128)}
 Q = 192
 VMEM_LIMIT = 64 * 2**20
@@ -35,7 +60,8 @@
     "widen_b": (4, 2048), "spatial_b": (2, 512), "reduce_b": (2, 512), "xp_b": (4, 2048), "bias_b": (2, 2048),
     "stride_b": (2, 512), "entry_b": (2, 512),
 }
-EX = {n: i for i, n in enumerate(EXCHANGES)}
+EX = {n: i % 2 for i, n in enumerate(n for n in EXCHANGES if n != "bias_b")}
+EX["bias_b"] = 2
 ROW = {"entry": 0, "stride": 2, "reduce": 4, "spatial": 6, "expand": 8, "project": 16, "widen": 24, "excite": 32, "gating": 36,
        "squeeze": 40, "shrink": 41}
 SMALL = 48
@@ -88,7 +114,7 @@
         s["W" + n] = pltpu.VMEM((4, 2, r, c), BF)
     for k, (r, c) in CLASSES.items():
         s["RC" + k] = pltpu.VMEM((2, 4, 2, r, c), BF)
-        s["R1" + k] = pltpu.VMEM((2, 2, r, c), BF)
+        s["R1" + k] = pltpu.VMEM((4, r, c), BF)
         s["R2" + k] = pltpu.VMEM((2, 4, r, c), BF)
         s["RZ" + k] = pltpu.VMEM((3, r, c), BF)
     for n, (r, c) in EXCHANGES.items():
@@ -124,25 +150,79 @@
         s[n] = pltpu.VMEM((8, WIDE), F32)
     for n in ("inner1", "inner2", "ing"):
         s[n] = pltpu.VMEM((8, 128), F32)
+    s["params"] = pltpu.VMEM((SMALL, 128), F32)
+    for n, _, rows in VECTORS:
+        s["v_" + n] = pltpu.VMEM((rows, 128), F32)
+    for n in ("A", "B"):
+        s["in" + n] = pltpu.VMEM((32, 512), BF)
     s["PR"] = pltpu.VMEM((4, SMALL, 128), F32)
     s["FS"] = pltpu.VMEM((4, SMALL, 128), F32)
     s["FR"] = pltpu.VMEM((4, SMALL, 128), F32)
     dma = pltpu.SemaphoreType.DMA
-    s["ag_s"] = dma((9, 9))
-    s["ag_r"] = dma((9, 9))
-    s["loc"] = dma((16,))
-    s["rs_s"] = dma((9, 9))
-    s["rs_r"] = dma((9, 9))
-    s["st_s"] = dma((13, 7))
-    s["st_r"] = dma((13, 8))
+    s["ag_s"] = dma((COUNT, 11))
+    s["ag_r"] = dma((COUNT, 11))
+    s["loc"] = dma((COUNT + 4,))
+    s["vec"] = dma((len(VECTORS) + 4,))
+    s["rs_s"] = dma((COUNT, 11))
+    s["rs_r"] = dma((COUNT, 11))
+    s["st_s"] = dma((3, 7))
+    s["st_r"] = dma((3, 8))
     s["mp_s"] = dma((5, 4))
     s["mp_r"] = dma((5, 4))
     s["free"] = pltpu.SemaphoreType.REGULAR((3,))
     return s
 
 
-IN_NAMES = ["images", "sizes", "cot_in", "params"] + ["in" + n for n in NAMES]
+VECTORS = []
+for _n in ("entry", "stride", "reduce", "spatial"):
+    VECTORS += [(_n + "_gain", ROW[_n], 1), (_n + "_shift", ROW[_n] + 1, 1)]
+for _n in ("expand", "project", "widen"):
+    VECTORS += [(_n + "_gain", ROW[_n], 4), (_n + "_shift", ROW[_n] + 4, 4)]
+VECTORS += [("excite_bias", ROW["excite"], 4), ("gating_bias", ROW["gating"], 4)]
+VECTORS += [("squeeze_bias", ROW["squeeze"], 1), ("shrink_bias", ROW["shrink"], 1)]
+PLAIN = [n for n in NAMES if n not in ("A", "B")]
+IN_NAMES = ["images", "sizes", "cot_in"] + ["in" + n for n in PLAIN] + ["sqA", "exA", "sqB", "exB"] + [v[0] for v in VECTORS]
 OUT_NAMES = ["result", "igrad"] + ["out" + n for n in NAMES] + ["small"]
+LAST_IN = ["result", "igrad"] + ["out" + n for n in NAMES] + ["small"]
+LAST_OUT = ["f_result", "f_igrad"] + ["f_" + n for n in PLAIN] + ["f_sqA", "f_exA", "f_sqB", "f_exB"] + [v[0] for v in VECTORS]
+
+
+def last_body(*refs):
+    g = dict(zip(LAST_IN + LAST_OUT, refs))
+    step = pl.program_id(0)
+
+    @pl.when(step == 0)
+    def _():
+        for n in PLAIN:
+            g["f_" + n][...] = g["out" + n][...]
+        for n in "AB":
+            g["f_sq" + n][...] = g["out" + n][0:16, :]
+            g["f_ex" + n][...] = g["out" + n][16:32, :]
+        for n, row, rows in VECTORS:
+            g[n][...] = g["small"][row : row + rows, :]
+
+    g["f_igrad"][...] = g["igrad"][...].astype(F32)
+    g["f_result"][...] = g["result"][...]
+
+
+class Copy:
+    def __init__(self, *given):
+        self.given = given
+
+    def made(self):
+        src, dst, ss, rs, dev = self.given
+        return pltpu.make_async_remote_copy(
+            src_ref=src, dst_ref=dst, send_sem=ss, recv_sem=rs, device_id=dev, device_id_type=MESH
+        )
+
+    def start(self, priority=0):
+        self.made().start(priority=priority)
+
+    def wait_recv(self):
+        self.made().wait_recv()
+
+    def wait_send(self):
+        self.made().wait_send()
 
 
 def body(*refs):
@@ -173,80 +253,141 @@
         return pl.ds(pl.multiple_of(j * w, w), w)
 
     def rcopy(src, dst, ss, rs, dev):
-        return pltpu.make_async_remote_copy(
-            src_ref=src, dst_ref=dst, send_sem=ss, recv_sem=rs, device_id=dev, device_id_type=MESH
-        )
+        return Copy(src, dst, ss, rs, dev)
 
     partners = [(lax.rem(z + k // 2, 4) * 2 + lax.rem(y + k % 2, 2), m) for k in range(1, 8)]
     partners += [mdev(k) for k in range(1, 4)]
+    vec = [pltpu.make_async_copy(g[v[0]], g["v_" + v[0]], s.vec.at[i]) for i, v in enumerate(VECTORS)]
+    for i, n in enumerate("AB"):
+        vec += [
+            pltpu.make_async_copy(g["sq" + n], g["in" + n].at[pl.ds(0, 16)], s.vec.at[len(VECTORS) + 2 * i]),
+            pltpu.make_async_copy(g["ex" + n], g["in" + n].at[pl.ds(16, 16)], s.vec.at[len(VECTORS) + 2 * i + 1]),
+        ]
+    own_pic = pltpu.make_async_copy(s.images.at[m], s.stage, s.loc.at[COUNT])
+    own_pic.start()
+    for t in vec:
+        t.start()
     barrier = pltpu.get_barrier_semaphore()
     for dev in partners:
         pl.semaphore_signal(barrier, inc=1, device_id=dev, device_id_type=MESH)
     pl.semaphore_wait(barrier, len(partners))
 
-    def part(n, zs, ys, mi):
+    def part(piece, zs, ys, mi):
+        n, i = piece
         rows, columns, dim, _ = TENSORS[n]
+        start, size = PIECES[n][i]
         if dim == 1:
-            return g["W" + n].at[zs, ys, :, col(mi, columns // 4)]
-        return g["W" + n].at[zs, ys, col(mi, rows // 4), :]
-
-    def ag(n, slot, region, dev, src=None):
-        i = INDEX[n]
+            return g["W" + n].at[zs, ys, pl.ds(start, size), col(mi, columns // 4)]
+        return g["W" + n].at[zs, ys, col(mi, rows // 4), pl.ds(start, size)]
+
+    def cut(piece):
+        n, i = piece
+        start, size = PIECES[n][i]
+        return (pl.ds(start, size), whole) if TENSORS[n][2] == 1 else (whole, pl.ds(start, size))
+
+    def shard(piece):
+        return g["in" + piece[0]].at[cut(piece)]
+
+    def ag(p, slot, region, dev, src=None):
+        i = INDEX[p]
         return rcopy(region if src is None else src, region, s.ag_s.at[i, slot], s.ag_r.at[i, slot], dev)
 
-    def ag_z(n):
-        own = part(n, z, y, m)
-        pltpu.make_async_copy(g["in" + n], own, s.loc.at[INDEX[n]]).start()
-        for k in range(1, 4):
-            ag(n, k - 1, own, zdev(k), g["in" + n]).start()
-
-    def ag_1(n):
-        pltpu.make_async_copy(g["in" + n], part(n, z, y, m), s.loc.at[INDEX[n]]).wait()
-        for k in range(1, 4):
-            ag(n, k - 1, part(n, lax.rem(z + 4 - k, 4), y, m), zdev(k)).wait_recv()
-        ag(n, 3, part(n, whole, y, m), xdev).start()
-        ag(n, 4, part(n, whole, y, m), ydev).start()
-
-    def ag_2(n):
-        ag(n, 3, part(n, whole, y, mx), xdev).wait_recv()
-        ag(n, 4, part(n, whole, 1 - y, m), ydev).wait_recv()
-        ag(n, 5, part(n, pl.ds(0, 2), y, mx), ydev).start()
-        ag(n, 6, part(n, pl.ds(2, 2), 1 - y, m), xdev).start()
-
-    def ag_c(n):
-        ag(n, 5, part(n, pl.ds(0, 2), 1 - y, mx), ydev).wait_recv()
-        ag(n, 6, part(n, pl.ds(2, 2), 1 - y, mx), xdev).wait_recv()
-        for xx in range(2):
-            ag(n, 7 + xx, part(n, whole, whole, xx * 2 + c), cdev).start()
-
-    def ag_done(n):
-        for xx in range(2):
-            ag(n, 7 + xx, part(n, whole, whole, xx * 2 + (1 - c)), cdev).wait_recv()
+    def place(p):
+        return pltpu.make_async_copy(shard(p), part(p, z, y, m), s.loc.at[INDEX[p]])
+
+    def ag_copies(p):
+        own = part(p, z, y, m)
+        out, here = {}, {}
+        if p in AG_Z_LAST:
+            out[0] = [ag(p, 3, own, xdev, shard(p)), ag(p, 4, own, ydev, shard(p))]
+            here[0] = [(3, part(p, z, y, mx)), (4, part(p, z, 1 - y, m))]
+            out[1] = [ag(p, 5, part(p, z, y, mx), ydev)]
+            here[1] = [(5, part(p, z, 1 - y, mx))]
+            out[2] = [ag(p, SLOTS[k - 1 + 3 * xx], part(p, z, whole, xx * 2 + c), zdev(k)) for k in range(1, 4) for xx in range(2)]
+            here[2] = [
+                (SLOTS[k - 1 + 3 * xx], part(p, lax.rem(z + 4 - k, 4), whole, xx * 2 + c)) for k in range(1, 4) for xx in range(2)
+            ]
+        else:
+            share = 3 if INDEX[p] in AG_MORE[3] else 4 if INDEX[p] in AG_MORE[4] else 2
+            low, high = pl.ds(0, share), pl.ds(share, 4 - share)
+            out[0] = [ag(p, k - 1, own, zdev(k), shard(p)) for k in range(1, 4)]
+            here[0] = [(k - 1, part(p, lax.rem(z + 4 - k, 4), y, m)) for k in range(1, 4)]
+            out[1] = [ag(p, 3, part(p, whole, y, m), xdev), ag(p, 4, part(p, whole, y, m), ydev)]
+            here[1] = [(3, part(p, whole, y, mx)), (4, part(p, whole, 1 - y, m))]
+            out[2] = [ag(p, 5, part(p, low, y, mx), ydev)]
+            here[2] = [(5, part(p, low, 1 - y, mx))]
+            if share < 4:
+                out[2] += [ag(p, 6, part(p, high, 1 - y, m), xdev)]
+                here[2] += [(6, part(p, high, 1 - y, mx))]
+        out[3] = [ag(p, 7 + xx, part(p, whole, whole, xx * 2 + c), cdev) for xx in range(2)]
+        here[3] = [(7 + xx, part(p, whole, whole, xx * 2 + (1 - c))) for xx in range(2)]
+        return out, here
+
+    def landed(p, here):
+        for slot, region in here:
+            ag(p, slot, region, cdev).wait_recv()
+
+    def ag_z(p):
+        place(p).start()
+        for t in ag_copies(p)[0][0]:
+            t.start()
+
+    def ag_1(p):
+        out, here = ag_copies(p)
+        place(p).wait()
+        landed(p, here[0])
+        for t in out[1]:
+            t.start()
+
+    def ag_2(p):
+        out, here = ag_copies(p)
+        landed(p, here[1])
+        for t in out[2]:
+            t.start()
+
+    def ag_c(p):
+        out, here = ag_copies(p)
+        landed(p, here[2])
+        for t in out[3]:
+            t.start()
 
     def ag_drain(n):
-        own = part(n, z, y, m)
-        for k in range(1, 4):
-            ag(n, k - 1, own, zdev(k), g["in" + n]).wait_send()
-        ag(n, 3, part(n, whole, y, m), xdev).wait_send()
-        ag(n, 4, part(n, whole, y, m), ydev).wait_send()
-        ag(n, 5, part(n, pl.ds(0, 2), y, mx), ydev).wait_send()
-        ag(n, 6, part(n, pl.ds(2, 2), 1 - y, m), xdev).wait_send()
-        for xx in range(2):
-            ag(n, 7 + xx, part(n, whole, whole, xx * 2 + c), cdev).wait_send()
+        if "ag" in OPT:
+            return
+        for i in range(len(PIECES[n])):
+            for copies in ag_copies((n, i))[0].values():
+                for t in copies:
+                    t.wait_send()
+
+    def stop(t):
+        pass
 
     ticks = {"k": 0}
 
     def tick():
+        if "ag" in OPT:
+            return
         k = ticks["k"]
         ticks["k"] = k + 1
-        if 0 <= k - 2 < 9:
-            ag_c(NAMES[k - 2])
-        if 0 <= k - 1 < 9:
-            ag_2(NAMES[k - 1])
-        if k < 9:
-            ag_1(NAMES[k])
-        if k + 2 < 9:
-            ag_z(NAMES[k + 2])
+        for stage, lags in ((ag_c, (2 * LAG, 2 * LAG)), (ag_2, (LAG, 0)), (ag_1, (0, -1)), (ag_z, (-LEAD, -LEAD))):
+            for slow in range(2):
+                j = k - lags[slow]
+                if 0 <= j < COUNT and (ORDER[j] in AG_Z_LAST) == bool(slow):
+                    stage(ORDER[j])
+
+    def mark(tag):
+        for t in TICKS:
+            if t == tag:
+                if ticks["k"] < COUNT + 2 * LAG:
+                    tick()
+
+    def need(n):
+        if "ag" in OPT:
+            return
+        while ticks["k"] <= LAST[n] + 2 * LAG:
+            tick()
+        for i in range(len(PIECES[n])):
+            landed((n, i), ag_copies((n, i))[1][3])
 
     def loop(count, fn, unroll=1):
         def step(j, carry):
@@ -255,111 +396,151 @@
 
         lax.fori_loop(0, count, step, 0, unroll=unroll)
 
-    def rs(n, slot, region, landing, dev):
-        i = INDEX[n]
+    def rs(p, slot, region, landing, dev):
+        i = INDEX[p]
         return rcopy(region, landing, s.rs_s.at[i, slot], s.rs_r.at[i, slot], dev)
 
     credits = {"T": 0, "V": 1, "B": 2}
-    takes = {"S": 0, "X": 1, "A": 2}
-
-    def rs_partners():
-        return [xdev, ydev, cdev] + [zdev(k) for k in range(1, 4)]
-
-    def rs_copies(n):
+    takes = {"S": ("T", 0), "X": ("V", 1), "A": ("B", 2)}
+    active = []
+
+    def bump(region, extra):
+        region[...] = region[...] + extra
+
+    def reduce_scatter(p):
+        n, piece = p
         k = TENSORS[n][3]
         rc, r1, r2, rz = g["RC" + k], g["R1" + k], g["R2" + k], g["RZ" + k]
-        out = {"c": [rs(n, xx, part(n, whole, whole, xx * 2 + (1 - c)), rc.at[xx], cdev) for xx in range(2)]}
-        out["1"] = [
-            rs(n, 2, part(n, pl.ds(0, 2), 1 - y, mx), r1.at[0], xdev),
-            rs(n, 3, part(n, pl.ds(2, 2), 1 - y, mx), r1.at[1], ydev),
+        c_ = cut(p)
+        pair = (pl.ds(0, 2),)
+        four = (pl.ds(0, 4),)
+        swap = [
+            rs(p, xx, part(p, whole, whole, xx * 2 + (1 - c)), rc.at[(xx, pl.ds(0, 4), pl.ds(0, 2)) + c_], cdev) for xx in range(2)
         ]
-        out["2"] = [
-            rs(n, 4, part(n, whole, y, mx), r2.at[0], xdev),
-            rs(n, 5, part(n, whole, 1 - y, m), r2.at[1], ydev),
-        ]
-        out["z"] = [rs(n, 5 + k, part(n, lax.rem(z + k, 4), y, m), rz.at[k - 1], zdev(k)) for k in range(1, 4)]
-        return out, rc, r1, r2, rz
-
-    def bump(region, extra):
-        region[...] = region[...] + extra
-
-    def reduce_scatter(n):
-        cp, rc, r1, r2, rz = rs_copies(n)
-        if n in takes:
-            pl.semaphore_wait(s.free.at[takes[n]], 6)
-        for t in cp["c"]:
+        z_last = p not in RS_Z_LAST
+        first, second, third = [], [], []
+        if z_last:
+            share = 3 if INDEX[p] in RS_MORE[3] else 4 if INDEX[p] in RS_MORE[4] else 2
+            low, high = pl.ds(0, 4 - share), pl.ds(4 - share, share)
+            if share < 4:
+                first += [rs(p, 2, part(p, low, 1 - y, mx), r1.at[(pl.ds(0, 4 - share),) + c_], xdev)]
+            first += [rs(p, 3, part(p, high, 1 - y, mx), r1.at[(pl.ds(4 - share, share),) + c_], ydev)]
+            second = [
+                rs(p, 4, part(p, whole, y, mx), r2.at[(0, pl.ds(0, 4)) + c_], xdev),
+                rs(p, 5, part(p, whole, 1 - y, m), r2.at[(1, pl.ds(0, 4)) + c_], ydev),
+            ]
+            third = [rs(p, 5 + k, part(p, lax.rem(z + k, 4), y, m), rz.at[(k - 1,) + c_], zdev(k)) for k in range(1, 4)]
+        else:
+            for k in range(1, 4):
+                for xx in range(2):
+                    landing = r2.at[(k - 1, pl.ds(xx * 2, 2)) + c_] if k < 3 else r1.at[(pl.ds(xx * 2, 2),) + c_]
+                    first += [rs(p, SLOTS[k - 1 + 3 * xx], part(p, lax.rem(z + k, 4), whole, xx * 2 + c), landing, zdev(k))]
+            second = [rs(p, 3, part(p, z, 1 - y, mx), rz.at[(0,) + c_], ydev)]
+            third = [rs(p, 4, part(p, z, y, mx), rz.at[(1,) + c_], xdev), rs(p, 5, part(p, z, 1 - y, m), rz.at[(2,) + c_], ydev)]
+        for t in swap:
             t.start()
         yield
-        for t in cp["c"]:
+        for t in swap:
             t.wait_recv()
 
         def add_c(j):
             zz, yy = j // 2, lax.rem(j, 2)
             for xx in range(2):
-                bump(part(n, zz, yy, xx * 2 + c), rc[xx, zz, yy])
+                bump(part(p, zz, yy, xx * 2 + c), rc[(xx, zz, yy) + c_])
 
         loop(8, add_c)
-        for t in cp["1"]:
+        for t in first:
             t.start()
-        yield
-        for t in cp["1"]:
+        for _ in range(RLAG if z_last else ZLAG):
+            yield
+        for t in first:
             t.wait_recv()
-        for h in range(2):
-            bump(part(n, h, 1 - y, m), r1[0, h])
-            bump(part(n, 2 + h, y, mx), r1[1, h])
-        for t in cp["2"]:
+        if z_last:
+            for h in range(4 - share):
+                bump(part(p, h, 1 - y, m), r1[(h,) + c_])
+            for h in range(share):
+                bump(part(p, 4 - share + h, y, mx), r1[(4 - share + h,) + c_])
+        else:
+            for yy in range(2):
+                for xx in range(2):
+                    got = [r2[(0, xx * 2 + yy) + c_], r2[(1, xx * 2 + yy) + c_], r1[(xx * 2 + yy,) + c_]]
+                    bump(part(p, z, yy, xx * 2 + c), (got[0].astype(F32) + got[1].astype(F32) + got[2].astype(F32)).astype(BF))
+        for t in second:
             t.start()
-        yield
-        for t in cp["2"]:
+        for _ in range(RLAG if z_last else 1):
+            yield
+        for t in second:
             t.wait_recv()
-
-        def add_2(zz):
-            bump(part(n, zz, y, m), (r2[0, zz].astype(F32) + r2[1, zz].astype(F32)).astype(BF))
-
-        loop(4, add_2)
-        for t in cp["z"]:
+        if z_last:
+
+            def add_2(zz):
+                bump(part(p, zz, y, m), (r2[(0, zz) + c_].astype(F32) + r2[(1, zz) + c_].astype(F32)).astype(BF))
+
+            loop(4, add_2)
+        else:
+            bump(part(p, z, y, mx), rz[(0,) + c_])
+        for t in third:
             t.start()
-        yield
-        for t in cp["z"]:
+        for _ in range(RLAG if z_last else 1):
+            yield
+        for t in third:
             t.wait_recv()
-        total = part(n, z, y, m)[...].astype(F32)
-        for k in range(3):
-            total = total + rz[k].astype(F32)
-        g["out" + n][...] = total
-        if n in credits:
-            for dev in rs_partners():
+        total = part(p, z, y, m)[...].astype(F32)
+        for k in range(0 if z_last else 1, 3):
+            total = total + rz[(k,) + c_].astype(F32)
+        g["out" + n][c_] = total
+        if n in credits and piece == len(PIECES[n]) - 1:
+            for dev in [xdev, ydev, cdev] + [zdev(k) for k in range(1, 4)]:
                 pl.semaphore_signal(s.free.at[credits[n]], inc=1, device_id=dev, device_id_type=MESH)
-        for stage in cp.values():
-            for t in stage:
-                t.wait_send()
-
-    active = []
+        for t in swap + first + second + third:
+            t.wait_send()
+
+    waiting = []
 
     def pump():
-        for gen in list(active):
+        for item in list(active):
             try:
-                next(gen)
+                next(item[1])
             except StopIteration:
-                active.remove(gen)
-
-    def begin(n):
-        gen = reduce_scatter(n)
-        active.append(gen)
-        next(gen)
+                active.remove(item)
+        for _ in range(STARTS):
+            if not waiting:
+                return
+            n, i = waiting[0]
+            if n in takes and i == 0:
+                if any(item[0][0] == takes[n][0] for item in active):
+                    return
+                pl.semaphore_wait(s.free.at[takes[n][1]], 6)
+            gen = reduce_scatter(waiting.pop(0))
+            active.append(((n, i), gen))
+            next(gen)
+
+    def pumps(tag):
+        for t in PUMPS:
+            if t == tag:
+                pump()
+
+    def begin(n, pieces=None):
+        if "rs" in OPT or "no" + n in OPT:
+            return
+        for i in range(len(PIECES[n])) if pieces is None else pieces:
+            waiting.append((n, i))
 
     def st_peers():
         return [lax.rem(z + k // 2, 4) * 2 + lax.rem(y + k % 2, 2) for k in range(1, 8)]
 
     def send_stats(e):
         buf, i = g["X_" + e], EX[e]
+        if "stats" in OPT:
+            return
         for k, dd in enumerate(st_peers()):
-            rcopy(buf.at[d], buf.at[d], s.st_s.at[i, k], s.st_r.at[i, d], (dd, m)).start()
+            rcopy(buf.at[d], buf.at[d], s.st_s.at[i, k], s.st_r.at[i, d], (dd, m)).start(priority=1 if 'prio' in OPT else 0)
 
     def get_stats(e):
         buf, i = g["X_" + e], EX[e]
-        for k, dd in enumerate(st_peers()):
+        for k, dd in enumerate([] if "stats" in OPT else st_peers()):
             rcopy(buf.at[dd], buf.at[dd], s.st_s.at[i, k], s.st_r.at[i, dd], (dd, m)).wait_recv()
-        for k, dd in enumerate(st_peers()):
+        for k, dd in enumerate([] if "stats" in OPT else st_peers()):
             rcopy(buf.at[d], buf.at[d], s.st_s.at[i, k], s.st_r.at[i, d], (dd, m)).wait_send()
         total = buf[0]
         for k in range(1, 8):
@@ -382,14 +563,22 @@
     img_src, img_dst = (lambda j: s.stage.at[:, col(j, 256)]), (lambda j: s.igrad.at[j])
     fin_src, fin_dst = (lambda j: s.FS.at[j]), (lambda j: s.FR.at[j])
 
-    ag_z("E")
+    if "ag" not in OPT:
+        for p in ORDER[:LEAD]:
+            ag_z(p)
+    for t in vec:
+        t.wait()
+    for n, row, rows in VECTORS:
+        s.params[row : row + rows, :] = g["v_" + n][...]
+    s.params[42:SMALL, :] = jnp.zeros((SMALL - 42, 128), F32)
     for t in mp_copies(1, par_src, par_dst):
         t.start()
-    own_pic = pltpu.make_async_copy(s.images.at[m], s.stage, s.loc.at[9])
-    own_pic.start()
-    ag_z("P")
     s.PR[m] = s.params[...]
 
+    if "start0" in OPT:
+        mp_wait(1, par_src, par_dst)
+        own_pic.wait()
+        return
     r64 = lax.broadcasted_iota(jnp.int32, (64, 128), 0)
     p64, q64 = r64 >> 3, r64 & 7
     s.pix[...] = jnp.ones((8, 128), F32)
@@ -419,6 +608,9 @@
     s.perm[...] = jnp.where(cp_ == source, 1.0, 0.0).astype(BF)
 
     own_pic.wait()
+    if "start1" in OPT:
+        mp_wait(1, par_src, par_dst)
+        return
     for i in range(3):
         def permute(j, i=i):
             v = dot(s.perm[...], s.stage[i * 256 : (i + 1) * 256, col(j, 256)]).astype(BF)
@@ -427,7 +619,6 @@
 
         loop(4, permute)
 
-    tick()
     tick()
     mp_wait(1, par_src, par_dst)
     for n, r in ROW.items():
@@ -491,8 +682,19 @@
         put(e, row, columns, total)
         put(e, row + 1, columns, square)
 
-    tick()
-    ag_done("E")
+    if "compute" in OPT:
+        for n in NAMES:
+            need(n)
+        for n in NAMES:
+            ag_drain(n)
+        for n in ["B", "V", "T", "R", "A", "X", "P", "S", "E"]:
+            for i in range(len(PIECES[n])):
+                begin(n, [i])
+                pump()
+        while active or waiting:
+            pump()
+        return
+    need("E")
 
     def entry_step(n):
         b = col(n, 256)
@@ -512,9 +714,9 @@
     put("entry", 2, slice(0, 512), lanes(colsum(s.insm[...]), 4))
     put("entry", 3, slice(0, 512), lanes(colsum(s.redm[...]), 4))
     send_stats("entry")
-
-    tick()
-    ag_done("P")
+    mark("a")
+
+    need("P")
 
     def project_step(n):
         b = col(n, 256)
@@ -523,6 +725,7 @@
         sums_wide("xp", b, v, None, 2)
 
     loop(8, project_step)
+    mark("b")
     tot = get_stats("entry")
     s.cnt[0:2, :] = tot[2:4]
     norm_vectors(s.nv5, 0, tot[0:1], tot[1:2], tot[2:3], s.gv5, 0)
@@ -534,6 +737,7 @@
         s.act_e[:, col(j, 128)] = (pre * sigmoid(pre) * mask).astype(BF)
 
     loop(16, entry_act_step, 2)
+    mark("c")
     for a in range(3):
         for b in range(3):
             t = a * 3 + b
@@ -544,6 +748,8 @@
                 v = dot(s.shift[which], v).astype(BF)
             s.taps1[:, t * 512 : t * 512 + 512] = v
 
+    mark("d")
+
     def conv3(taps, w, raw, e):
         def step(n):
             b = col(n, 256)
@@ -555,20 +761,20 @@
 
         loop(2, step)
 
-    tick()
-    ag_done("S")
+    need("S")
     conv3(s.taps1, s.WS, s.s_raw, "stride")
     send_stats("stride")
     for t in mp_copies(0, cot_src, cot_dst):
         t.start()
-    own_cot = pltpu.make_async_copy(cot_src(m), cot_dst(m), s.loc.at[10])
+    own_cot = pltpu.make_async_copy(cot_src(m), cot_dst(m), s.loc.at[COUNT + 1])
     own_cot.start()
-    tick()
-    ag_done("X")
+    mark("e")
+    need("X")
     tot = get_stats("stride")
     count5 = s.cnt[1:2, :]
     norm_vectors(s.nv5, 1, tot[0:1], tot[1:2], count5, s.gv5, 2)
     activate(s.s_raw, 1, s.act_s)
+    mark("f")
 
     for n in ("isum1", "isum2", "G0", "G1"):
         g[n][...] = jnp.zeros((8, WIDE), F32)
@@ -584,8 +790,8 @@
 
     widening(s.act_s, s.WX, s.x_raw, "xp", s.isum1)
     send_stats("xp")
-    tick()
-    ag_done("A")
+    mark("g")
+    need("A")
     count20 = lanes(s.cnt[1:2, :], 4)
     tot = get_stats("xp")
     norm_vectors(s.nv20, 0, tot[0:1], tot[1:2], count20, s.gv20, 0)
@@ -600,6 +806,7 @@
         scale[...] = sigmoid(gate)
 
     squeeze_excite(0, s.isum1, s.WA, s.PR[0, 40:41, :], 6, s.pool1, s.inner1, s.scale1)
+    mark("h")
 
     def first_sum(j, i):
         b, rows = col(j, 128), slice(i * 64, i * 64 + 64)
@@ -613,9 +820,9 @@
             s.first[rows, col(j, 128)] = (v * sigmoid(v) * s.redm[rows, :]).astype(BF)
 
     loop(16, first_step, 2)
-
-    tick()
-    ag_done("R")
+    mark("i")
+
+    need("R")
 
     def reduce_step(n):
         b = col(n, 256)
@@ -625,7 +832,7 @@
 
     loop(2, reduce_step)
     send_stats("reduce")
-    tick()
+    mark("j")
     tot = get_stats("reduce")
     norm_vectors(s.nv5, 2, tot[0:1], tot[1:2], count5, s.gv5, 4)
     activate(s.r_raw, 2, s.act_p)
@@ -634,17 +841,19 @@
         if t != 4:
             v = dot(s.shift[t], v).astype(BF)
         s.taps2[:, t * 512 : t * 512 + 512] = v
-    ag_done("T")
+    mark("k")
+    need("T")
     conv3(s.taps2, s.WT, s.p_raw, "spatial")
     send_stats("spatial")
-    tick()
-    ag_done("V")
+    mark("l")
+    need("V")
     tot = get_stats("spatial")
     norm_vectors(s.nv5, 3, tot[0:1], tot[1:2], count5, s.gv5, 6)
     activate(s.p_raw, 3, s.act_p)
+    mark("m")
     widening(s.act_p, s.WV, s.w_raw, "widen", s.isum2)
     send_stats("widen")
-    ag_done("B")
+    need("B")
     own_cot.wait()
     mp_wait(0, cot_src, cot_dst)
     tot = get_stats("widen")
@@ -669,9 +878,15 @@
     loop(16, result_step, 2)
     for t in mp_copies(2, res_src, res_dst):
         t.start()
-    own_res = pltpu.make_async_copy(res_src(m), res_dst(m), s.loc.at[11])
+    own_res = pltpu.make_async_copy(res_src(m), res_dst(m), s.loc.at[COUNT + 2])
     own_res.start()
 
+    if "fwd" in OPT:
+        for n in NAMES:
+            ag_drain(n)
+        own_res.wait()
+        mp_wait(2, res_src, res_dst)
+        return
     def keep512(n, k, v):
         for j in range(4):
             s.FS[j, ROW[n] + k : ROW[n] + k + 1, :] = v[:, j * 128 : j * 128 + 128]
@@ -791,6 +1006,7 @@
     excite_weights("B", s.pool2, s.inner2)
     begin("B")
     tot = get_stats("widen_b")
+    pumps("A")
     keep2048(ROW["widen"], tot[0:1])
     keep2048(ROW["widen"] + 4, tot[1:2])
     keep2048(ROW["gating"], tot[2:3])
@@ -798,14 +1014,16 @@
         s.FS[j, ROW["shrink"] : ROW["shrink"] + 1, :] = tot[3:4, 0:128]
     norm_back_vectors(s.nv20, 2, tot[0:1], tot[1:2], count20)
     wide_grad(2, s.w_raw, s.g1, s.scale2)
+    pumps("B")
     widening_back(s.g1, s.WV)
     narrow_back("spatial_b", 3, s.acc, s.p_raw)
     send_stats("spatial_b")
-    pump()
+    pumps("C")
     widening_weights("V", s.act_p, s.g1)
+    pumps("D")
     narrow_stats("spatial_b", "spatial")
     narrow_grad(3, s.p_raw)
-    pump()
+    pumps("E")
     s.acc[...] = jnp.zeros((Q, 512), F32)
 
     def spatial_back(t):
@@ -813,13 +1031,15 @@
         s.acc[...] += dot_cols(v, s.WT[:, :, col(t, 64), :].reshape(512, 512))
 
     loop(9, spatial_back)
+    pumps("F")
     narrow_back("reduce_b", 2, s.acc, s.r_raw)
     send_stats("reduce_b")
-    pump()
+    pumps("G")
     conv3_weights("T", s.taps2)
+    pumps("H")
     narrow_stats("reduce_b", "reduce")
     narrow_grad(2, s.r_raw)
-    pump()
+    pumps("I")
 
     def reduce_back(k):
         v = dot_cols(s.gs[...], s.WR[k // 2, lax.rem(k, 2)])
@@ -843,6 +1063,7 @@
             put("xp_b", 3, b, shift_sum)
 
     loop(8, reduce_back)
+    pumps("J")
     sums = excite_back(0, s.isum1, s.WA, s.inner1, s.scale1)
     put("xp_b", 0, slice(0, WIDE), sums[0])
     put("xp_b", 1, slice(0, WIDE), sums[1])
@@ -850,7 +1071,7 @@
     put("bias_b", 0, slice(0, WIDE), sums[2])
     put("bias_b", 1, slice(0, WIDE), lanes(sums[3], 16))
     send_stats("bias_b")
-    pump()
+    pumps("K")
     ag_drain("R")
 
     def reduce_weights(k):
@@ -858,19 +1079,22 @@
 
     loop(8, reduce_weights)
     begin("R")
+    pumps("L")
     ag_drain("A")
     excite_weights("A", s.pool1, s.inner1)
     begin("A")
+    pumps("M")
     tot = get_stats("xp_b")
     for k, n in enumerate(("expand", "project")):
         keep2048(ROW[n], tot[2 * k : 2 * k + 1])
         keep2048(ROW[n] + 4, tot[2 * k + 1 : 2 * k + 2])
         norm_back_vectors(s.nv20, k, tot[2 * k : 2 * k + 1], tot[2 * k + 1 : 2 * k + 2], count20)
     wide_grad(0, s.x_raw, s.g1, s.scale1)
+    pumps("N")
     widening_back(s.g1, s.WX)
     narrow_back("stride_b", 1, s.acc, s.s_raw)
     send_stats("stride_b")
-    pump()
+    pumps("O")
     own_res.wait()
     mp_wait(2, res_src, res_dst)
     wide_grad(1, s.j_raw, s.g2, None)
@@ -880,7 +1104,9 @@
         s.sgrad[:, col(zz, 256)] = dot_cols(s.g2[...], w)
 
     loop(4, project_back)
+    pumps("P")
     widening_weights("X", s.act_s, s.g1)
+    pumps("Q")
     ag_drain("P")
 
     def project_weights(n):
@@ -891,9 +1117,10 @@
 
     loop(8, project_weights)
     begin("P")
+    pumps("R")
     narrow_stats("stride_b", "stride")
     narrow_grad(1, s.s_raw)
-    pump()
+    pumps("S")
 
     for k in range(4):
         pa, pb = k // 2, k % 2
@@ -931,8 +1158,9 @@
 
     loop(4, entry_back)
     send_stats("entry_b")
-    pump()
+    pumps("U")
     conv3_weights("S", s.taps1)
+    pumps("V")
     narrow_stats("entry_b", "entry")
 
     def entry_grad(j):
@@ -943,6 +1171,7 @@
         s.act_e[:, b] = v.astype(BF)
 
     loop(16, entry_grad, 2)
+    pumps("W")
     tot = get_stats("bias_b")
     keep2048(ROW["excite"], tot[0:1])
     for j in range(4):
@@ -972,8 +1201,9 @@
         loop(4, unpermute)
     for t in mp_copies(3, img_src, img_dst):
         t.start()
-    own_img = pltpu.make_async_copy(img_src(m), img_dst(m), s.loc.at[12])
+    own_img = pltpu.make_async_copy(img_src(m), img_dst(m), s.loc.at[COUNT + 3])
     own_img.start()
+    pumps("X")
     ag_drain("E")
 
     def entry_weights(zz):
@@ -984,7 +1214,8 @@
 
     loop(4, entry_weights)
     begin("E")
-    while active:
+    pumps("Y")
+    while active or waiting:
         pump()
     mp_wait(4, fin_src, fin_dst)
     s.small[...] = ((s.FR[0] + s.FR[1]) + s.FR[2]) + s.FR[3]
@@ -996,57 +1227,76 @@
      expand_gain, expand_shift, project_weight, project_gain, project_shift, squeeze_weight, squeeze_bias, excite_weight,
      excite_bias, reduce_weight, reduce_gain, reduce_shift, spatial_weight, spatial_gain, spatial_shift, widen_weight,
      widen_gain, widen_shift, shrink_weight, shrink_bias, gating_weight, gating_bias, cotangent) = arrays
-    small = [entry_gain, entry_shift, stride_gain, stride_shift, reduce_gain, reduce_shift, spatial_gain, spatial_shift,
-             expand_gain, expand_shift, project_gain, project_shift, widen_gain, widen_shift, excite_bias, gating_bias,
-             squeeze_bias, shrink_bias]
-    params = jnp.concatenate([v.reshape(-1, 128) for v in small] + [jnp.zeros((SMALL - 42, 128), F32)], axis=0)
-    shards = {
+    weights = {
         "E": entry_weight,
         "P": project_weight,
         "S": stride_weight.reshape(576, 128),
         "X": expand_weight,
-        "A": jnp.concatenate([squeeze_weight.T, excite_weight], axis=0),
         "R": reduce_weight,
         "T": spatial_weight.reshape(576, 128),
         "V": widen_weight,
-        "B": jnp.concatenate([shrink_weight.T, gating_weight], axis=0),
     }
+    given = dict(
+        entry_gain=entry_gain, entry_shift=entry_shift, stride_gain=stride_gain, stride_shift=stride_shift,
+        reduce_gain=reduce_gain, reduce_shift=reduce_shift, spatial_gain=spatial_gain, spatial_shift=spatial_shift,
+        expand_gain=expand_gain, expand_shift=expand_shift, project_gain=project_gain, project_shift=project_shift,
+        widen_gain=widen_gain, widen_shift=widen_shift, excite_bias=excite_bias, gating_bias=gating_bias,
+        squeeze_bias=squeeze_bias, shrink_bias=shrink_bias,
+    )
+    small = [given[n].reshape(rows, 128) for n, _, rows in VECTORS]
+    hbm, vmem = pl.BlockSpec(memory_space=pl.ANY), pl.BlockSpec(memory_space=pltpu.VMEM)
     outs = [jax.ShapeDtypeStruct((4, Q, 512), BF), jax.ShapeDtypeStruct((4, 768, 256), BF)]
     outs += [jax.ShapeDtypeStruct(CLASSES[TENSORS[n][3]], F32) for n in NAMES]
     outs += [jax.ShapeDtypeStruct((SMALL, 128), F32)]
-    hbm, vmem = pl.BlockSpec(memory_space=pl.ANY), pl.BlockSpec(memory_space=pltpu.VMEM)
     got = pl.pallas_call(
         body,
         out_shape=outs,
-        in_specs=[hbm, pl.BlockSpec(memory_space=pltpu.SMEM), hbm, vmem] + [hbm] * len(NAMES),
+        in_specs=[hbm, pl.BlockSpec(memory_space=pltpu.SMEM), hbm] + [hbm] * (len(PLAIN) + 4 + len(VECTORS)),
         out_specs=[hbm, hbm] + [vmem] * (len(NAMES) + 1),
         scratch_shapes=list(scratch_list().values()),
-        compiler_params=pltpu.CompilerParams(
-            collective_id=0, has_side_effects=True, vmem_limit_bytes=VMEM_LIMIT
-        ),
+        compiler_params=pltpu.CompilerParams(collective_id=0, has_side_effects=True, vmem_limit_bytes=VMEM_LIMIT),
         cost_estimate=pl.CostEstimate(flops=14_000_000_000, bytes_accessed=30_000_000, transcendentals=10_000_000),
-    )(images.reshape(4, 768, 1024), image_size, cotangent.reshape(4, Q, 512), params, *[shards[n] for n in NAMES])
-    result, igrad, weights, rows = got[0], got[1], dict(zip(NAMES, got[2:-1])), got[-1]
-
-    def vector(first, count):
-        return rows[first : first + count].reshape(-1)
+    )(
+        images.reshape(4, 768, 1024), image_size, cotangent.reshape(4, Q, 512), *[weights[n] for n in PLAIN],
+        squeeze_weight.T, excite_weight, shrink_weight.T, gating_weight, *small,
+    )
+
+    def held(shape):
+        return pl.BlockSpec(shape, lambda i: (0, 0))
+
+    kinds = [held(CLASSES[TENSORS[n][3]]) for n in NAMES]
+    last = [jax.ShapeDtypeStruct((4, Q, 512), BF), jax.ShapeDtypeStruct((4, 768, 256), F32)]
+    last += [jax.ShapeDtypeStruct(CLASSES[TENSORS[n][3]], F32) for n in PLAIN]
+    last += [jax.ShapeDtypeStruct(v, F32) for v in ((16, 512),) * 4]
+    last += [jax.ShapeDtypeStruct((rows, 128), F32) for _, _, rows in VECTORS]
+    blocks = [pl.BlockSpec((1, Q, 512), lambda i: (i, 0, 0)), pl.BlockSpec((1, 768, 256), lambda i: (i, 0, 0))]
+    final = pl.pallas_call(
+        last_body,
+        grid=(4,),
+        out_shape=last,
+        in_specs=blocks + kinds + [held((SMALL, 128))],
+        out_specs=blocks + [held(CLASSES[TENSORS[n][3]]) for n in PLAIN] + [held(v) for v in ((16, 512),) * 4]
+        + [held((rows, 128)) for _, _, rows in VECTORS],
+        compiler_params=pltpu.CompilerParams(vmem_limit_bytes=VMEM_LIMIT),
+        cost_estimate=pl.CostEstimate(flops=1_000_000, bytes_accessed=10_000_000, transcendentals=0),
+    )(*got)
+    f = dict(zip(LAST_OUT, final))
 
     def pair(n):
-        k = 1 if n in NORM512 else 4
-        return vector(ROW[n], k), vector(ROW[n] + k, k)
+        return f[n + "_gain"].reshape(-1), f[n + "_shift"].reshape(-1)
 
     return (
-        result.reshape(cotangent.shape),
-        igrad.reshape(4, 3, 16, 16, 256).astype(F32),
-        weights["E"], *pair("entry"),
-        weights["S"].reshape(stride_weight.shape), *pair("stride"),
-        weights["X"], *pair("expand"),
-        weights["P"], *pair("project"),
-        weights["A"][:16].T, vector(ROW["squeeze"], 1), weights["A"][16:], vector(ROW["excite"], 4),
-        weights["R"], *pair("reduce"),
-        weights["T"].reshape(spatial_weight.shape), *pair("spatial"),
-        weights["V"], *pair("widen"),
-        weights["B"][:16].T, vector(ROW["shrink"], 1), weights["B"][16:], vector(ROW["gating"], 4),
+        f["f_result"].reshape(cotangent.shape),
+        f["f_igrad"].reshape(4, 3, 16, 16, 256),
+        f["f_E"], *pair("entry"),
+        f["f_S"].reshape(stride_weight.shape), *pair("stride"),
+        f["f_X"], *pair("expand"),
+        f["f_P"], *pair("project"),
+        f["f_sqA"].T, f["squeeze_bias"].reshape(-1), f["f_exA"], f["excite_bias"].reshape(-1),
+        f["f_R"], *pair("reduce"),
+        f["f_T"].reshape(spatial_weight.shape), *pair("spatial"),
+        f["f_V"], *pair("widen"),
+        f["f_sqB"].T, f["shrink_bias"].reshape(-1), f["f_exB"], f["gating_bias"].reshape(-1),
     )
 
 

time: 338 us -> 281 us (0.83)
  Pallas kernels: 311 us -> 279 us
  local copies, waits for them, and re-layouts: 19.2 us -> 1.38 us
  other arithmetic: 6.31 us -> 0 us
    pallas_call x1, Pallas kernels: 311 us -> 274 us  [fused_shards(): pl.pallas_call(body, out_shape=outs, in_specs=[hbm, pl.BlockSpec(memory_s...]
    concatenate x1 -> x0, local copies, waits for them, and re-layouts: 7.83 us -> none  [fused_shards(): jnp.concatenate([v.reshape(-1, 128) for v in small] + [jnp.zeros((SMALL -...]
    unnamed x25 -> x1, local copies, waits for them, and re-layouts: 7.02 us -> 1.38 us
    pallas_call x0 -> x1, Pallas kernels: none -> 5.43 us  [fused_shards(): pl.pallas_call(last_body, grid=(4,), out_shape=last, in_specs=blocks + ki...]
    convert_element_type x1 -> x0, other arithmetic: 3.61 us -> none  [fused_shards(): igrad.reshape(4, 3, 16, 16, 256).astype(F32)]
where the time goes in v3:
time: 281 us
  Pallas kernels  279 us (99%)
    pallas_call x1, Pallas kernels, fused_shards(): pl.pallas_call(body, out_shape=outs, in_specs=[hbm, pl.BlockSpec(memory_s...  274 us

profile of v3, /device:TPU:0, one launch (start us, length us, event | category | flops | bytes accessed | tf_op | source)
XLA Modules:
  0.0 281.2 jit_solution(3085959426241719999)
XLA Ops:
  0.7 1.4 copy.63.refs_1_
  2.0 273.6 %shard_map.543 = (bf16[4,192,512]{2,1,0:T(8,128)(2,1)}, bf16[4,768,256]{2,1,0:T(8,128)(2,1)}, f32[128,128]{1,0:T(8,128)}, f32[128,512]{1,0:T(8,128)}, f32[576,12...) custom-call(bf16[4,768,1024]{2,1,0:T(8,128)(2,1)} %bitcast.48, ...), custom_call_target="tpu_custom_call" | custom-call | flops 14000000000 | bytes 30000000 | tf_op jit(solution)/shard_map/pallas_call | solution.py:1251
  275.6 5.4 %shard_map.544 = (bf16[4,192,512]{2,1,0:T(8,128)(2,1)}, f32[4,768,256]{2,1,0:T(8,128)}, f32[128,128]{1,0:T(8,128)}, f32[128,512]{1,0:T(8,128)}, f32[576,128]{1,0...) custom-call(bf16[4,192,512]{2,1,0:T(8,128)(2,1)} %get-tuple-element., ...), custom_call_target="tpu_custom_call" | custom-call | flops 1000000 | bytes 10000000 | tf_op jit(solution)/shard_map/pallas_call | solution.py:1273

commit v4 on v3

--- a/solution.py
+++ b/solution.py
@@ -38,18 +38,16 @@
 }
 ORDER = [(n, i) for n in NAMES for i in range(len(PIECES[n]))]
 INDEX = {piece: i for i, piece in enumerate(ORDER)}
-AG_Z_LAST = ()
-RS_Z_LAST = ()
-AG_MORE = {3: (), 4: ()}
-RS_MORE = {3: (), 4: ()}
-ZLAG = 5
-SLOTS = (0, 1, 2, 6, 9, 10)
+AG_MORE = ()
+RS_MORE = (0, 5, 6, 7, 8)
+AG_ROWS, RS_ROWS = 8, 12
 LAST = {n: INDEX[n, len(PIECES[n]) - 1] for n in NAMES}
 COUNT = len(ORDER)
 LEAD, LAG, RLAG = 3, 2, 3
 OPT = ()
 TICKS = "bch"
 STARTS = 1
+ENDLAG = 2
 PUMPS = "ABCDEFGHIJKLMNOPQRSUVWXY"
 CLASSES = {"E": (128, 128), "P": (128, 512), "S": (576, 128), "X": (128, 256), "A": (32, 512), "R": (256, 128)}
 Q = 192
@@ -159,12 +157,13 @@
     s["FS"] = pltpu.VMEM((4, SMALL, 128), F32)
     s["FR"] = pltpu.VMEM((4, SMALL, 128), F32)
     dma = pltpu.SemaphoreType.DMA
-    s["ag_s"] = dma((COUNT, 11))
-    s["ag_r"] = dma((COUNT, 11))
+    s["ag_s"] = dma((AG_ROWS, 9))
+    s["ag_r"] = dma((AG_ROWS, 7))
+    s["ag_rc"] = dma((COUNT, 2))
     s["loc"] = dma((COUNT + 4,))
     s["vec"] = dma((len(VECTORS) + 4,))
-    s["rs_s"] = dma((COUNT, 11))
-    s["rs_r"] = dma((COUNT, 11))
+    s["rs_s"] = dma((RS_ROWS, 9))
+    s["rs_r"] = dma((RS_ROWS, 9))
     s["st_s"] = dma((3, 7))
     s["st_r"] = dma((3, 8))
     s["mp_s"] = dma((5, 4))
@@ -290,7 +289,9 @@
 
     def ag(p, slot, region, dev, src=None):
         i = INDEX[p]
-        return rcopy(region if src is None else src, region, s.ag_s.at[i, slot], s.ag_r.at[i, slot], dev)
+        row = i % AG_ROWS
+        arrival = s.ag_r.at[row, slot] if slot < 7 else s.ag_rc.at[i, slot - 7]
+        return rcopy(region if src is None else src, region, s.ag_s.at[row, slot], arrival, dev)
 
     def place(p):
         return pltpu.make_async_copy(shard(p), part(p, z, y, m), s.loc.at[INDEX[p]])
@@ -298,27 +299,16 @@
     def ag_copies(p):
         own = part(p, z, y, m)
         out, here = {}, {}
-        if p in AG_Z_LAST:
-            out[0] = [ag(p, 3, own, xdev, shard(p)), ag(p, 4, own, ydev, shard(p))]
-            here[0] = [(3, part(p, z, y, mx)), (4, part(p, z, 1 - y, m))]
-            out[1] = [ag(p, 5, part(p, z, y, mx), ydev)]
-            here[1] = [(5, part(p, z, 1 - y, mx))]
-            out[2] = [ag(p, SLOTS[k - 1 + 3 * xx], part(p, z, whole, xx * 2 + c), zdev(k)) for k in range(1, 4) for xx in range(2)]
-            here[2] = [
-                (SLOTS[k - 1 + 3 * xx], part(p, lax.rem(z + 4 - k, 4), whole, xx * 2 + c)) for k in range(1, 4) for xx in range(2)
-            ]
-        else:
-            share = 3 if INDEX[p] in AG_MORE[3] else 4 if INDEX[p] in AG_MORE[4] else 2
-            low, high = pl.ds(0, share), pl.ds(share, 4 - share)
-            out[0] = [ag(p, k - 1, own, zdev(k), shard(p)) for k in range(1, 4)]
-            here[0] = [(k - 1, part(p, lax.rem(z + 4 - k, 4), y, m)) for k in range(1, 4)]
-            out[1] = [ag(p, 3, part(p, whole, y, m), xdev), ag(p, 4, part(p, whole, y, m), ydev)]
-            here[1] = [(3, part(p, whole, y, mx)), (4, part(p, whole, 1 - y, m))]
-            out[2] = [ag(p, 5, part(p, low, y, mx), ydev)]
-            here[2] = [(5, part(p, low, 1 - y, mx))]
-            if share < 4:
-                out[2] += [ag(p, 6, part(p, high, 1 - y, m), xdev)]
-                here[2] += [(6, part(p, high, 1 - y, mx))]
+        share = 3 if INDEX[p] in AG_MORE else 2
+        low, high = pl.ds(0, share), pl.ds(share, 4 - share)
+        out[0] = [ag(p, k - 1, own, zdev(k), shard(p)) for k in range(1, 4)]
+        here[0] = [(k - 1, part(p, lax.rem(z + 4 - k, 4), y, m)) for k in range(1, 4)]
+        out[1] = [ag(p, 3, part(p, whole, y, m), xdev), ag(p, 4, part(p, whole, y, m), ydev)]
+        here[1] = [(3, part(p, whole, y, mx)), (4, part(p, whole, 1 - y, m))]
+        out[2] = [ag(p, 5, part(p, low, y, mx), ydev)]
+        here[2] = [(5, part(p, low, 1 - y, mx))]
+        out[2] += [ag(p, 6, part(p, high, 1 - y, m), xdev)]
+        here[2] += [(6, part(p, high, 1 - y, mx))]
         out[3] = [ag(p, 7 + xx, part(p, whole, whole, xx * 2 + c), cdev) for xx in range(2)]
         here[3] = [(7 + xx, part(p, whole, whole, xx * 2 + (1 - c))) for xx in range(2)]
         return out, here
@@ -328,6 +318,8 @@
             ag(p, slot, region, cdev).wait_recv()
 
     def ag_z(p):
+        if INDEX[p] >= AG_ROWS:
+            ag_sent(ORDER[INDEX[p] - AG_ROWS])
         place(p).start()
         for t in ag_copies(p)[0][0]:
             t.start()
@@ -351,16 +343,17 @@
         for t in out[3]:
             t.start()
 
+    def ag_sent(p):
+        for copies in ag_copies(p)[0].values():
+            for t in copies:
+                t.wait_send()
+
     def ag_drain(n):
         if "ag" in OPT:
             return
         for i in range(len(PIECES[n])):
-            for copies in ag_copies((n, i))[0].values():
-                for t in copies:
-                    t.wait_send()
-
-    def stop(t):
-        pass
+            if INDEX[n, i] >= COUNT - AG_ROWS:
+                ag_sent((n, i))
 
     ticks = {"k": 0}
 
@@ -369,11 +362,9 @@
             return
         k = ticks["k"]
         ticks["k"] = k + 1
-        for stage, lags in ((ag_c, (2 * LAG, 2 * LAG)), (ag_2, (LAG, 0)), (ag_1, (0, -1)), (ag_z, (-LEAD, -LEAD))):
-            for slow in range(2):
-                j = k - lags[slow]
-                if 0 <= j < COUNT and (ORDER[j] in AG_Z_LAST) == bool(slow):
-                    stage(ORDER[j])
+        for stage, lag in ((ag_c, 2 * LAG), (ag_2, LAG), (ag_1, 0), (ag_z, -LEAD)):
+            if 0 <= k - lag < COUNT:
+                stage(ORDER[k - lag])
 
     def mark(tag):
         for t in TICKS:
@@ -396,47 +387,41 @@
 
         lax.fori_loop(0, count, step, 0, unroll=unroll)
 
-    def rs(p, slot, region, landing, dev):
-        i = INDEX[p]
-        return rcopy(region, landing, s.rs_s.at[i, slot], s.rs_r.at[i, slot], dev)
+    def rs(row, slot, region, landing, dev):
+        return rcopy(region, landing, s.rs_s.at[row, slot], s.rs_r.at[row, slot], dev)
 
     credits = {"T": 0, "V": 1, "B": 2}
     takes = {"S": ("T", 0), "X": ("V", 1), "A": ("B", 2)}
     active = []
 
+    def pause():
+        steps = 0
+        while steps < state["lag"]:
+            steps += 1
+            yield
+
     def bump(region, extra):
         region[...] = region[...] + extra
 
-    def reduce_scatter(p):
+    def reduce_scatter(p, row):
         n, piece = p
         k = TENSORS[n][3]
         rc, r1, r2, rz = g["RC" + k], g["R1" + k], g["R2" + k], g["RZ" + k]
         c_ = cut(p)
-        pair = (pl.ds(0, 2),)
-        four = (pl.ds(0, 4),)
         swap = [
-            rs(p, xx, part(p, whole, whole, xx * 2 + (1 - c)), rc.at[(xx, pl.ds(0, 4), pl.ds(0, 2)) + c_], cdev) for xx in range(2)
+            rs(row, xx, part(p, whole, whole, xx * 2 + (1 - c)), rc.at[(xx, pl.ds(0, 4), pl.ds(0, 2)) + c_], cdev) for xx in range(2)
         ]
-        z_last = p not in RS_Z_LAST
-        first, second, third = [], [], []
-        if z_last:
-            share = 3 if INDEX[p] in RS_MORE[3] else 4 if INDEX[p] in RS_MORE[4] else 2
-            low, high = pl.ds(0, 4 - share), pl.ds(4 - share, share)
-            if share < 4:
-                first += [rs(p, 2, part(p, low, 1 - y, mx), r1.at[(pl.ds(0, 4 - share),) + c_], xdev)]
-            first += [rs(p, 3, part(p, high, 1 - y, mx), r1.at[(pl.ds(4 - share, share),) + c_], ydev)]
-            second = [
-                rs(p, 4, part(p, whole, y, mx), r2.at[(0, pl.ds(0, 4)) + c_], xdev),
-                rs(p, 5, part(p, whole, 1 - y, m), r2.at[(1, pl.ds(0, 4)) + c_], ydev),
-            ]
-            third = [rs(p, 5 + k, part(p, lax.rem(z + k, 4), y, m), rz.at[(k - 1,) + c_], zdev(k)) for k in range(1, 4)]
-        else:
-            for k in range(1, 4):
-                for xx in range(2):
-                    landing = r2.at[(k - 1, pl.ds(xx * 2, 2)) + c_] if k < 3 else r1.at[(pl.ds(xx * 2, 2),) + c_]
-                    first += [rs(p, SLOTS[k - 1 + 3 * xx], part(p, lax.rem(z + k, 4), whole, xx * 2 + c), landing, zdev(k))]
-            second = [rs(p, 3, part(p, z, 1 - y, mx), rz.at[(0,) + c_], ydev)]
-            third = [rs(p, 4, part(p, z, y, mx), rz.at[(1,) + c_], xdev), rs(p, 5, part(p, z, 1 - y, m), rz.at[(2,) + c_], ydev)]
+        share = 3 if INDEX[p] in RS_MORE else 2
+        low, high = pl.ds(0, 4 - share), pl.ds(4 - share, share)
+        first = [
+            rs(row, 2, part(p, low, 1 - y, mx), r1.at[(low,) + c_], xdev),
+            rs(row, 3, part(p, high, 1 - y, mx), r1.at[(high,) + c_], ydev),
+        ]
+        second = [
+            rs(row, 4, part(p, whole, y, mx), r2.at[(0, pl.ds(0, 4)) + c_], xdev),
+            rs(row, 5, part(p, whole, 1 - y, m), r2.at[(1, pl.ds(0, 4)) + c_], ydev),
+        ]
+        third = [rs(row, 5 + k, part(p, lax.rem(z + k, 4), y, m), rz.at[(k - 1,) + c_], zdev(k)) for k in range(1, 4)]
         for t in swap:
             t.start()
         yield
@@ -451,42 +436,30 @@
         loop(8, add_c)
         for t in first:
             t.start()
-        for _ in range(RLAG if z_last else ZLAG):
-            yield
+        yield from pause()
         for t in first:
             t.wait_recv()
-        if z_last:
-            for h in range(4 - share):
-                bump(part(p, h, 1 - y, m), r1[(h,) + c_])
-            for h in range(share):
-                bump(part(p, 4 - share + h, y, mx), r1[(4 - share + h,) + c_])
-        else:
-            for yy in range(2):
-                for xx in range(2):
-                    got = [r2[(0, xx * 2 + yy) + c_], r2[(1, xx * 2 + yy) + c_], r1[(xx * 2 + yy,) + c_]]
-                    bump(part(p, z, yy, xx * 2 + c), (got[0].astype(F32) + got[1].astype(F32) + got[2].astype(F32)).astype(BF))
+        for h in range(4 - share):
+            bump(part(p, h, 1 - y, m), r1[(h,) + c_])
+        for h in range(4 - share, 4):
+            bump(part(p, h, y, mx), r1[(h,) + c_])
         for t in second:
             t.start()
-        for _ in range(RLAG if z_last else 1):
-            yield
+        yield from pause()
         for t in second:
             t.wait_recv()
-        if z_last:
-
-            def add_2(zz):
-                bump(part(p, zz, y, m), (r2[(0, zz) + c_].astype(F32) + r2[(1, zz) + c_].astype(F32)).astype(BF))
-
-            loop(4, add_2)
-        else:
-            bump(part(p, z, y, mx), rz[(0,) + c_])
+
+        def add_2(zz):
+            bump(part(p, zz, y, m), (r2[(0, zz) + c_].astype(F32) + r2[(1, zz) + c_].astype(F32)).astype(BF))
+
+        loop(4, add_2)
         for t in third:
             t.start()
-        for _ in range(RLAG if z_last else 1):
-            yield
+        yield from pause()
         for t in third:
             t.wait_recv()
         total = part(p, z, y, m)[...].astype(F32)
-        for k in range(0 if z_last else 1, 3):
+        for k in range(3):
             total = total + rz[(k,) + c_].astype(F32)
         g["out" + n][c_] = total
         if n in credits and piece == len(PIECES[n]) - 1:
@@ -496,6 +469,7 @@
             t.wait_send()
 
     waiting = []
+    state = {"lag": RLAG, "begun": 0}
 
     def pump():
         for item in list(active):
@@ -511,12 +485,17 @@
                 if any(item[0][0] == takes[n][0] for item in active):
                     return
                 pl.semaphore_wait(s.free.at[takes[n][1]], 6)
-            gen = reduce_scatter(waiting.pop(0))
+            assert len(active) < RS_ROWS
+            gen = reduce_scatter(waiting.pop(0), state["begun"] % RS_ROWS)
+            state["begun"] += 1
             active.append(((n, i), gen))
             next(gen)
 
     def pumps(tag):
+        state["lag"] = RLAG
         for t in PUMPS:
+            if t in "123456":
+                state["lag"] = int(t)
             if t == tag:
                 pump()
 
@@ -1215,6 +1194,7 @@
     loop(4, entry_weights)
     begin("E")
     pumps("Y")
+    state["lag"] = ENDLAG
     while active or waiting:
         pump()
     mp_wait(4, fin_src, fin_dst)

time: 281 us -> 275 us (0.979)
  Pallas kernels: 279 us -> 272 us
    pallas_call x1, Pallas kernels: 274 us -> 267 us  [fused_shards(): pl.pallas_call(body, out_shape=outs, in_specs=[hbm, pl.BlockSpec(memory_s...]
where the time goes in v4:
time: 275 us
  Pallas kernels  272 us (99%)
    pallas_call x1, Pallas kernels, fused_shards(): pl.pallas_call(body, out_shape=outs, in_specs=[hbm, pl.BlockSpec(memory_s...  267 us

profile of v4, /device:TPU:0, one launch (start us, length us, event | category | flops | bytes accessed | tf_op | source)
XLA Modules:
  0.0 274.5 jit_solution(7044348044939821746)
XLA Ops:
  0.7 1.4 copy.63.refs_1_
  2.0 266.9 %shard_map.543 = (bf16[4,192,512]{2,1,0:T(8,128)(2,1)}, bf16[4,768,256]{2,1,0:T(8,128)(2,1)}, f32[128,128]{1,0:T(8,128)}, f32[128,512]{1,0:T(8,128)}, f32[576,12...) custom-call(bf16[4,768,1024]{2,1,0:T(8,128)(2,1)} %bitcast.48, ...), custom_call_target="tpu_custom_call" | custom-call | flops 14000000000 | bytes 30000000 | tf_op jit(solution)/shard_map/pallas_call | solution.py:1231
  268.9 5.4 %shard_map.544 = (bf16[4,192,512]{2,1,0:T(8,128)(2,1)}, f32[4,768,256]{2,1,0:T(8,128)}, f32[128,128]{1,0:T(8,128)}, f32[128,512]{1,0:T(8,128)}, f32[576,128]{1,0...) custom-call(bf16[4,192,512]{2,1,0:T(8,128)(2,1)} %get-tuple-element., ...), custom_call_target="tpu_custom_call" | custom-call | flops 1000000 | bytes 10000000 | tf_op jit(solution)/shard_map/pallas_call | solution.py:1253

commit v5 on v4

--- a/solution.py
+++ b/solution.py
@@ -39,7 +39,7 @@
 ORDER = [(n, i) for n in NAMES for i in range(len(PIECES[n]))]
 INDEX = {piece: i for i, piece in enumerate(ORDER)}
 AG_MORE = ()
-RS_MORE = (0, 5, 6, 7, 8)
+RS_MORE = (0, 2, 4, 5, 6, 7, 8)
 AG_ROWS, RS_ROWS = 8, 12
 LAST = {n: INDEX[n, len(PIECES[n]) - 1] for n in NAMES}
 COUNT = len(ORDER)
@@ -1068,35 +1068,35 @@
         keep2048(ROW[n], tot[2 * k : 2 * k + 1])
         keep2048(ROW[n] + 4, tot[2 * k + 1 : 2 * k + 2])
         norm_back_vectors(s.nv20, k, tot[2 * k : 2 * k + 1], tot[2 * k + 1 : 2 * k + 2], count20)
+    own_res.wait()
+    mp_wait(2, res_src, res_dst)
+    wide_grad(1, s.j_raw, s.g2, None)
+
+    def project_back(zz):
+        w = s.WP[zz].reshape(256, WIDE)
+        s.sgrad[:, col(zz, 256)] = dot_cols(s.g2[...], w)
+
+    loop(4, project_back)
+    pumps("P")
+    ag_drain("P")
+
+    def project_weights(n):
+        b = col(n, 256)
+        for h in range(2):
+            v = dot_rows(s.picT[0:Q, h * 512 : h * 512 + 512], s.g2[:, b]).astype(BF)
+            s.WP[2 * h : 2 * h + 2, :, :, b] = v.reshape(2, 2, 128, 256)
+
+    loop(8, project_weights)
+    begin("P")
+    pumps("R")
     wide_grad(0, s.x_raw, s.g1, s.scale1)
     pumps("N")
     widening_back(s.g1, s.WX)
     narrow_back("stride_b", 1, s.acc, s.s_raw)
     send_stats("stride_b")
     pumps("O")
-    own_res.wait()
-    mp_wait(2, res_src, res_dst)
-    wide_grad(1, s.j_raw, s.g2, None)
-
-    def project_back(zz):
-        w = s.WP[zz].reshape(256, WIDE)
-        s.sgrad[:, col(zz, 256)] = dot_cols(s.g2[...], w)
-
-    loop(4, project_back)
-    pumps("P")
     widening_weights("X", s.act_s, s.g1)
     pumps("Q")
-    ag_drain("P")
-
-    def project_weights(n):
-        b = col(n, 256)
-        for h in range(2):
-            v = dot_rows(s.picT[0:Q, h * 512 : h * 512 + 512], s.g2[:, b]).astype(BF)
-            s.WP[2 * h : 2 * h + 2, :, :, b] = v.reshape(2, 2, 128, 256)
-
-    loop(8, project_weights)
-    begin("P")
-    pumps("R")
     narrow_stats("stride_b", "stride")
     narrow_grad(1, s.s_raw)
     pumps("S")
@@ -1249,10 +1249,10 @@
     last += [jax.ShapeDtypeStruct(CLASSES[TENSORS[n][3]], F32) for n in PLAIN]
     last += [jax.ShapeDtypeStruct(v, F32) for v in ((16, 512),) * 4]
     last += [jax.ShapeDtypeStruct((rows, 128), F32) for _, _, rows in VECTORS]
-    blocks = [pl.BlockSpec((1, Q, 512), lambda i: (i, 0, 0)), pl.BlockSpec((1, 768, 256), lambda i: (i, 0, 0))]
+    blocks = [pl.BlockSpec((2, Q, 512), lambda i: (i, 0, 0)), pl.BlockSpec((2, 768, 256), lambda i: (i, 0, 0))]
     final = pl.pallas_call(
         last_body,
-        grid=(4,),
+        grid=(2,),
         out_shape=last,
         in_specs=blocks + kinds + [held((SMALL, 128))],
         out_specs=blocks + [held(CLASSES[TENSORS[n][3]]) for n in PLAIN] + [held(v) for v in ((16, 512),) * 4]

time: 275 us -> 268 us (0.975)
  Pallas kernels: 272 us -> 266 us
    pallas_call x1, Pallas kernels: 267 us -> 261 us  [fused_shards(): pl.pallas_call(body, out_shape=outs, in_specs=[hbm, pl.BlockSpec(memory_s...]
where the time goes in v5:
time: 268 us
  Pallas kernels  266 us (99%)
    pallas_call x1, Pallas kernels, fused_shards(): pl.pallas_call(body, out_shape=outs, in_specs=[hbm, pl.BlockSpec(memory_s...  261 us

profile of v5, /device:TPU:0, one launch (start us, length us, event | category | flops | bytes accessed | tf_op | source)
XLA Modules:
  0.0 268.0 jit_solution(17661507943798448121)
XLA Ops:
  0.7 1.4 copy.63.refs_1_
  2.0 261.3 %shard_map.543 = (bf16[4,192,512]{2,1,0:T(8,128)(2,1)}, bf16[4,768,256]{2,1,0:T(8,128)(2,1)}, f32[128,128]{1,0:T(8,128)}, f32[128,512]{1,0:T(8,128)}, f32[576,12...) custom-call(bf16[4,768,1024]{2,1,0:T(8,128)(2,1)} %bitcast.48, ...), custom_call_target="tpu_custom_call" | custom-call | flops 14000000000 | bytes 30000000 | tf_op jit(solution)/shard_map/pallas_call | solution.py:1231
  263.3 4.5 %shard_map.544 = (bf16[4,192,512]{2,1,0:T(8,128)(2,1)}, f32[4,768,256]{2,1,0:T(8,128)}, f32[128,128]{1,0:T(8,128)}, f32[128,512]{1,0:T(8,128)}, f32[576,128]{1,0...) custom-call(bf16[4,192,512]{2,1,0:T(8,128)(2,1)} %get-tuple-element., ...), custom_call_target="tpu_custom_call" | custom-call | flops 1000000 | bytes 10000000 | tf_op jit(solution)/shard_map/pallas_call | solution.py:1253
